TPU v7x, 32 devices: a whole 2x2x4 slice. The times are simulated.
32 devices in a mesh: groups: 2 (over y), dp: 4 (over z), seq: 2 (over x), head: 2 (over core).
Axes of the slice: x: 2, y: 2, z: 4, core: 2. Of those that a mesh axis runs over, the one named last changes fastest.
Arguments:
- projected: bfloat16 [3, 2048, 16, 2, 128], P(None, ('groups', 'dp', 'seq'), None, 'head'), parts along dimension 1, may hold values from -60 to 60
- assignment: int32 [8, 2, 4], P(('groups', 'dp'), 'seq'), parts along dimension 0, may hold values from 0 to 3, as said below
- segments: int32 [8, 256], P(('groups', 'dp')), parts along dimension 0, may hold values from 0 to 3, never falling along the last dimension, each value on 1 to 192 neighbouring positions
- advantage: float32 [8, 4], P(('groups', 'dp')), parts along dimension 0, may hold values from -4 to 4
- out_weight: bfloat16 [16, 2, 128, 5120], P('dp', 'head', None, 'seq'), may hold values from -0.09375 to 0.09375
- cotangent: bfloat16 [2048, 5120], P(('groups', 'dp'), 'seq'), parts along dimension 0, may hold values from -6 to 6
Outputs:
- mixed: bfloat16 [2048, 5120], P(('groups', 'dp'), ('seq', 'head')), parts along dimension 0
- weight_grad: float32 [32, 2, 128, 5120], P(('groups', 'dp'), 'head', None, 'seq'), parts along dimension 0
There are 2 independent parts, one for each index of `groups`. A program takes and returns all parts, laid end to end along the dimension named above; an argument that names none is the same for every part. Nothing has to cross between parts.
Inputs may be any that keep to these rules, and one draw needn't show every extreme that they name: `assignment`: for each sequence shard, every trainer row receives exactly 4 blocks and at most 2 from one owner; every owner sends 2 blocks to some trainer row.
All inputs are finite; a program needn't handle non-finite values.
Results may differ from a plain program's by a relative error of at most 0.008.
Values may be sent and summed in bfloat16 or wider, within the bound.
No kernel may reach another device: no remote copies, remote signals or barrier semaphores. Data moves between devices by JAX's collectives and lax.ppermute only.
A program may use at most 128 MiB of HBM per device.

v0:
```python
import math

import jax
import jax.numpy as jnp
from jax import lax
from jax.sharding import PartitionSpec as P

CAP = 2


def attend_heads(queries, keys_all, values_all, seg_query, seg_key):
    head_size = queries.shape[-1]
    scores = jnp.einsum("tkc,ukc->ktu", queries, keys_all, preferred_element_type=jnp.float32) * (
        1.0 / math.sqrt(head_size)
    )
    pos_query = jnp.arange(queries.shape[0], dtype=jnp.int32)
    pos_key = jnp.arange(keys_all.shape[0], dtype=jnp.int32)
    keep = (seg_query[:, None] == seg_key[None, :]) & (pos_key[None, :] <= pos_query[:, None])
    scores = jnp.where(keep[None], scores, -1e30)
    rowmax = jnp.max(scores, axis=-1, keepdims=True)
    expd = jnp.where(keep[None], jnp.exp(scores - rowmax), 0.0)
    probs = (expd / jnp.sum(expd, axis=-1, keepdims=True)).astype(jnp.bfloat16)
    attended = jnp.einsum("ktu,ukc->tkc", probs, values_all, preferred_element_type=jnp.float32)
    return attended.astype(jnp.bfloat16)


def body(projected, assignment, segments, advantage, out_weight, cotangent):
    shards = lax.axis_size("dp")
    tok_rows = projected.shape[1]
    head_count = projected.shape[2]
    head_size = projected.shape[4]
    block_len = tok_rows // shards
    out_cols = out_weight.shape[3]
    blocks = jnp.transpose(
        projected.reshape(3, shards, block_len, head_count, head_size), (1, 0, 2, 3, 4)
    )
    targets = assignment.reshape(shards)
    member = (targets[:, None] == jnp.arange(shards, dtype=jnp.int32)[None, :]).astype(jnp.int32)
    ranks = jnp.sum((jnp.cumsum(member, axis=0) - member) * member, axis=1)
    counts = jnp.sum(member, axis=0).reshape(shards, 1)
    outgoing = jnp.zeros((shards, CAP, 3, block_len, head_count, head_size), projected.dtype)
    outgoing = outgoing.at[targets, ranks].set(blocks)
    incoming, arrived = (
        lax.all_to_all(outgoing, "dp", split_axis=0, concat_axis=0, tiled=True),
        lax.all_to_all(counts, "dp", split_axis=0, concat_axis=0, tiled=True),
    )
    arrived = arrived.reshape(shards)
    firsts = jnp.cumsum(arrived) - arrived
    slots = jnp.arange(CAP, dtype=jnp.int32)
    places = jnp.where(slots[None, :] < arrived[:, None], firsts[:, None] + slots[None, :], shards)
    packed = jnp.zeros((shards, 3, block_len, head_count, head_size), projected.dtype)
    packed = packed.at[places.reshape(-1)].set(
        incoming.reshape(shards * CAP, 3, block_len, head_count, head_size), mode="drop"
    )
    local = jnp.transpose(packed, (1, 0, 2, 3, 4)).reshape(3, tok_rows, head_count, head_size)
    seg_row = segments[0]
    labels = jnp.arange(advantage.shape[1], dtype=jnp.int32)
    member_seg = (seg_row[:, None] == labels[None, :]).astype(jnp.float32)
    sizes_tok = jnp.sum(member_seg * jnp.sum(member_seg, axis=0)[None, :], axis=1)
    adv_tok = jnp.sum(member_seg * advantage[0][None, :], axis=1)
    scaled = (cotangent.astype(jnp.float32) * (adv_tok / sizes_tok)[:, None]).astype(jnp.bfloat16)
    gathered = lax.all_gather(out_weight, "dp", axis=0, tiled=True)
    weight_rows = gathered.reshape(head_count, head_size, out_cols)
    switched = lax.all_to_all(local, "seq", split_axis=2, concat_axis=1, tiled=True)
    attended = attend_heads(switched[0], switched[1], switched[2], seg_row, seg_row)
    piece = lax.all_gather(attended, "seq", axis=1, tiled=True)
    total = jnp.einsum("tkc,kcn->tn", piece, weight_rows, preferred_element_type=jnp.float32)
    term = jnp.einsum("tkc,tn->kcn", piece, scaled, preferred_element_type=jnp.float32)
    total, grads = (total, term)
    mixed = lax.psum_scatter(total.astype(jnp.bfloat16), "head", scatter_dimension=1, tiled=True)
    weight_grad = lax.psum_scatter(
        grads.reshape(head_count, 1, head_size, out_cols).astype(jnp.bfloat16),
        "dp",
        scatter_dimension=0,
        tiled=True,
    ).astype(jnp.float32)
    return (mixed, weight_grad)


def solution(mesh):
    placed = (
        P(None, ("groups", "dp", "seq"), None, "head", None),
        P(("groups", "dp"), "seq", None),
        P(("groups", "dp"), None),
        P(("groups", "dp"), None),
        P("dp", "head", None, "seq"),
        P(("groups", "dp"), "seq"),
    )
    return jax.shard_map(
        body,
        mesh=mesh,
        in_specs=placed,
        out_specs=(P(("groups", "dp"), ("seq", "head")), P(("groups", "dp"), "head", None, "seq")),
        check_vma=False,
    )
```

profile of v0, /device:TPU:8, one launch (start us, length us, event | category | flops | bytes accessed | tf_op | source)
XLA Modules:
  0.0 540.4 jit_solution(2237697578767285100)
XLA Ops:
  7.2 0.7 fusion.20
  7.9 0.8 select_reduce_fusion.2
  8.8 0.7 copy.55
  9.4 5.3 all-to-all-start
  14.8 0.7 fusion.24
  15.4 1.7 copy.72
  17.1 2.3 broadcast_in_dim.49
  19.4 4.6 scatter_fusion
  24.1 5.1 all-to-all-start.1
  29.7 66.3 %all-to-all-done.1 = bf16[4,2,3,32,16,128]{5,4,3,2,1,0:T(8,128)(2,1)S(1)} async-done(((bf16[4,2,3,32,16,128]{5,4,3,2,1,0:T(8,128)(2,1)}), bf16[4,2,3,32,16,128]{5,4,3,2,1,0:T(8,128)(2,1)S(1)}, u32[]{:S(2)}, u32[]{:S(2)}) %all-to-all-start.1) | async-done | bytes 3145760 | tf_op jit(solution)/shard_map/all_to_all | solution.py:44
  96.0 1.7 copy-done
  97.7 0.3 broadcast_in_dim.46
  97.9 5.5 %scatter_fusion.1 = bf16[4,3,32,16,128]{4,3,2,1,0:T(8,128)(2,1)S(1)} fusion(bf16[4,3,32,16,128]{4,3,2,1,0:T(8,128)(2,1)S(1)} %broadcast_in_dim.46, s32[8]{0:T(128)S(1)} %fusion.23, bf16[8,3,32,16,128]{4,3,2,1,0:T(8,128)(2,1)} %bitcast.62), kind=kCustom, calls=%fused_computation.1 | custom fusion | bytes 9437216 | tf_op jit(solution)/shard_map/scatter | solution.py:52
  103.4 0.3 copy.57
  103.7 1.6 copy.58
  105.2 3.8 all-to-all-start.2
  109.2 17.5 %all-to-all-done.2 = bf16[3,128,16,128]{3,1,0,2:T(8,128)(2,1)S(1)} async-done(((bf16[3,128,16,128]{3,1,0,2:T(8,128)(2,1)}), bf16[3,128,16,128]{3,1,0,2:T(8,128)(2,1)S(1)}, u32[]{:S(2)}, u32[]{:S(2)}) %all-to-all-start.2) | async-done | bytes 1572896 | tf_op jit(solution)/shard_map/all_to_all | solution.py:64
  126.8 1.0 copy.71
  127.8 0.3 fusion.27
  128.1 0.5 copy.60
  128.6 0.3 squeeze.9
  129.2 2.3 fusion.28
  131.5 1.9 fusion.13
  133.4 1.0 copy.64
  134.5 0.7 all-gather.5.cloned.1.call-update
  135.5 21.5 %all-gather.3.cloned.1.call-done = bf16[256,16,128]{2,0,1:T(8,128)(2,1)} async-done(((bf16[256,8,128]{2,0,1:T(8,128)(2,1)}), bf16[256,16,128]{2,0,1:T(8,128)(2,1)}) %all-gather.3.cloned.1.call-update) | async-done | bytes 1048592 | tf_op jit(solution)/shard_map/all_gather | solution.py:66
  156.9 6.9 %convert_bitcast_fusion = bf16[16,1,128,2560]{3,2,0,1:T(8,128)(2,1)} fusion(bf16[256,16,128]{2,0,1:T(8,128)(2,1)} %all-gather.3.cloned.1.call-done, bf16[256,2560]{1,0:T(8,128)(2,1)S(1)} %copy-done.1, f32[256]{0:T(256)S(1)} %div.17), kind=kOutput, calls=%fused_computation.5 | convolution fusion | flops 2691563520 | bytes 12846080 | tf_op jit(solution)/shard_map/tkc,tn->kcn/dot_general | solution.py:68
  163.9 175.6 %all-gather.5.cloned.1.call-done = bf16[16,1,128,2560]{3,2,1,0:T(8,128)(2,1)} async-done(((bf16[4,1,128,2560]{3,2,1,0:T(8,128)(2,1)}), bf16[16,1,128,2560]{3,2,1,0:T(8,128)(2,1)}) %all-gather.5.cloned.1.call-update) | async-done | bytes 10485776 | tf_op jit(solution)/shard_map/all_gather | solution.py:62
  339.5 6.8 %fusion.6 = bf16[256,2560]{1,0:T(8,128)(2,1)} fusion(bf16[256,16,128]{2,0,1:T(8,128)(2,1)S(1)} %copy-done.2, bf16[16,1,128,2560]{3,2,1,0:T(8,128)(2,1)} %all-gather.5.cloned.1.call-done), kind=kOutput, calls=%fused_computation.7 | convolution fusion | flops 2685009920 | bytes 12845056 | tf_op jit(solution)/shard_map/tkc,kcn->tn/dot_general | solution.py:67
  346.3 174.8 %reduce-scatter.5.cloned.1.call-done = bf16[4,1,128,2560]{3,2,0,1:T(8,128)(2,1)} async-done(((bf16[16,1,128,2560]{3,2,0,1:T(8,128)(2,1)}), bf16[4,1,128,2560]{3,2,0,1:T(8,128)(2,1)}) %reduce-scatter.5.cloned.1.call-update) | async-done | bytes 2621456 | tf_op jit(solution)/shard_map/reduce_scatter | solution.py:71
  521.1 4.8 bitcast_convert_fusion
  525.9 8.0 %reduce-scatter.3.cloned.1.call-done = bf16[256,1280]{1,0:T(8,128)(2,1)} async-done(((bf16[256,2560]{1,0:T(8,128)(2,1)}), bf16[256,1280]{1,0:T(8,128)(2,1)}) %reduce-scatter.3.cloned.1.call-update) | async-done | bytes 655376 | tf_op jit(solution)/shard_map/reduce_scatter | solution.py:70
  (30 shorter events, 1.4 us)
Async XLA Ops:
  9.4 14.6 %all-to-all-start = ((s32[4,1,1]{2,1,0:T(1,128)}), s32[4,1,1]{2,1,0:T(1,128)S(1)}, u32[]{:S(2)}, u32[]{:S(2)}) async-start(s32[4,1,1]{2,1,0:T(1,128)} %copy.55), calls=%async_computation | async-start | bytes 4096 | tf_op jit(solution)/shard_map/all_to_all | solution.py:45
  24.1 71.9 %all-to-all-start.1 = ((bf16[4,2,3,32,16,128]{5,4,3,2,1,0:T(8,128)(2,1)}), bf16[4,2,3,32,16,128]{5,4,3,2,1,0:T(8,128)(2,1)S(1)}, u32[]{:S(2)}, u32[]{:S(2)}) async-start(bf16[4,2,3,32,16,128]{5,4,3,2,1,0:T(8,128)(2,1)} %scatter_fusion), calls=%async_computation.1 | async-start | bytes 6291456 | tf_op jit(solution)/shard_map/all_to_all | solution.py:44
  96.0 1.7 copy-start
  105.2 3.9 copy-start.3
  105.2 21.5 %all-to-all-start.2 = ((bf16[3,128,16,128]{3,1,0,2:T(8,128)(2,1)}), bf16[3,128,16,128]{3,1,0,2:T(8,128)(2,1)S(1)}, u32[]{:S(2)}, u32[]{:S(2)}) async-start(bf16[3,128,16,128]{3,1,0,2:T(8,128)(2,1)} %copy.58), calls=%async_computation.2 | async-start | bytes 3145728 | tf_op jit(solution)/shard_map/all_to_all | solution.py:64
  109.0 47.9 %all-gather.3.cloned.1.call-start = ((), (), s32[]{:S(2)}) async-start(), calls=%async_computation.5 | async-start | bytes 1572864 | tf_op jit(solution)/shard_map/all_gather | solution.py:66
  133.4 2.0 copy-start.4
  133.4 23.5 %copy-start.1 = (bf16[256,2560]{1,0:T(8,128)(2,1)S(1)}, bf16[256,2560]{1,0:T(8,128)(2,1)}, u32[]{:S(2)}) copy-start(bf16[256,2560]{1,0:T(8,128)(2,1)} %param.11) | copy-start | bytes 3932164
  134.4 205.0 %all-gather.5.cloned.1.call-start = ((), (), s32[]{:S(2)}) async-start(), calls=%async_computation.6 | async-start | bytes 13107200 | tf_op jit(solution)/shard_map/all_gather | solution.py:62
  135.2 385.9 %reduce-scatter.5.cloned.1.call-start = ((), (), s32[]{:S(2)}) async-start(), calls=%async_computation.8 | async-start | bytes 13107200 | tf_op jit(solution)/shard_map/reduce_scatter | solution.py:71
  163.8 175.6 %copy-start.2 = (bf16[256,16,128]{2,0,1:T(8,128)(2,1)S(1)}, bf16[256,16,128]{2,0,1:T(8,128)(2,1)}, u32[]{:S(2)}) copy-start(bf16[256,16,128]{2,0,1:T(8,128)(2,1)} %all-gather.3.cloned.1.call-done) | copy-start | bytes 3145732
  163.9 370.0 %reduce-scatter.3.cloned.1.call-start = ((), (), s32[]{:S(2)}) async-start(), calls=%async_computation.7 | async-start | bytes 1966080 | tf_op jit(solution)/shard_map/reduce_scatter | solution.py:70
Sparse Core Ops, SparseCore 0:
  134.6 22.3 all-gather.2
  158.5 180.9 all-gather.4
  341.8 179.2 reduce-scatter.4
  523.8 10.0 reduce-scatter.2
where the time goes:
time: 542 us; the launch traced here: 540 us
  waiting for transfers between devices  464 us (86%)
  local copies, waits for them, and re-layouts  22 us (4%)
  matrix products  17.9 us (3%)
  starting transfers between devices  14.4 us (3%)
  between operations  13.9 us (3%)
  other arithmetic  7.79 us (1%)
    all_gather x1, waiting for transfers between devices, body(): gathered = lax.all_gather(out_weight, 'dp', axis=0, tiled=True)  176 us
    reduce_scatter x1, waiting for transfers between devices, body(): lax.psum_scatter(grads.reshape(head_count, 1, head_size, out_cols).astype...  175 us
    all_to_all x1, waiting for transfers between devices, body(): lax.all_to_all(outgoing, 'dp', split_axis=0, concat_axis=0, tiled=True)  66.3 us
    all_gather x1, waiting for transfers between devices, body(): piece = lax.all_gather(attended, 'seq', axis=1, tiled=True)  21.5 us
    all_to_all x1, waiting for transfers between devices, body(): lax.all_to_all(local, 'seq', split_axis=2, concat_axis=1, tiled=True)  17.5 us
  transfers between devices with their start and end apart: 7, of which 6 were waited for; matrix products, arithmetic and copies ran while one was open for 5% of the time, Pallas kernels for 0%

commit v1 on v0

--- a/solution.py
+++ b/solution.py
@@ -1,8 +1,11 @@
+import functools
 import math
 
 import jax
 import jax.numpy as jnp
 from jax import lax
+from jax.experimental import pallas as pl
+from jax.experimental.pallas import tpu as pltpu
 from jax.sharding import PartitionSpec as P
 
 CAP = 2
@@ -24,7 +27,15 @@
     return attended.astype(jnp.bfloat16)
 
 
-def body(projected, assignment, segments, advantage, out_weight, cotangent):
+def token_weight(seg_row, adv_row):
+    labels = jnp.arange(adv_row.shape[0], dtype=jnp.int32)
+    member_seg = (seg_row[:, None] == labels[None, :]).astype(jnp.float32)
+    sizes_tok = jnp.sum(member_seg * jnp.sum(member_seg, axis=0)[None, :], axis=1)
+    adv_tok = jnp.sum(member_seg * adv_row[None, :], axis=1)
+    return adv_tok / sizes_tok
+
+
+def body_rows(projected, assignment, segments, advantage, out_weight, cotangent):
     shards = lax.axis_size("dp")
     tok_rows = projected.shape[1]
     head_count = projected.shape[2]
@@ -54,11 +65,8 @@
     )
     local = jnp.transpose(packed, (1, 0, 2, 3, 4)).reshape(3, tok_rows, head_count, head_size)
     seg_row = segments[0]
-    labels = jnp.arange(advantage.shape[1], dtype=jnp.int32)
-    member_seg = (seg_row[:, None] == labels[None, :]).astype(jnp.float32)
-    sizes_tok = jnp.sum(member_seg * jnp.sum(member_seg, axis=0)[None, :], axis=1)
-    adv_tok = jnp.sum(member_seg * advantage[0][None, :], axis=1)
-    scaled = (cotangent.astype(jnp.float32) * (adv_tok / sizes_tok)[:, None]).astype(jnp.bfloat16)
+    weight = token_weight(seg_row, advantage[0])
+    scaled = (cotangent.astype(jnp.float32) * weight[:, None]).astype(jnp.bfloat16)
     gathered = lax.all_gather(out_weight, "dp", axis=0, tiled=True)
     weight_rows = gathered.reshape(head_count, head_size, out_cols)
     switched = lax.all_to_all(local, "seq", split_axis=2, concat_axis=1, tiled=True)
@@ -66,15 +74,156 @@
     piece = lax.all_gather(attended, "seq", axis=1, tiled=True)
     total = jnp.einsum("tkc,kcn->tn", piece, weight_rows, preferred_element_type=jnp.float32)
     term = jnp.einsum("tkc,tn->kcn", piece, scaled, preferred_element_type=jnp.float32)
-    total, grads = (total, term)
     mixed = lax.psum_scatter(total.astype(jnp.bfloat16), "head", scatter_dimension=1, tiled=True)
     weight_grad = lax.psum_scatter(
-        grads.reshape(head_count, 1, head_size, out_cols).astype(jnp.bfloat16),
+        term.reshape(head_count, 1, head_size, out_cols).astype(jnp.bfloat16),
         "dp",
         scatter_dimension=0,
         tiled=True,
     ).astype(jnp.float32)
     return (mixed, weight_grad)
+
+
+def attention_kernel(rows, nseq, nblk, blk, assign, seg_lane, seg_sub, recv, out, packed, order):
+    heads, head_size = recv.shape[2], recv.shape[4]
+    row_len = seg_lane.shape[1]
+    per_shard = row_len // nseq // blk
+    for s in range(nseq):
+        counts = [jnp.int32(0)] * rows
+        for o in range(rows):
+            for b in range(nblk):
+                target = assign[o * nseq + s, b]
+                slot = counts[0]
+                for r in range(1, rows):
+                    slot = jnp.where(target == r, counts[r], slot)
+                order[(target * nseq + s) * per_shard + slot] = o * nblk + b
+                counts = [counts[r] + (target == r).astype(jnp.int32) for r in range(rows)]
+    pos_query = lax.broadcasted_iota(jnp.int32, (row_len, row_len), 0)
+    pos_key = lax.broadcasted_iota(jnp.int32, (row_len, row_len), 1)
+    causal = pos_key <= pos_query
+    scale = 1.0 / math.sqrt(head_size)
+    for r in range(rows):
+        keep = causal & (seg_sub[:, r : r + 1] == seg_lane[r : r + 1, :])
+        for s in range(nseq):
+            for slot in range(per_shard):
+                source = order[(r * nseq + s) * per_shard + slot]
+                owner, block = lax.div(source, nblk), lax.rem(source, nblk)
+                first = pl.multiple_of(block * blk, blk)
+                place = (s * per_shard + slot) * blk
+                packed[:, :, place : place + blk, :] = recv[owner * nseq + s, :, :, pl.ds(first, blk), :]
+        for h in range(heads):
+            scores = lax.dot_general(
+                packed[0, h], packed[1, h], (((1,), (1,)), ((), ())), preferred_element_type=jnp.float32
+            ) * scale
+            scores = jnp.where(keep, scores, -1e30)
+            rowmax = jnp.max(scores, axis=-1, keepdims=True)
+            expd = jnp.where(keep, jnp.exp(scores - rowmax), 0.0)
+            probs = (expd / jnp.sum(expd, axis=-1, keepdims=True)).astype(jnp.bfloat16)
+            attended = jnp.dot(probs, packed[2, h], preferred_element_type=jnp.float32)
+            out[r * row_len : (r + 1) * row_len, h * head_size : (h + 1) * head_size] = attended.astype(
+                jnp.bfloat16
+            )
+
+
+def attend_rows(recv, assign, segs, nblk):
+    peers, _, heads, tokens, head_size = recv.shape
+    rows, row_len = segs.shape
+    nseq = peers // rows
+    return pl.pallas_call(
+        functools.partial(attention_kernel, rows, nseq, nblk, tokens // nblk),
+        out_shape=jax.ShapeDtypeStruct((rows * row_len, heads * head_size), jnp.bfloat16),
+        in_specs=[
+            pl.BlockSpec(memory_space=pltpu.SMEM),
+            pl.BlockSpec(memory_space=pltpu.VMEM),
+            pl.BlockSpec(memory_space=pltpu.VMEM),
+            pl.BlockSpec(memory_space=pltpu.VMEM),
+        ],
+        out_specs=pl.BlockSpec(memory_space=pltpu.VMEM),
+        scratch_shapes=[
+            pltpu.VMEM((3, heads, row_len, head_size), jnp.bfloat16),
+            pltpu.SMEM((rows * nblk * nseq,), jnp.int32),
+        ],
+        compiler_params=pltpu.CompilerParams(vmem_limit_bytes=32 << 20),
+        cost_estimate=pl.CostEstimate(
+            flops=4 * rows * heads * row_len * row_len * head_size,
+            bytes_accessed=recv.size * 2 + rows * row_len * heads * head_size * 2,
+            transcendentals=rows * heads * row_len * row_len,
+        ),
+        name="attend_rows",
+    )(assign, segs, segs.T, recv)
+
+
+def swap(x, axis):
+    return lax.ppermute(x, axis, [(0, 1), (1, 0)])
+
+
+def body_heads(projected, assignment, segments, advantage, out_weight, cotangent):
+    ndp, nseq = lax.axis_size("dp"), lax.axis_size("seq")
+    me, my_seq, my_head = lax.axis_index("dp"), lax.axis_index("seq"), lax.axis_index("head")
+    tokens, pairs, head_size = projected.shape[1], projected.shape[2], projected.shape[4]
+    nblk = assignment.shape[2]
+    row_len = segments.shape[1]
+    mine = pairs // (ndp * nseq)
+    cols = out_weight.shape[3]
+    half = cols // 2
+    width = mine * head_size
+
+    small = jnp.concatenate([assignment.reshape(nblk), segments.reshape(row_len)])
+    small = jnp.broadcast_to(small[None], (ndp * nseq, nblk + row_len))
+    small = lax.all_to_all(small, ("dp", "seq"), split_axis=0, concat_axis=0, tiled=True)
+    assign, segs = small[:, :nblk], small[::nseq, nblk:]
+
+    sent = projected.reshape(3, tokens, ndp * nseq, mine, head_size).transpose(2, 0, 3, 1, 4)
+    recv = lax.all_to_all(sent, ("dp", "seq"), split_axis=0, concat_axis=0, tiled=True)
+
+    weight = token_weight(segments[0], advantage[0])
+    own_cols = lax.dynamic_slice_in_dim(cotangent, my_head * half, half, 1)
+    scaled = (own_cols.astype(jnp.float32) * weight[:, None]).astype(jnp.bfloat16)
+
+    rows_w = out_weight.reshape(nseq * width, cols)
+    keep_w = lax.dynamic_slice_in_dim(rows_w, my_head * half, half, 1)
+    other_w = swap(lax.dynamic_slice_in_dim(rows_w, (1 - my_head) * half, half, 1), "head")
+
+    recv, scaled = lax.optimization_barrier((recv, scaled))
+    att = attend_rows(recv, assign, segs, nblk)
+
+    def both(x):
+        other = swap(x, "head")
+        return jnp.where(my_head == 0, jnp.concatenate([x, other], 1), jnp.concatenate([other, x], 1))
+
+    pieces = [scaled] + [
+        lax.ppermute(scaled, "dp", [(i, i ^ k) for i in range(ndp)]) for k in range(1, ndp)
+    ]
+    pieces = [both(x) for x in pieces]
+
+    att_seq = swap(att, "seq")
+    att_head = swap(att, "head")
+    att_diag = swap(att_seq, "head")
+
+    def slab(w, s):
+        return lax.dynamic_slice_in_dim(w, s * width, width, 0)
+
+    def rows_of(x, k):
+        return lax.dynamic_slice_in_dim(x, (me ^ k) * row_len, row_len, 0)
+
+    weights = jnp.concatenate(
+        [slab(keep_w, my_seq), slab(other_w, my_seq), slab(keep_w, 1 - my_seq), slab(other_w, 1 - my_seq)], 0
+    )
+    terms = []
+    for k in reversed(range(ndp)):
+        row = jnp.concatenate([rows_of(x, k) for x in (att, att_head, att_seq, att_diag)], 1)
+        total = jnp.dot(row, weights, preferred_element_type=jnp.float32)
+        if k:
+            total = lax.ppermute(total.astype(jnp.bfloat16), "dp", [(i, i ^ k) for i in range(ndp)])
+        terms.append(total.astype(jnp.float32))
+    mixed = functools.reduce(jnp.add, terms).astype(jnp.bfloat16)
+
+    pair = jnp.where(my_seq == 0, jnp.concatenate([att, att_seq], 1), jnp.concatenate([att_seq, att], 1))
+    left = jnp.concatenate([rows_of(pair, k) for k in range(ndp)], 0)
+    grad = lax.dot_general(
+        left, jnp.concatenate(pieces, 0), (((0,), (0,)), ((), ())), preferred_element_type=jnp.float32
+    )
+    return mixed, grad.reshape(nseq * mine, 1, head_size, cols)
 
 
 def solution(mesh):
@@ -86,6 +235,12 @@
         P("dp", "head", None, "seq"),
         P(("groups", "dp"), "seq"),
     )
+
+    def body(projected, *rest):
+        ndp, nseq = mesh.shape["dp"], mesh.shape["seq"]
+        fits = projected.shape[2] % (ndp * nseq) == 0 and (ndp, nseq) == (4, 2)
+        return (body_heads if fits else body_rows)(projected, *rest)
+
     return jax.shard_map(
         body,
         mesh=mesh,

time: 542 us -> 184 us (0.34)
  the two profiles are of different devices: /device:TPU:8 before, /device:TPU:0 now
where the time goes in v1:
time: 184 us; the launch traced here: 183 us
  waiting for transfers between devices  108 us (59%)
  starting transfers between devices  47.5 us (26%)
  local copies, waits for them, and re-layouts  10.3 us (6%)
  matrix products  9.51 us (5%)
  other arithmetic  3.74 us (2%)
  Pallas kernels  2.99 us (2%)
    ppermute x3, waiting for transfers between devices, body_heads(): lax.ppermute(total.astype(jnp.bfloat16), 'dp', [(i, i ^ k) for i in range...  35 us
    ppermute x3, waiting for transfers between devices, body_heads(): lax.ppermute(scaled, 'dp', [(i, i ^ k) for i in range(ndp)])  33.8 us
    all_to_all x1, waiting for transfers between devices, body_heads(): lax.all_to_all(sent, ('dp', 'seq'), split_axis=0, concat_axis=0, tiled=True)  31.3 us
    ppermute x3, starting transfers between devices, body_heads(): lax.ppermute(total.astype(jnp.bfloat16), 'dp', [(i, i ^ k) for i in range...  29.6 us
    all_to_all x1, starting transfers between devices, body_heads(): lax.all_to_all(small, ('dp', 'seq'), split_axis=0, concat_axis=0, tiled=T...  7.25 us
    dot_general x1, matrix products, body_heads(): lax.dot_general(left, jnp.concatenate(pieces, 0), (((0,), (0,)), ((), ())...  5.27 us
    ppermute x8, waiting for transfers between devices, swap(): return lax.ppermute(x, axis, [(0, 1), (1, 0)])  4.59 us
    ppermute x3, starting transfers between devices, body_heads(): lax.ppermute(scaled, 'dp', [(i, i ^ k) for i in range(ndp)])  4.45 us
  transfers between devices with their start and end apart: 16, of which 6 were waited for; matrix products, arithmetic and copies ran while one was open for 11% of the time, Pallas kernels for 2%

profile of v1, /device:TPU:0, one launch (start us, length us, event | category | flops | bytes accessed | tf_op | source)
XLA Modules:
  0.0 183.2 jit_solution(17265370883671355982)
XLA Ops:
  0.6 0.8 pad_add_fusion
  1.4 0.6 broadcast_in_dim.2
  2.0 7.3 %all-to-all-start = ((s32[8,1,260]{2,1,0:T(1,128)}), s32[8,1,260]{2,1,0:T(1,128)S(1)}, u32[]{:S(2)}, u32[]{:S(2)}) async-start(s32[8,1,260]{2,1,0:T(1,128)} %broadcast_in_dim.2), calls=%async_computation | async-start | bytes 24576 | tf_op jit(solution)/shard_map/all_to_all | solution.py:173
  9.2 3.0 %copy.31 = bf16[3,128,8,2,128]{4,1,3,0,2:T(8,128)(2,1)} copy(bf16[3,128,8,2,128]{4,3,2,1,0:T(2,128)(2,1)} %bitcast.16) | data formatting | bytes 3145728 | tf_op jit(solution)/shard_map/reshape | solution.py:176
  12.2 3.6 %all-to-all-done = s32[8,1,260]{2,1,0:T(1,128)S(1)} async-done(((s32[8,1,260]{2,1,0:T(1,128)}), s32[8,1,260]{2,1,0:T(1,128)S(1)}, u32[]{:S(2)}, u32[]{:S(2)}) %all-to-all-start) | async-done | bytes 8352 | tf_op jit(solution)/shard_map/all_to_all | solution.py:173
  15.8 3.7 %all-to-all-start.1 = ((bf16[8,3,2,128,128]{4,3,2,1,0:T(8,128)(2,1)}), bf16[8,3,2,128,128]{4,3,2,1,0:T(8,128)(2,1)S(1)}, u32[]{:S(2)}, u32[]{:S(2)}) async-start(bf16[8,3,2,128,128]{4,3,2,1,0:T(8,128)(2,1)} %bitcast.12), calls=%async_computation.1 | async-start | bytes 3145728 | tf_op jit(solution)/shard_map/all_to_all | solution.py:177
  19.5 2.5 %constant_dynamic-slice_fusion.18 = bf16[512,1280]{1,0:T(8,128)(2,1)} fusion(bf16[512,2560]{1,0:T(8,128)(2,1)} %bitcast.14, s32[]{:T(128)S(6)} %select_n.82), kind=kLoop, calls=%fused_computation.74 | loop fusion | bytes 2621444 | tf_op jit(solution)/shard_map/dynamic_slice | solution.py:185
  22.2 1.3 multiply_convert_fusion
  23.7 0.3 slice.7
  24.1 31.3 %all-to-all-done.1.recv = bf16[8,3,2,128,128]{4,3,2,1,0:T(8,128)(2,1)S(1)} async-done(((bf16[8,3,2,128,128]{4,3,2,1,0:T(8,128)(2,1)}), bf16[8,3,2,128,128]{4,3,2,1,0:T(8,128)(2,1)S(1)}, u32[]{:S(2)}, u32[]{:S(2)}) %all-to-all-start.1) | async-done | bytes 1572896 | tf_op jit(solution)/shard_map/all_to_all | solution.py:177
  55.5 3.0 %attend_rows.1 = bf16[1024,256]{1,0:T(8,128)(2,1)S(1)} custom-call(s32[8,4]{1,0:T(8,128)S(1)} %copy.25.assign, s32[4,256]{1,0:T(4,128)S(1)} %copy.26.seg_lane, s32[256,4]{1,0:T(8,128)S(1)} %bitcast.13, bf16[8,3,2,128,128]{4,3,2,1,0:T(8,128)(2,1)S(1)} %all-to-all-done.1.recv), custom_call_target="tpu_custom_call" | custom-call | flops 268435456 | bytes 2097152 | tf_op jit(solution)/shard_map/attend_rows/pallas_call | solution.py:132
  58.5 1.3 collective-permute-start.1
  59.8 2.0 %fusion.49 = (bf16[256,1280]{1,0:T(8,128)(2,1)S(1)}, bf16[256,1280]{1,0:T(8,128)(2,1)S(1)}) fusion(bf16[512,2560]{1,0:T(8,128)(2,1)} %bitcast.15, s32[]{:T(128)S(6)} %select_n.80, s32[]{:T(128)S(6)} %select_n.81, s32[]{:T(128)S(6)} %select_n.84), kind=kLoop, calls=%fused_computation.89 | loop fusion | bytes 2621452 | tf_op jit(solution)/shard_map/dynamic_slice | solution.py:204
  61.9 2.0 %collective-permute-start.8 = (bf16[256,1280]{1,0:T(8,128)(2,1)S(1)}, bf16[256,1280]{1,0:T(8,128)(2,1)S(1)}, u32[]{:S(2)}, u32[]{:S(2)}) collective-permute-start(bf16[256,1280]{1,0:T(8,128)(2,1)S(1)} %multiply_convert_fusion), channel_id=1, source_target_pairs={{0,4},{4,0},{8,12},{12,8},{1,5},{5,1},{9,13},{13,9},{2,6},{6,2},{1... | collective-permute-start | bytes 1966088 | tf_op jit(solution)/shard_map/ppermute | solution.py:195
  63.9 2.4 %collective-permute-start.12 = (bf16[256,1280]{1,0:T(8,128)(2,1)S(1)}, bf16[256,1280]{1,0:T(8,128)(2,1)S(1)}, u32[]{:S(2)}, u32[]{:S(2)}) collective-permute-start(bf16[256,1280]{1,0:T(8,128)(2,1)S(1)} %multiply_convert_fusion), channel_id=1, source_target_pairs={{0,12},{4,8},{8,4},{12,0},{1,13},{5,9},{9,5},{13,1},{2,14},{6,10},... | collective-permute-start | bytes 1966088 | tf_op jit(solution)/shard_map/ppermute | solution.py:195
  66.3 4.6 %collective-permute-done.1 = bf16[1024,256]{1,0:T(8,128)(2,1)S(1)} collective-permute-done((bf16[1024,256]{1,0:T(8,128)(2,1)S(1)}, bf16[1024,256]{1,0:T(8,128)(2,1)S(1)}, u32[]{:S(2)}, u32[]{:S(2)}) %collective-permute-start.1) | collective-permute-done | bytes 524320 | tf_op jit(solution)/shard_map/ppermute | solution.py:157
  70.9 1.4 constant_dynamic-slice_fusion.17
  72.6 0.6 collective-permute-start.2
  73.3 19.8 %collective-permute-done.10 = bf16[256,1280]{1,0:T(8,128)(2,1)S(1)} collective-permute-done((bf16[256,1280]{1,0:T(8,128)(2,1)S(1)}, bf16[256,1280]{1,0:T(8,128)(2,1)S(1)}, u32[]{:S(2)}, u32[]{:S(2)}) %collective-permute-start.10) | collective-permute-done | bytes 655392 | tf_op jit(solution)/shard_map/ppermute | solution.py:195
  93.1 14.0 %collective-permute-done.8 = bf16[256,1280]{1,0:T(8,128)(2,1)S(1)} collective-permute-done((bf16[256,1280]{1,0:T(8,128)(2,1)S(1)}, bf16[256,1280]{1,0:T(8,128)(2,1)S(1)}, u32[]{:S(2)}, u32[]{:S(2)}) %collective-permute-start.8) | collective-permute-done | bytes 655392 | tf_op jit(solution)/shard_map/ppermute | solution.py:195
  107.1 0.5 collective-permute-start.13
  107.6 0.3 maximum_select_fusion
  108.0 0.8 convolution_convert_fusion.2
  108.9 2.4 %collective-permute-start.4 = (bf16[256,1280]{1,0:T(8,128)(2,1)S(1)}, bf16[256,1280]{1,0:T(8,128)(2,1)S(1)}, u32[]{:S(2)}, u32[]{:S(2)}) collective-permute-start(bf16[256,1280]{1,0:T(8,128)(2,1)S(1)} %convolution_convert_fusion.2), channel_id=1, source_target_pairs={{0,12},{4,8},{8,4},{12,0},{1,13},{5,9},{9,5},{13,1},{2,14},{6,10},... | collective-permute-start | bytes 1966088 | tf_op jit(solution)/shard_map/ppermute | solution.py:217
  111.3 0.8 convolution_convert_fusion.1
  112.1 27.1 %collective-permute-start.5 = (bf16[256,1280]{1,0:T(8,128)(2,1)S(1)}, bf16[256,1280]{1,0:T(8,128)(2,1)S(1)}, u32[]{:S(2)}, u32[]{:S(2)}) collective-permute-start(bf16[256,1280]{1,0:T(8,128)(2,1)S(1)} %convolution_convert_fusion.1), channel_id=1, source_target_pairs={{0,8},{4,12},{8,0},{12,4},{1,9},{5,13},{9,1},{13,5},{2,10},{6,14},... | collective-permute-start | bytes 1966088 | tf_op jit(solution)/shard_map/ppermute | solution.py:217
  139.2 0.8 convolution_convert_fusion
  140.5 0.3 maximum_select_fusion.1
  140.9 0.3 maximum_select_fusion.3
  141.2 5.3 %fusion = f32[512,2560]{1,0:T(8,128)} fusion(bf16[256,2560]{1,0:T(8,128)(2,1)S(1)} %maximum_select_fusion.3, bf16[256,2560]{1,0:T(8,128)(2,1)S(1)} %maximum_select_fusion.2, bf16[256,2560]{1,0:T(8,128)(2,1)S(1)} %maximum_select_fusion.1, bf16[256,2560]{1,0:T(8,128)(2,1)S(1)} %maximum_select_fusion, bf16[256,512]{1,0:T(8,128)(2,1)S(1)} %get-tuple-element.21, ...), kind=kOutput, calls=%fused_computation | convolution fusion | flops 2709520384 | bytes 11534336 | tf_op jit(solution)/shard_map/dot_general | solution.py:223
  146.4 35.0 %collective-permute-done.5 = bf16[256,1280]{1,0:T(8,128)(2,1)S(1)} collective-permute-done((bf16[256,1280]{1,0:T(8,128)(2,1)S(1)}, bf16[256,1280]{1,0:T(8,128)(2,1)S(1)}, u32[]{:S(2)}, u32[]{:S(2)}) %collective-permute-start.5) | collective-permute-done | bytes 655392 | tf_op jit(solution)/shard_map/ppermute | solution.py:217
  181.5 1.7 fusion.8
  (35 shorter events, 1.6 us)
Async XLA Ops:
  2.0 13.8 %all-to-all-start = ((s32[8,1,260]{2,1,0:T(1,128)}), s32[8,1,260]{2,1,0:T(1,128)S(1)}, u32[]{:S(2)}, u32[]{:S(2)}) async-start(s32[8,1,260]{2,1,0:T(1,128)} %broadcast_in_dim.2), calls=%async_computation | async-start | bytes 24576 | tf_op jit(solution)/shard_map/all_to_all | solution.py:173
  15.8 6.2 %copy-start = (s32[1,256]{1,0:T(1,128)S(1)}, s32[1,256]{1,0:T(1,128)}, u32[]{:S(2)}) copy-start(s32[1,256]{1,0:T(1,128)} %param.8) | copy-start | bytes 3076
  15.8 6.3 %copy-start.1 = (f32[1,4]{1,0:T(1,128)S(1)}, f32[1,4]{1,0:T(1,128)}, u32[]{:S(2)}) copy-start(f32[1,4]{1,0:T(1,128)} %param.9) | copy-start | bytes 52
  15.8 39.7 %all-to-all-start.1 = ((bf16[8,3,2,128,128]{4,3,2,1,0:T(8,128)(2,1)}), bf16[8,3,2,128,128]{4,3,2,1,0:T(8,128)(2,1)S(1)}, u32[]{:S(2)}, u32[]{:S(2)}) async-start(bf16[8,3,2,128,128]{4,3,2,1,0:T(8,128)(2,1)} %bitcast.12), calls=%async_computation.1 | async-start | bytes 3145728 | tf_op jit(solution)/shard_map/all_to_all | solution.py:177
  22.0 41.9 %collective-permute-start.3 = (bf16[512,1280]{1,0:T(8,128)(2,1)}, bf16[512,1280]{1,0:T(8,128)(2,1)}, u32[]{:S(2)}, u32[]{:S(2)}) collective-permute-start(bf16[512,1280]{1,0:T(8,128)(2,1)} %constant_dynamic-slice_fusion.18), channel_id=1, source_target_pairs={{0,1},{1,0},{2,3},{3,2},{4,5},{5,4},{6,7},{7,6},{8,9},{9,8},{10,11... | collective-permute-start | bytes 3932168 | tf_op jit(solution)/shard_map/ppermute | solution.py:157
  58.5 12.4 %collective-permute-start.1 = (bf16[1024,256]{1,0:T(8,128)(2,1)S(1)}, bf16[1024,256]{1,0:T(8,128)(2,1)S(1)}, u32[]{:S(2)}, u32[]{:S(2)}) collective-permute-start(bf16[1024,256]{1,0:T(8,128)(2,1)S(1)} %attend_rows.1), channel_id=1, source_target_pairs={{0,2},{2,0},{1,3},{3,1},{4,6},{6,4},{5,7},{7,5},{8,10},{10,8},{9,1... | collective-permute-start | bytes 1572872 | tf_op jit(solution)/shard_map/ppermute | solution.py:157
  61.8 10.8 %collective-permute-start = (bf16[1024,256]{1,0:T(8,128)(2,1)S(1)}, bf16[1024,256]{1,0:T(8,128)(2,1)S(1)}, u32[]{:S(2)}, u32[]{:S(2)}) collective-permute-start(bf16[1024,256]{1,0:T(8,128)(2,1)S(1)} %attend_rows.1), channel_id=1, source_target_pairs={{0,1},{1,0},{2,3},{3,2},{4,5},{5,4},{6,7},{7,6},{8,9},{9,8},{10,11... | collective-permute-start | bytes 1572872 | tf_op jit(solution)/shard_map/ppermute | solution.py:157
  61.9 31.2 %collective-permute-start.10 = (bf16[256,1280]{1,0:T(8,128)(2,1)S(1)}, bf16[256,1280]{1,0:T(8,128)(2,1)S(1)}, u32[]{:S(2)}, u32[]{:S(2)}) collective-permute-start(bf16[256,1280]{1,0:T(8,128)(2,1)S(1)} %multiply_convert_fusion), channel_id=1, source_target_pairs={{0,8},{4,12},{8,0},{12,4},{1,9},{5,13},{9,1},{13,5},{2,10},{6,14},... | collective-permute-start | bytes 1966088 | tf_op jit(solution)/shard_map/ppermute | solution.py:195
  61.9 45.1 %collective-permute-start.8 = (bf16[256,1280]{1,0:T(8,128)(2,1)S(1)}, bf16[256,1280]{1,0:T(8,128)(2,1)S(1)}, u32[]{:S(2)}, u32[]{:S(2)}) collective-permute-start(bf16[256,1280]{1,0:T(8,128)(2,1)S(1)} %multiply_convert_fusion), channel_id=1, source_target_pairs={{0,4},{4,0},{8,12},{12,8},{1,5},{5,1},{9,13},{13,9},{2,6},{6,2},{1... | collective-permute-start | bytes 1966088 | tf_op jit(solution)/shard_map/ppermute | solution.py:195
  63.9 43.2 %collective-permute-start.12 = (bf16[256,1280]{1,0:T(8,128)(2,1)S(1)}, bf16[256,1280]{1,0:T(8,128)(2,1)S(1)}, u32[]{:S(2)}, u32[]{:S(2)}) collective-permute-start(bf16[256,1280]{1,0:T(8,128)(2,1)S(1)} %multiply_convert_fusion), channel_id=1, source_target_pairs={{0,12},{4,8},{8,4},{12,0},{1,13},{5,9},{9,5},{13,1},{2,14},{6,10},... | collective-permute-start | bytes 1966088 | tf_op jit(solution)/shard_map/ppermute | solution.py:195
  70.9 36.7 %collective-permute-start.7 = (bf16[256,1280]{1,0:T(8,128)(2,1)S(1)}, bf16[256,1280]{1,0:T(8,128)(2,1)S(1)}, u32[]{:S(2)}, u32[]{:S(2)}) collective-permute-start(bf16[256,1280]{1,0:T(8,128)(2,1)S(1)} %multiply_convert_fusion), channel_id=1, source_target_pairs={{0,1},{1,0},{2,3},{3,2},{4,5},{5,4},{6,7},{7,6},{8,9},{9,8},{10,11... | collective-permute-start | bytes 1966088 | tf_op jit(solution)/shard_map/ppermute | solution.py:157
  72.6 35.3 %collective-permute-start.2 = (bf16[1024,256]{1,0:T(8,128)(2,1)S(1)}, bf16[1024,256]{1,0:T(8,128)(2,1)S(1)}, u32[]{:S(2)}, u32[]{:S(2)}) collective-permute-start(bf16[1024,256]{1,0:T(8,128)(2,1)S(1)} %collective-permute-done.1), channel_id=1, source_target_pairs={{0,1},{1,0},{2,3},{3,2},{4,5},{5,4},{6,7},{7,6},{8,9},{9,8},{10,11... | collective-permute-start | bytes 1572872 | tf_op jit(solution)/shard_map/ppermute | solution.py:157
  93.1 47.0 %collective-permute-start.11 = (bf16[256,1280]{1,0:T(8,128)(2,1)S(1)}, bf16[256,1280]{1,0:T(8,128)(2,1)S(1)}, u32[]{:S(2)}, u32[]{:S(2)}) collective-permute-start(bf16[256,1280]{1,0:T(8,128)(2,1)S(1)} %collective-permute-done.10), channel_id=1, source_target_pairs={{0,1},{1,0},{2,3},{3,2},{4,5},{5,4},{6,7},{7,6},{8,9},{9,8},{10,11... | collective-permute-start | bytes 1966088 | tf_op jit(solution)/shard_map/ppermute | solution.py:157
  107.1 33.4 %collective-permute-start.9 = (bf16[256,1280]{1,0:T(8,128)(2,1)S(1)}, bf16[256,1280]{1,0:T(8,128)(2,1)S(1)}, u32[]{:S(2)}, u32[]{:S(2)}) collective-permute-start(bf16[256,1280]{1,0:T(8,128)(2,1)S(1)} %collective-permute-done.8), channel_id=1, source_target_pairs={{0,1},{1,0},{2,3},{3,2},{4,5},{5,4},{6,7},{7,6},{8,9},{9,8},{10,11... | collective-permute-start | bytes 1966088 | tf_op jit(solution)/shard_map/ppermute | solution.py:157
  107.1 33.8 %collective-permute-start.13 = (bf16[256,1280]{1,0:T(8,128)(2,1)S(1)}, bf16[256,1280]{1,0:T(8,128)(2,1)S(1)}, u32[]{:S(2)}, u32[]{:S(2)}) collective-permute-start(bf16[256,1280]{1,0:T(8,128)(2,1)S(1)} %collective-permute-done.12), channel_id=1, source_target_pairs={{0,1},{1,0},{2,3},{3,2},{4,5},{5,4},{6,7},{7,6},{8,9},{9,8},{10,11... | collective-permute-start | bytes 1966088 | tf_op jit(solution)/shard_map/ppermute | solution.py:157
  108.9 37.6 %collective-permute-start.4 = (bf16[256,1280]{1,0:T(8,128)(2,1)S(1)}, bf16[256,1280]{1,0:T(8,128)(2,1)S(1)}, u32[]{:S(2)}, u32[]{:S(2)}) collective-permute-start(bf16[256,1280]{1,0:T(8,128)(2,1)S(1)} %convolution_convert_fusion.2), channel_id=1, source_target_pairs={{0,12},{4,8},{8,4},{12,0},{1,13},{5,9},{9,5},{13,1},{2,14},{6,10},... | collective-permute-start | bytes 1966088 | tf_op jit(solution)/shard_map/ppermute | solution.py:217
  112.1 69.3 %collective-permute-start.5 = (bf16[256,1280]{1,0:T(8,128)(2,1)S(1)}, bf16[256,1280]{1,0:T(8,128)(2,1)S(1)}, u32[]{:S(2)}, u32[]{:S(2)}) collective-permute-start(bf16[256,1280]{1,0:T(8,128)(2,1)S(1)} %convolution_convert_fusion.1), channel_id=1, source_target_pairs={{0,8},{4,12},{8,0},{12,4},{1,9},{5,13},{9,1},{13,5},{2,10},{6,14},... | collective-permute-start | bytes 1966088 | tf_op jit(solution)/shard_map/ppermute | solution.py:217
  140.1 41.4 %collective-permute-start.6 = (bf16[256,1280]{1,0:T(8,128)(2,1)S(1)}, bf16[256,1280]{1,0:T(8,128)(2,1)S(1)}, u32[]{:S(2)}, u32[]{:S(2)}) collective-permute-start(bf16[256,1280]{1,0:T(8,128)(2,1)S(1)} %convolution_convert_fusion), channel_id=1, source_target_pairs={{0,4},{4,0},{8,12},{12,8},{1,5},{5,1},{9,13},{13,9},{2,6},{6,2},{1... | collective-permute-start | bytes 1966088 | tf_op jit(solution)/shard_map/ppermute | solution.py:217

commit v2 on v1

--- a/solution.py
+++ b/solution.py
@@ -9,6 +9,9 @@
 from jax.sharding import PartitionSpec as P
 
 CAP = 2
+SHORT = pl.CostEstimate(flops=1000, bytes_accessed=1000, transcendentals=0)
+ROW_AT = ((3, 2, 1, 0), (3, 2, 0, 1), (0, 1, 3, 2), (0, 1, 2, 3))
+PLACE_OF = ((3, 2, 1, 0), (2, 3, 1, 0), (0, 1, 3, 2), (0, 1, 2, 3))
 
 
 def attend_heads(queries, keys_all, values_all, seg_query, seg_key):
@@ -84,33 +87,44 @@
     return (mixed, weight_grad)
 
 
-def attention_kernel(rows, nseq, nblk, blk, assign, seg_lane, seg_sub, recv, out, packed, order):
-    heads, head_size = recv.shape[2], recv.shape[4]
-    row_len = seg_lane.shape[1]
+def attention_kernel(places, labels, nblk, blk, assign, row_at, place_of, segs, recv, out, packed, order):
+    heads, row_len, head_size = packed.shape[1:]
+    tokens = nblk * blk
+    rows = segs.shape[0]
+    nseq = recv.shape[0] // rows
     per_shard = row_len // nseq // blk
     for s in range(nseq):
         counts = [jnp.int32(0)] * rows
         for o in range(rows):
             for b in range(nblk):
-                target = assign[o * nseq + s, b]
+                target = place_of[assign[o * nseq + s, b]]
                 slot = counts[0]
                 for r in range(1, rows):
                     slot = jnp.where(target == r, counts[r], slot)
                 order[(target * nseq + s) * per_shard + slot] = o * nblk + b
                 counts = [counts[r] + (target == r).astype(jnp.int32) for r in range(rows)]
-    pos_query = lax.broadcasted_iota(jnp.int32, (row_len, row_len), 0)
-    pos_key = lax.broadcasted_iota(jnp.int32, (row_len, row_len), 1)
+    pos_query = lax.broadcasted_iota(jnp.int32, (row_len, 1), 0)
+    pos_key = lax.broadcasted_iota(jnp.int32, (1, row_len), 1)
     causal = pos_key <= pos_query
     scale = 1.0 / math.sqrt(head_size)
-    for r in range(rows):
-        keep = causal & (seg_sub[:, r : r + 1] == seg_lane[r : r + 1, :])
+    for i, r in enumerate(places):
+        ids = segs[pl.ds(row_at[r], 1), :]
+        query_id, key_id = jnp.zeros_like(pos_query), ids
+        for label in range(1, labels):
+            lower = jnp.sum((ids < label).astype(jnp.int32), axis=1, keepdims=True)
+            query_id = query_id + (pos_query >= lower).astype(jnp.int32)
+        keep = causal & (query_id == key_id)
         for s in range(nseq):
             for slot in range(per_shard):
                 source = order[(r * nseq + s) * per_shard + slot]
                 owner, block = lax.div(source, nblk), lax.rem(source, nblk)
                 first = pl.multiple_of(block * blk, blk)
                 place = (s * per_shard + slot) * blk
-                packed[:, :, place : place + blk, :] = recv[owner * nseq + s, :, :, pl.ds(first, blk), :]
+                for c in range(3):
+                    for h in range(heads):
+                        packed[c, h, place : place + blk, :] = recv[
+                            owner * nseq + s, pl.ds((c * heads + h) * tokens + first, blk), :
+                        ]
         for h in range(heads):
             scores = lax.dot_general(
                 packed[0, h], packed[1, h], (((1,), (1,)), ((), ())), preferred_element_type=jnp.float32
@@ -120,41 +134,91 @@
             expd = jnp.where(keep, jnp.exp(scores - rowmax), 0.0)
             probs = (expd / jnp.sum(expd, axis=-1, keepdims=True)).astype(jnp.bfloat16)
             attended = jnp.dot(probs, packed[2, h], preferred_element_type=jnp.float32)
-            out[r * row_len : (r + 1) * row_len, h * head_size : (h + 1) * head_size] = attended.astype(
+            out[i * row_len : (i + 1) * row_len, h * head_size : (h + 1) * head_size] = attended.astype(
                 jnp.bfloat16
             )
 
 
-def attend_rows(recv, assign, segs, nblk):
-    peers, _, heads, tokens, head_size = recv.shape
+def attend_rows(places, recv, assign, row_at, place_of, segs, labels, heads):
+    head_size = recv.shape[2]
     rows, row_len = segs.shape
-    nseq = peers // rows
+    nblk = assign.shape[1]
+    tokens = row_len * rows // recv.shape[0]
+    count = len(places)
+    smem, vmem = pl.BlockSpec(memory_space=pltpu.SMEM), pl.BlockSpec(memory_space=pltpu.VMEM)
     return pl.pallas_call(
-        functools.partial(attention_kernel, rows, nseq, nblk, tokens // nblk),
-        out_shape=jax.ShapeDtypeStruct((rows * row_len, heads * head_size), jnp.bfloat16),
-        in_specs=[
-            pl.BlockSpec(memory_space=pltpu.SMEM),
-            pl.BlockSpec(memory_space=pltpu.VMEM),
-            pl.BlockSpec(memory_space=pltpu.VMEM),
-            pl.BlockSpec(memory_space=pltpu.VMEM),
-        ],
-        out_specs=pl.BlockSpec(memory_space=pltpu.VMEM),
+        functools.partial(attention_kernel, places, labels, nblk, tokens // nblk),
+        out_shape=jax.ShapeDtypeStruct((count * row_len, heads * head_size), jnp.bfloat16),
+        in_specs=[smem, smem, smem, vmem, vmem],
+        out_specs=vmem,
         scratch_shapes=[
             pltpu.VMEM((3, heads, row_len, head_size), jnp.bfloat16),
-            pltpu.SMEM((rows * nblk * nseq,), jnp.int32),
+            pltpu.SMEM((recv.shape[0] * nblk,), jnp.int32),
         ],
         compiler_params=pltpu.CompilerParams(vmem_limit_bytes=32 << 20),
-        cost_estimate=pl.CostEstimate(
-            flops=4 * rows * heads * row_len * row_len * head_size,
-            bytes_accessed=recv.size * 2 + rows * row_len * heads * head_size * 2,
-            transcendentals=rows * heads * row_len * row_len,
+        cost_estimate=SHORT,
+        name="attend_rows",
+    )(assign, row_at, place_of, segs, recv)
+
+
+def gradient_kernel(place, far, near, far_seq, near_seq, *refs):
+    own, other, out, turned = refs[:4], refs[4:8], refs[8], refs[9]
+    width = far.shape[1]
+    row_len = own[0].shape[0]
+
+    @pl.when((pl.program_id(0) == 0) & (pl.program_id(1) == 0))
+    def _():
+        for s, parts in enumerate(((far, near), (far_seq, near_seq))):
+            first = pl.multiple_of(width * (place[0] if s == 0 else 1 - place[0]), width)
+            for i, part in enumerate(parts):
+                turned[pl.ds(first, width), 2 * i * row_len : 2 * (i + 1) * row_len] = part[...].T
+
+    for side, group in enumerate((own, other)):
+
+        @pl.when(pl.program_id(0) == side)
+        def _():
+            rows = jnp.concatenate([x[...] for x in group], 0)
+            out[...] = jnp.dot(turned[...], rows, preferred_element_type=jnp.float32)
+
+
+def weight_gradient(att, att_seq, pieces, others, my_seq, my_head):
+    width = att[0].shape[1]
+    row_len, half = pieces[0].shape
+    tile = math.gcd(half, 640)
+    tiles = half // tile
+    whole = pl.BlockSpec(att[0].shape, lambda side, t, place: (0, 0))
+    own = pl.BlockSpec((row_len, tile), lambda side, t, place: (0, jnp.where(side == 0, t, tiles - 1)))
+    other = pl.BlockSpec((row_len, tile), lambda side, t, place: (0, jnp.where(side == 0, 0, t)))
+    out = pl.BlockSpec(
+        (2 * width, tile), lambda side, t, place: (0, jnp.where(side == 0, place[1], 1 - place[1]) * tiles + t)
+    )
+    return pl.pallas_call(
+        gradient_kernel,
+        out_shape=jax.ShapeDtypeStruct((2 * width, 2 * half), jnp.float32),
+        grid_spec=pltpu.PrefetchScalarGridSpec(
+            num_scalar_prefetch=1,
+            grid=(2, tiles),
+            in_specs=[whole] * 4 + [own] * 4 + [other] * 4,
+            out_specs=out,
+            scratch_shapes=[pltpu.VMEM((2 * width, 4 * row_len), jnp.bfloat16)],
         ),
-        name="attend_rows",
-    )(assign, segs, segs.T, recv)
-
-
-def swap(x, axis):
-    return lax.ppermute(x, axis, [(0, 1), (1, 0)])
+        compiler_params=pltpu.CompilerParams(vmem_limit_bytes=40 << 20),
+        cost_estimate=SHORT,
+        name="weight_gradient",
+    )(jnp.stack([my_seq, my_head]).astype(jnp.int32), *att, *att_seq, *pieces, *others)
+
+
+def swap(x, axis, name="swap"):
+    with jax.named_scope(name):
+        return lax.ppermute(x, axis, [(0, 1), (1, 0)])
+
+
+def after(x, *first):
+    return lax.optimization_barrier((x, *first))[0]
+
+
+def add(x, y):
+    return (x.astype(jnp.float32) + y.astype(jnp.float32)).astype(jnp.bfloat16)
 
 
 def body_heads(projected, assignment, segments, advantage, out_weight, cotangent):
@@ -163,18 +227,20 @@
     tokens, pairs, head_size = projected.shape[1], projected.shape[2], projected.shape[4]
     nblk = assignment.shape[2]
     row_len = segments.shape[1]
-    mine = pairs // (ndp * nseq)
+    peers = ndp * nseq
+    mine = pairs // peers
     cols = out_weight.shape[3]
     half = cols // 2
     width = mine * head_size
 
-    small = jnp.concatenate([assignment.reshape(nblk), segments.reshape(row_len)])
-    small = jnp.broadcast_to(small[None], (ndp * nseq, nblk + row_len))
-    small = lax.all_to_all(small, ("dp", "seq"), split_axis=0, concat_axis=0, tiled=True)
-    assign, segs = small[:, :nblk], small[::nseq, nblk:]
-
-    sent = projected.reshape(3, tokens, ndp * nseq, mine, head_size).transpose(2, 0, 3, 1, 4)
+    sent = projected.reshape(3, tokens, peers, mine, head_size).transpose(2, 0, 3, 1, 4)
+    sent = sent.reshape(peers, 3 * mine * tokens, head_size)
+    small = [segments[0], assignment.reshape(nblk), jnp.zeros((16 * head_size - row_len - nblk,), jnp.int32)]
+    small = jnp.concatenate(small).astype(jnp.bfloat16).reshape(1, 16, head_size)
+    sent = jnp.concatenate([sent, jnp.broadcast_to(small, (peers, 16, head_size))], 1)
     recv = lax.all_to_all(sent, ("dp", "seq"), split_axis=0, concat_axis=0, tiled=True)
+    small = recv[:, 3 * mine * tokens :].astype(jnp.int32).reshape(peers, 16 * head_size)
+    assign, segs = small[:, row_len : row_len + nblk], small[::nseq, :row_len]
 
     weight = token_weight(segments[0], advantage[0])
     own_cols = lax.dynamic_slice_in_dim(cotangent, my_head * half, half, 1)
@@ -184,46 +250,61 @@
     keep_w = lax.dynamic_slice_in_dim(rows_w, my_head * half, half, 1)
     other_w = swap(lax.dynamic_slice_in_dim(rows_w, (1 - my_head) * half, half, 1), "head")
 
-    recv, scaled = lax.optimization_barrier((recv, scaled))
-    att = attend_rows(recv, assign, segs, nblk)
-
-    def both(x):
-        other = swap(x, "head")
-        return jnp.where(my_head == 0, jnp.concatenate([x, other], 1), jnp.concatenate([other, x], 1))
-
-    pieces = [scaled] + [
-        lax.ppermute(scaled, "dp", [(i, i ^ k) for i in range(ndp)]) for k in range(1, ndp)
-    ]
-    pieces = [both(x) for x in pieces]
-
-    att_seq = swap(att, "seq")
-    att_head = swap(att, "head")
-    att_diag = swap(att_seq, "head")
-
     def slab(w, s):
         return lax.dynamic_slice_in_dim(w, s * width, width, 0)
 
-    def rows_of(x, k):
-        return lax.dynamic_slice_in_dim(x, (me ^ k) * row_len, row_len, 0)
-
     weights = jnp.concatenate(
         [slab(keep_w, my_seq), slab(other_w, my_seq), slab(keep_w, 1 - my_seq), slab(other_w, 1 - my_seq)], 0
     )
-    terms = []
-    for k in reversed(range(ndp)):
-        row = jnp.concatenate([rows_of(x, k) for x in (att, att_head, att_seq, att_diag)], 1)
-        total = jnp.dot(row, weights, preferred_element_type=jnp.float32)
-        if k:
-            total = lax.ppermute(total.astype(jnp.bfloat16), "dp", [(i, i ^ k) for i in range(ndp)])
-        terms.append(total.astype(jnp.float32))
-    mixed = functools.reduce(jnp.add, terms).astype(jnp.bfloat16)
-
-    pair = jnp.where(my_seq == 0, jnp.concatenate([att, att_seq], 1), jnp.concatenate([att_seq, att], 1))
-    left = jnp.concatenate([rows_of(pair, k) for k in range(ndp)], 0)
-    grad = lax.dot_general(
-        left, jnp.concatenate(pieces, 0), (((0,), (0,)), ((), ())), preferred_element_type=jnp.float32
-    )
-    return mixed, grad.reshape(nseq * mine, 1, head_size, cols)
+
+    recv, assign, segs, scaled, weights = lax.optimization_barrier((recv, assign, segs, scaled, weights))
+
+    row_at = jnp.asarray(ROW_AT, jnp.int32)[me]
+    place_of = jnp.asarray(PLACE_OF, jnp.int32)[me]
+    attend = functools.partial(
+        attend_rows, assign=assign, row_at=row_at, place_of=place_of, segs=segs, labels=advantage.shape[1], heads=mine
+    )
+    across, middle = ((0, 1), (1, 0), (2, 3), (3, 2)), ((1, 2), (2, 1))
+
+    def send(x, perm, name):
+        with jax.named_scope(name):
+            return lax.ppermute(x, "dp", perm)
+
+    def project(att, att_head, att_seq, att_diag):
+        rows = jnp.concatenate([att, att_head, att_seq, att_diag], 1)
+        return jnp.dot(rows, weights, preferred_element_type=jnp.float32).astype(jnp.bfloat16)
+
+    inner = (me == 1) | (me == 2)
+
+    from_2, mid_1 = send(scaled, across, "swap_0"), send(scaled, middle, "mid_0")
+
+    far = attend((0, 1), recv)
+    far_seq, far_head = swap(far, "seq", "far_seq"), swap(far, "head", "far_head")
+    near = after(attend((2, 3), recv), far_seq)
+    far_seq, from_2, mid_1 = lax.optimization_barrier((far_seq, from_2, mid_1))
+    far_diag = swap(far_seq, "head", "far_diag")
+    near_seq, near_head = swap(near, "seq", "near_seq"), swap(near, "head", "near_head")
+    far_terms = project(far, far_head, far_seq, far_diag)
+    first, second = far_terms[:row_len], far_terms[row_len:]
+    near_diag = swap(near_seq, "head", "near_diag")
+    near_terms = project(near, near_head, near_seq, near_diag)
+    third, own = near_terms[:row_len], near_terms[row_len:]
+
+    swapped_1 = send(jnp.where(inner, mid_1, first), across, "swap_1")
+    mid_0 = send(after(from_2, first), middle, "mid_1")
+    swapped_1, mid_0, second, third = lax.optimization_barrier((swapped_1, mid_0, second, third))
+    swapped_2 = send(jnp.where(inner, mid_0, second), across, "swap_2")
+    crossed_2 = send(add(first, swapped_1), middle, "mid_2")
+    swapped_2, crossed_2 = lax.optimization_barrier((swapped_2, crossed_2))
+    swapped_3 = send(add(third, crossed_2), across, "swap_3")
+    crossed_3 = send(add(second, swapped_2), middle, "mid_3")
+
+    pieces = [jnp.where(inner, mid_0, swapped_2), jnp.where(inner, mid_1, swapped_1), from_2, scaled]
+    others = [swap(x, "head", f"piece_{i}") for i, x in enumerate(pieces)]
+    grad = weight_gradient((far, near), (far_seq, near_seq), pieces, others, my_seq, my_head)
+    swapped_3, crossed_3, grad = lax.optimization_barrier((swapped_3, crossed_3, grad))
+    mixed = own.astype(jnp.float32) + swapped_3.astype(jnp.float32) + crossed_3.astype(jnp.float32)
+    return mixed.astype(jnp.bfloat16), grad.reshape(nseq * mine, 1, head_size, cols)
 
 
 def solution(mesh):

time: 184 us -> 135 us (0.73)
  the two profiles are of different devices: /device:TPU:0 before, /device:TPU:8 now
where the time goes in v2:
time: 135 us; the launch traced here: 133 us
  waiting for transfers between devices  71.6 us (53%)
  starting transfers between devices  25.3 us (19%)
  Pallas kernels  11.7 us (9%)
  other arithmetic  10.1 us (7%)
  local copies, waits for them, and re-layouts  9.03 us (7%)
  matrix products  4.89 us (4%)
    ppermute x8, waiting for transfers between devices, send(): return lax.ppermute(x, 'dp', perm)  39.6 us
    all_to_all x1, waiting for transfers between devices, body_heads(): lax.all_to_all(sent, ('dp', 'seq'), split_axis=0, concat_axis=0, tiled=True)  26 us
    ppermute x8, starting transfers between devices, send(): return lax.ppermute(x, 'dp', perm)  14.5 us
    pallas_call x1, Pallas kernels, weight_gradient(): pl.pallas_call(gradient_kernel, out_shape=jax.ShapeDtypeStruct((2 * width...  7.48 us
    all_to_all x1, starting transfers between devices, body_heads(): lax.all_to_all(sent, ('dp', 'seq'), split_axis=0, concat_axis=0, tiled=True)  6.25 us
    ppermute x11, waiting for transfers between devices, swap(): return lax.ppermute(x, axis, [(0, 1), (1, 0)])  6.05 us
    dot_general x2, matrix products, project(): jnp.dot(rows, weights, preferred_element_type=jnp.float32)  4.89 us
    ppermute x11, starting transfers between devices, swap(): return lax.ppermute(x, axis, [(0, 1), (1, 0)])  4.52 us
  transfers between devices with their start and end apart: 20, of which 11 were waited for; matrix products, arithmetic and copies ran while one was open for 13% of the time, Pallas kernels for 9%

profile of v2, /device:TPU:8, one launch (start us, length us, event | category | flops | bytes accessed | tf_op | source)
XLA Modules:
  0.0 133.5 jit_solution(599913684411659371)
XLA Ops:
  2.0 1.8 %copy.12 = bf16[3,128,8,2,128]{4,1,3,0,2:T(8,128)(2,1)S(1)} copy(bf16[3,128,8,2,128]{4,3,2,1,0:T(2,128)(2,1)} %bitcast.30) | data formatting | bytes 3145728 | tf_op jit(solution)/shard_map/reshape | solution.py:236
  3.9 1.3 pad_maximum_fusion.1
  5.2 6.3 %all-to-all-start = ((bf16[8,784,128]{2,1,0:T(8,128)(2,1)}), bf16[8,784,128]{2,1,0:T(8,128)(2,1)S(1)}, u32[]{:S(2)}, u32[]{:S(2)}) async-start(bf16[8,784,128]{2,1,0:T(8,128)(2,1)} %pad_maximum_fusion.1), calls=%async_computation | async-start | bytes 3211264 | tf_op jit(solution)/shard_map/all_to_all | solution.py:241
  11.4 2.5 %constant_dynamic-slice_fusion.4 = bf16[512,1280]{1,0:T(8,128)(2,1)} fusion(bf16[512,2560]{1,0:T(8,128)(2,1)} %bitcast.28, s32[]{:T(128)S(6)} %select_n.49), kind=kLoop, calls=%fused_computation.37 | loop fusion | bytes 2621444 | tf_op jit(solution)/shard_map/dynamic_slice | solution.py:251
  14.2 2.0 %fusion.18 = (bf16[256,1280]{1,0:T(8,128)(2,1)S(1)}, bf16[256,1280]{1,0:T(8,128)(2,1)S(1)}) fusion(bf16[512,2560]{1,0:T(8,128)(2,1)} %bitcast.29, s32[]{:T(128)S(6)} %select_n.47, s32[]{:T(128)S(6)} %select_n.48, s32[]{:T(128)S(6)} %select_n.51), kind=kLoop, calls=%fused_computation.44 | loop fusion | bytes 2621452 | tf_op jit(solution)/shard_map/dynamic_slice | solution.py:254
  16.2 1.3 multiply_convert_fusion.refs_3_
  17.5 1.4 %constant_dynamic-slice_fusion.3 = (bf16[256,1280]{1,0:T(8,128)(2,1)S(1)}, bf16[256,1280]{1,0:T(8,128)(2,1)S(1)}) fusion(bf16[512,1280]{1,0:T(8,128)(2,1)} %collective-permute-done, s32[]{:T(128)S(6)} %select_n.46, s32[]{:T(128)S(6)} %select_n.50), kind=kLoop, calls=%fused_computation.36 | loop fusion | bytes 2621448 | tf_op jit(solution)/shard_map/dynamic_slice | solution.py:254
  18.9 1.6 %pad_maximum_fusion = bf16[1024,1280]{1,0:T(8,128)(2,1)} fusion(bf16[256,1280]{1,0:T(8,128)(2,1)S(1)} %get-tuple-element.51, bf16[256,1280]{1,0:T(8,128)(2,1)S(1)} %get-tuple-element.47, bf16[256,1280]{1,0:T(8,128)(2,1)S(1)} %get-tuple-element.50, bf16[256,1280]{1,0:T(8,128)(2,1)S(1)} %get-tuple-element.46), kind=kLoop, calls=%fused_computation.2 | loop fusion | flops 10485760 | bytes 5242880 | tf_op jit(solution)/shard_map/concatenate | solution.py:256
  20.5 26.0 %all-to-all-done.recv = bf16[8,784,128]{2,1,0:T(8,128)(2,1)S(1)} async-done(((bf16[8,784,128]{2,1,0:T(8,128)(2,1)}), bf16[8,784,128]{2,1,0:T(8,128)(2,1)S(1)}, u32[]{:S(2)}, u32[]{:S(2)}) %all-to-all-start) | async-done | bytes 1605664 | tf_op jit(solution)/shard_map/all_to_all | solution.py:241
  46.6 2.8 %collective-permute-start.6 = (bf16[256,1280]{1,0:T(8,128)(2,1)S(1)}, bf16[256,1280]{1,0:T(8,128)(2,1)}, u32[]{:S(2)}, u32[]{:S(2)}) collective-permute-start(bf16[256,1280]{1,0:T(8,128)(2,1)S(1)} %multiply_convert_fusion.refs_3_), channel_id=1, source_target_pairs={{4,8},{8,4},{5,9},{9,5},{6,10},{10,6},{7,11},{11,7},{20,24},{24,20... | collective-permute-start | bytes 1966088 | tf_op jit(solution)/shard_map/mid_0/ppermute | solution.py:271
  49.3 1.4 %collective-permute-start.5 = (bf16[256,1280]{1,0:T(8,128)(2,1)S(1)}, bf16[256,1280]{1,0:T(8,128)(2,1)S(1)}, u32[]{:S(2)}, u32[]{:S(2)}) collective-permute-start(bf16[256,1280]{1,0:T(8,128)(2,1)S(1)} %multiply_convert_fusion.refs_3_), channel_id=1, source_target_pairs={{0,4},{4,0},{8,12},{12,8},{1,5},{5,1},{9,13},{13,9},{2,6},{6,2},{1... | collective-permute-start | bytes 1966088 | tf_op jit(solution)/shard_map/swap_0/ppermute | solution.py:271
  51.5 2.1 %attend_rows.3.far = bf16[512,256]{1,0:T(8,128)(2,1)S(1)} custom-call(s32[8,4]{1,0:T(8,128)S(1)} %slice.29.assign, s32[4]{0:T(128)S(1)} %get-tuple-element.52.row_at, s32[4]{0:T(128)S(1)} %get-tuple-element.53.place_of, s32[4,256]{1,0:T(4,128)S(1)} %slice.23.segs, bf16[8,784,128]{2,1,0:T(8,128)(2,1)S(1)} %all-to-all-done.recv), custom_call_target="tpu_custom_call" | custom-call | flops 1000 | bytes 1000 | tf_op jit(solution)/shard_map/attend_rows/pallas_call | solution.py:149
  53.6 1.5 %collective-permute-start.1 = (bf16[512,256]{1,0:T(8,128)(2,1)S(1)}, bf16[512,256]{1,0:T(8,128)(2,1)}, u32[]{:S(2)}, u32[]{:S(2)}) collective-permute-start(bf16[512,256]{1,0:T(8,128)(2,1)S(1)} %attend_rows.3.far), channel_id=1, source_target_pairs={{0,2},{2,0},{1,3},{3,1},{4,6},{6,4},{5,7},{7,5},{8,10},{10,8},{9,1... | collective-permute-start | bytes 786440 | tf_op jit(solution)/shard_map/far_seq/ppermute | solution.py:213
  55.0 2.1 %attend_rows.2.near = bf16[512,256]{1,0:T(8,128)(2,1)S(1)} custom-call(s32[8,4]{1,0:T(8,128)S(1)} %slice.29.assign, s32[4]{0:T(128)S(1)} %get-tuple-element.52.row_at, s32[4]{0:T(128)S(1)} %get-tuple-element.53.place_of, s32[4,256]{1,0:T(4,128)S(1)} %slice.23.segs, bf16[8,784,128]{2,1,0:T(8,128)(2,1)S(1)} %all-to-all-done.recv), custom_call_target="tpu_custom_call" | custom-call | flops 1000 | bytes 1000 | tf_op jit(solution)/shard_map/attend_rows/pallas_call | solution.py:149
  57.1 3.3 %collective-permute-done.1.far_seq = bf16[512,256]{1,0:T(8,128)(2,1)} collective-permute-done((bf16[512,256]{1,0:T(8,128)(2,1)S(1)}, bf16[512,256]{1,0:T(8,128)(2,1)}, u32[]{:S(2)}, u32[]{:S(2)}) %collective-permute-start.1) | collective-permute-done | bytes 262176 | tf_op jit(solution)/shard_map/far_seq/ppermute | solution.py:213
  60.4 1.7 %collective-permute-start.3 = (bf16[512,256]{1,0:T(8,128)(2,1)S(1)}, bf16[512,256]{1,0:T(8,128)(2,1)S(1)}, u32[]{:S(2)}, u32[]{:S(2)}) collective-permute-start(bf16[512,256]{1,0:T(8,128)(2,1)S(1)} %attend_rows.2.near), channel_id=1, source_target_pairs={{0,2},{2,0},{1,3},{3,1},{4,6},{6,4},{5,7},{7,5},{8,10},{10,8},{9,1... | collective-permute-start | bytes 786440 | tf_op jit(solution)/shard_map/near_seq/ppermute | solution.py:213
  62.1 3.1 %collective-permute-done.6 = bf16[256,1280]{1,0:T(8,128)(2,1)} collective-permute-done((bf16[256,1280]{1,0:T(8,128)(2,1)S(1)}, bf16[256,1280]{1,0:T(8,128)(2,1)}, u32[]{:S(2)}, u32[]{:S(2)}) %collective-permute-start.6) | collective-permute-done | bytes 655392 | tf_op jit(solution)/shard_map/mid_0/ppermute | solution.py:271
  66.8 5.0 %collective-permute-start.10 = (bf16[256,1280]{1,0:T(8,128)(2,1)S(1)}, bf16[256,1280]{1,0:T(8,128)(2,1)S(1)}, u32[]{:S(2)}, u32[]{:S(2)}) collective-permute-start(bf16[256,1280]{1,0:T(8,128)(2,1)S(1)} %collective-permute-done.5.refs_2_), channel_id=1, source_target_pairs={{4,8},{8,4},{5,9},{9,5},{6,10},{10,6},{7,11},{11,7},{20,24},{24,20... | collective-permute-start | bytes 1966088 | tf_op jit(solution)/shard_map/mid_1/ppermute | solution.py:271
  71.8 3.4 %convolution_convert_fusion = bf16[512,1280]{1,0:T(8,128)(2,1)S(1)} fusion(bf16[1024,1280]{1,0:T(8,128)(2,1)} %pad_maximum_fusion, bf16[512,256]{1,0:T(8,128)(2,1)S(1)} %collective-permute-done.8, bf16[512,256]{1,0:T(8,128)(2,1)} %collective-permute-done.1.far_seq, bf16[512,256]{1,0:T(8,128)(2,1)S(1)} %collective-permute-done.7, ...), kind=kOutput, calls=%fused_computation | convolution fusion | flops 1347026944 | bytes 4980736 | tf_op jit(solution)/shard_map/dot_general | solution.py:275
  75.2 1.4 %fusion.19 = (bf16[256,1280]{1,0:T(8,128)(2,1)S(1)}, bf16[256,1280]{1,0:T(8,128)(2,1)S(1)}) fusion(bf16[512,1280]{1,0:T(8,128)(2,1)S(1)} %convolution_convert_fusion, bf16[256,1280]{1,0:T(8,128)(2,1)} %collective-permute-done.6, pred[]{:T(512)S(6)} %or.3), kind=kLoop, calls=%fused_computation.45 | loop fusion | flops 327680 | bytes 3276801 | tf_op jit(solution)/shard_map/slice | solution.py:288
  77.2 1.5 %convolution_convert_fusion.1 = bf16[512,1280]{1,0:T(8,128)(2,1)S(1)} fusion(bf16[1024,1280]{1,0:T(8,128)(2,1)S(1)} %copy-done, bf16[512,256]{1,0:T(8,128)(2,1)S(1)} %collective-permute-done.4, bf16[512,256]{1,0:T(8,128)(2,1)S(1)} %collective-permute-done.3.near_seq, bf16[512,256]{1,0:T(8,128)(2,1)S(1)} %collective-permute-done.2, ...), kind=kOutput, calls=%fused_computation.1 | convolution fusion | flops 1347026944 | bytes 4980736 | tf_op jit(solution)/shard_map/dot_general | solution.py:275
  78.7 8.5 %collective-permute-done.10 = bf16[256,1280]{1,0:T(8,128)(2,1)S(1)} collective-permute-done((bf16[256,1280]{1,0:T(8,128)(2,1)S(1)}, bf16[256,1280]{1,0:T(8,128)(2,1)S(1)}, u32[]{:S(2)}, u32[]{:S(2)}) %collective-permute-start.10) | collective-permute-done | bytes 655392 | tf_op jit(solution)/shard_map/mid_1/ppermute | solution.py:271
  87.2 6.3 %collective-permute-done.9 = bf16[256,1280]{1,0:T(8,128)(2,1)S(1)} collective-permute-done((bf16[256,1280]{1,0:T(8,128)(2,1)S(1)}, bf16[256,1280]{1,0:T(8,128)(2,1)S(1)}, u32[]{:S(2)}, u32[]{:S(2)}) %collective-permute-start.9) | collective-permute-done | bytes 655392 | tf_op jit(solution)/shard_map/swap_1/ppermute | solution.py:271
  94.1 2.2 %collective-permute-start.12 = (bf16[256,1280]{1,0:T(8,128)(2,1)S(1)}, bf16[256,1280]{1,0:T(8,128)(2,1)S(1)}, u32[]{:S(2)}, u32[]{:S(2)}) collective-permute-start(bf16[256,1280]{1,0:T(8,128)(2,1)S(1)} %add_convert_fusion.3), channel_id=1, source_target_pairs={{4,8},{8,4},{5,9},{9,5},{6,10},{10,6},{7,11},{11,7},{20,24},{24,20... | collective-permute-start | bytes 1966088 | tf_op jit(solution)/shard_map/mid_2/ppermute | solution.py:271
  96.9 1.2 broadcast_select_fusion.refs_1_
  98.2 11.7 %collective-permute-done.11 = bf16[256,1280]{1,0:T(8,128)(2,1)S(1)} collective-permute-done((bf16[256,1280]{1,0:T(8,128)(2,1)S(1)}, bf16[256,1280]{1,0:T(8,128)(2,1)S(1)}, u32[]{:S(2)}, u32[]{:S(2)}) %collective-permute-start.11) | collective-permute-done | bytes 655392 | tf_op jit(solution)/shard_map/swap_2/ppermute | solution.py:271
  109.9 2.2 %collective-permute-done.12 = bf16[256,1280]{1,0:T(8,128)(2,1)S(1)} collective-permute-done((bf16[256,1280]{1,0:T(8,128)(2,1)S(1)}, bf16[256,1280]{1,0:T(8,128)(2,1)S(1)}, u32[]{:S(2)}, u32[]{:S(2)}) %collective-permute-start.12) | collective-permute-done | bytes 655392 | tf_op jit(solution)/shard_map/mid_2/ppermute | solution.py:271
  112.3 2.6 %collective-permute-start.14 = (bf16[256,1280]{1,0:T(8,128)(2,1)S(1)}, bf16[256,1280]{1,0:T(8,128)(2,1)S(1)}, u32[]{:S(2)}, u32[]{:S(2)}) collective-permute-start(bf16[256,1280]{1,0:T(8,128)(2,1)S(1)} %add_convert_fusion.1), channel_id=1, source_target_pairs={{4,8},{8,4},{5,9},{9,5},{6,10},{10,6},{7,11},{11,7},{20,24},{24,20... | collective-permute-start | bytes 1966088 | tf_op jit(solution)/shard_map/mid_3/ppermute | solution.py:271
  115.4 1.7 %collective-permute-done.15.refs_4_ = bf16[256,1280]{1,0:T(8,128)(2,1)S(1)} collective-permute-done((bf16[256,1280]{1,0:T(8,128)(2,1)S(1)}, bf16[256,1280]{1,0:T(8,128)(2,1)S(1)}, u32[]{:S(2)}, u32[]{:S(2)}) %collective-permute-start.15) | collective-permute-done | bytes 655392 | tf_op jit(solution)/shard_map/piece_0/ppermute | solution.py:213
  117.1 7.5 %weight_gradient.1 = f32[512,2560]{1,0:T(8,128)} custom-call(s32[2]{0:T(128)S(1)} %pad_add_fusion.place, bf16[512,256]{1,0:T(8,128)(2,1)S(1)} %attend_rows.3.far, bf16[512,256]{1,0:T(8,128)(2,1)S(1)} %attend_rows.2.near, bf16[512,256]{1,0:T(8,128)(2,1)} %collective-permute-done.1.far_seq, bf16[512,256]{1,0:T(8,128)(2,1)S(1)} %collective-permute-done.3.near_seq, ...), custom_call_target="tpu_custom_call" | custom-call | flops 1000 | bytes 1000 | tf_op jit(solution)/shard_map/weight_gradient/pallas_call | solution.py:195
  124.6 4.8 %collective-permute-done.14 = bf16[256,1280]{1,0:T(8,128)(2,1)S(1)} collective-permute-done((bf16[256,1280]{1,0:T(8,128)(2,1)S(1)}, bf16[256,1280]{1,0:T(8,128)(2,1)S(1)}, u32[]{:S(2)}, u32[]{:S(2)}) %collective-permute-start.14) | collective-permute-done | bytes 655392 | tf_op jit(solution)/shard_map/mid_3/ppermute | solution.py:271
  129.4 3.0 %collective-permute-done.13 = bf16[256,1280]{1,0:T(8,128)(2,1)S(1)} collective-permute-done((bf16[256,1280]{1,0:T(8,128)(2,1)S(1)}, bf16[256,1280]{1,0:T(8,128)(2,1)S(1)}, u32[]{:S(2)}, u32[]{:S(2)}) %collective-permute-start.13) | collective-permute-done | bytes 655392 | tf_op jit(solution)/shard_map/swap_3/ppermute | solution.py:271
  (54 shorter events, 7.5 us)
Async XLA Ops:
  5.2 41.3 %all-to-all-start = ((bf16[8,784,128]{2,1,0:T(8,128)(2,1)}), bf16[8,784,128]{2,1,0:T(8,128)(2,1)S(1)}, u32[]{:S(2)}, u32[]{:S(2)}) async-start(bf16[8,784,128]{2,1,0:T(8,128)(2,1)} %pad_maximum_fusion.1), calls=%async_computation | async-start | bytes 3211264 | tf_op jit(solution)/shard_map/all_to_all | solution.py:241
  11.4 2.5 %copy-start.3 = (s32[1,256]{1,0:T(1,128)S(1)}, s32[1,256]{1,0:T(1,128)}, u32[]{:S(2)}) copy-start(s32[1,256]{1,0:T(1,128)} %param.10) | copy-start | bytes 3076
  11.4 2.6 %copy-start.4 = (f32[1,4]{1,0:T(1,128)S(1)}, f32[1,4]{1,0:T(1,128)}, u32[]{:S(2)}) copy-start(f32[1,4]{1,0:T(1,128)} %param.11) | copy-start | bytes 52
  13.9 3.5 %collective-permute-start = (bf16[512,1280]{1,0:T(8,128)(2,1)}, bf16[512,1280]{1,0:T(8,128)(2,1)}, u32[]{:S(2)}, u32[]{:S(2)}) collective-permute-start(bf16[512,1280]{1,0:T(8,128)(2,1)} %constant_dynamic-slice_fusion.4), channel_id=1, source_target_pairs={{0,1},{1,0},{2,3},{3,2},{4,5},{5,4},{6,7},{7,6},{8,9},{9,8},{10,11... | collective-permute-start | bytes 3932168 | tf_op jit(solution)/shard_map/swap/ppermute | solution.py:213
  46.6 18.7 %collective-permute-start.6 = (bf16[256,1280]{1,0:T(8,128)(2,1)S(1)}, bf16[256,1280]{1,0:T(8,128)(2,1)}, u32[]{:S(2)}, u32[]{:S(2)}) collective-permute-start(bf16[256,1280]{1,0:T(8,128)(2,1)S(1)} %multiply_convert_fusion.refs_3_), channel_id=1, source_target_pairs={{4,8},{8,4},{5,9},{9,5},{6,10},{10,6},{7,11},{11,7},{20,24},{24,20... | collective-permute-start | bytes 1966088 | tf_op jit(solution)/shard_map/mid_0/ppermute | solution.py:271
  49.3 15.9 %collective-permute-start.5 = (bf16[256,1280]{1,0:T(8,128)(2,1)S(1)}, bf16[256,1280]{1,0:T(8,128)(2,1)S(1)}, u32[]{:S(2)}, u32[]{:S(2)}) collective-permute-start(bf16[256,1280]{1,0:T(8,128)(2,1)S(1)} %multiply_convert_fusion.refs_3_), channel_id=1, source_target_pairs={{0,4},{4,0},{8,12},{12,8},{1,5},{5,1},{9,13},{13,9},{2,6},{6,2},{1... | collective-permute-start | bytes 1966088 | tf_op jit(solution)/shard_map/swap_0/ppermute | solution.py:271
  53.6 6.8 %collective-permute-start.1 = (bf16[512,256]{1,0:T(8,128)(2,1)S(1)}, bf16[512,256]{1,0:T(8,128)(2,1)}, u32[]{:S(2)}, u32[]{:S(2)}) collective-permute-start(bf16[512,256]{1,0:T(8,128)(2,1)S(1)} %attend_rows.3.far), channel_id=1, source_target_pairs={{0,2},{2,0},{1,3},{3,1},{4,6},{6,4},{5,7},{7,5},{8,10},{10,8},{9,1... | collective-permute-start | bytes 786440 | tf_op jit(solution)/shard_map/far_seq/ppermute | solution.py:213
  60.4 6.4 %collective-permute-start.3 = (bf16[512,256]{1,0:T(8,128)(2,1)S(1)}, bf16[512,256]{1,0:T(8,128)(2,1)S(1)}, u32[]{:S(2)}, u32[]{:S(2)}) collective-permute-start(bf16[512,256]{1,0:T(8,128)(2,1)S(1)} %attend_rows.2.near), channel_id=1, source_target_pairs={{0,2},{2,0},{1,3},{3,1},{4,6},{6,4},{5,7},{7,5},{8,10},{10,8},{9,1... | collective-permute-start | bytes 786440 | tf_op jit(solution)/shard_map/near_seq/ppermute | solution.py:213
  62.1 9.7 %collective-permute-start.7 = (bf16[512,256]{1,0:T(8,128)(2,1)S(1)}, bf16[512,256]{1,0:T(8,128)(2,1)S(1)}, u32[]{:S(2)}, u32[]{:S(2)}) collective-permute-start(bf16[512,256]{1,0:T(8,128)(2,1)S(1)} %attend_rows.3.far), channel_id=1, source_target_pairs={{0,1},{1,0},{2,3},{3,2},{4,5},{5,4},{6,7},{7,6},{8,9},{9,8},{10,11... | collective-permute-start | bytes 786440 | tf_op jit(solution)/shard_map/far_head/ppermute | solution.py:213
  65.2 6.6 %collective-permute-start.8 = (bf16[512,256]{1,0:T(8,128)(2,1)}, bf16[512,256]{1,0:T(8,128)(2,1)S(1)}, u32[]{:S(2)}, u32[]{:S(2)}) collective-permute-start(bf16[512,256]{1,0:T(8,128)(2,1)} %collective-permute-done.1.far_seq), channel_id=1, source_target_pairs={{0,1},{1,0},{2,3},{3,2},{4,5},{5,4},{6,7},{7,6},{8,9},{9,8},{10,11... | collective-permute-start | bytes 786440 | tf_op jit(solution)/shard_map/far_diag/ppermute | solution.py:213
  65.2 11.5 %collective-permute-start.2 = (bf16[512,256]{1,0:T(8,128)(2,1)S(1)}, bf16[512,256]{1,0:T(8,128)(2,1)S(1)}, u32[]{:S(2)}, u32[]{:S(2)}) collective-permute-start(bf16[512,256]{1,0:T(8,128)(2,1)S(1)} %attend_rows.2.near), channel_id=1, source_target_pairs={{0,1},{1,0},{2,3},{3,2},{4,5},{5,4},{6,7},{7,6},{8,9},{9,8},{10,11... | collective-permute-start | bytes 786440 | tf_op jit(solution)/shard_map/near_head/ppermute | solution.py:213
  66.8 9.9 %collective-permute-start.4 = (bf16[512,256]{1,0:T(8,128)(2,1)S(1)}, bf16[512,256]{1,0:T(8,128)(2,1)S(1)}, u32[]{:S(2)}, u32[]{:S(2)}) collective-permute-start(bf16[512,256]{1,0:T(8,128)(2,1)S(1)} %collective-permute-done.3.near_seq), channel_id=1, source_target_pairs={{0,1},{1,0},{2,3},{3,2},{4,5},{5,4},{6,7},{7,6},{8,9},{9,8},{10,11... | collective-permute-start | bytes 786440 | tf_op jit(solution)/shard_map/near_diag/ppermute | solution.py:213
  66.8 20.4 %collective-permute-start.10 = (bf16[256,1280]{1,0:T(8,128)(2,1)S(1)}, bf16[256,1280]{1,0:T(8,128)(2,1)S(1)}, u32[]{:S(2)}, u32[]{:S(2)}) collective-permute-start(bf16[256,1280]{1,0:T(8,128)(2,1)S(1)} %collective-permute-done.5.refs_2_), channel_id=1, source_target_pairs={{4,8},{8,4},{5,9},{9,5},{6,10},{10,6},{7,11},{11,7},{20,24},{24,20... | collective-permute-start | bytes 1966088 | tf_op jit(solution)/shard_map/mid_1/ppermute | solution.py:271
  75.2 1.9 %copy-start = (bf16[1024,1280]{1,0:T(8,128)(2,1)S(1)}, bf16[1024,1280]{1,0:T(8,128)(2,1)}, u32[]{:S(2)}) copy-start(bf16[1024,1280]{1,0:T(8,128)(2,1)} %pad_maximum_fusion) | copy-start | bytes 7864324
  76.6 16.9 %collective-permute-start.9 = (bf16[256,1280]{1,0:T(8,128)(2,1)S(1)}, bf16[256,1280]{1,0:T(8,128)(2,1)S(1)}, u32[]{:S(2)}, u32[]{:S(2)}) collective-permute-start(bf16[256,1280]{1,0:T(8,128)(2,1)S(1)} %get-tuple-element.49), channel_id=1, source_target_pairs={{0,4},{4,0},{8,12},{12,8},{1,5},{5,1},{9,13},{13,9},{2,6},{6,2},{1... | collective-permute-start | bytes 1966088 | tf_op jit(solution)/shard_map/swap_1/ppermute | solution.py:271
  78.7 15.1 %copy-start.1 = (bf16[512,1280]{1,0:T(8,128)(2,1)}, bf16[512,1280]{1,0:T(8,128)(2,1)S(1)}, u32[]{:S(2)}) copy-start(bf16[512,1280]{1,0:T(8,128)(2,1)S(1)} %convolution_convert_fusion.1) | copy-start | bytes 3932164
  93.8 16.1 %collective-permute-start.11 = (bf16[256,1280]{1,0:T(8,128)(2,1)S(1)}, bf16[256,1280]{1,0:T(8,128)(2,1)S(1)}, u32[]{:S(2)}, u32[]{:S(2)}) collective-permute-start(bf16[256,1280]{1,0:T(8,128)(2,1)S(1)} %broadcast_select_fusion.2), channel_id=1, source_target_pairs={{0,4},{4,0},{8,12},{12,8},{1,5},{5,1},{9,13},{13,9},{2,6},{6,2},{1... | collective-permute-start | bytes 1966088 | tf_op jit(solution)/shard_map/swap_2/ppermute | solution.py:271
  94.1 18.0 %collective-permute-start.12 = (bf16[256,1280]{1,0:T(8,128)(2,1)S(1)}, bf16[256,1280]{1,0:T(8,128)(2,1)S(1)}, u32[]{:S(2)}, u32[]{:S(2)}) collective-permute-start(bf16[256,1280]{1,0:T(8,128)(2,1)S(1)} %add_convert_fusion.3), channel_id=1, source_target_pairs={{4,8},{8,4},{5,9},{9,5},{6,10},{10,6},{7,11},{11,7},{20,24},{24,20... | collective-permute-start | bytes 1966088 | tf_op jit(solution)/shard_map/mid_2/ppermute | solution.py:271
  96.3 18.8 %collective-permute-start.18 = (bf16[256,1280]{1,0:T(8,128)(2,1)S(1)}, bf16[256,1280]{1,0:T(8,128)(2,1)S(1)}, u32[]{:S(2)}, u32[]{:S(2)}) collective-permute-start(bf16[256,1280]{1,0:T(8,128)(2,1)S(1)} %multiply_convert_fusion.refs_3_), channel_id=1, source_target_pairs={{0,1},{1,0},{2,3},{3,2},{4,5},{5,4},{6,7},{7,6},{8,9},{9,8},{10,11... | collective-permute-start | bytes 1966088 | tf_op jit(solution)/shard_map/piece_3/ppermute | solution.py:213
  96.4 18.9 %collective-permute-start.17 = (bf16[256,1280]{1,0:T(8,128)(2,1)S(1)}, bf16[256,1280]{1,0:T(8,128)(2,1)S(1)}, u32[]{:S(2)}, u32[]{:S(2)}) collective-permute-start(bf16[256,1280]{1,0:T(8,128)(2,1)S(1)} %collective-permute-done.5.refs_2_), channel_id=1, source_target_pairs={{0,1},{1,0},{2,3},{3,2},{4,5},{5,4},{6,7},{7,6},{8,9},{9,8},{10,11... | collective-permute-start | bytes 1966088 | tf_op jit(solution)/shard_map/piece_2/ppermute | solution.py:213
  98.1 16.9 %slice-start = ((bf16[512,1280]{1,0:T(8,128)(2,1)}), bf16[256,1280]{1,0:T(8,128)(2,1)S(1)}, s32[]{:S(2)}) async-start(bf16[512,1280]{1,0:T(8,128)(2,1)} %copy-done.1), calls=%async_computation.1 | async-start | bytes 1310720 | tf_op jit(solution)/shard_map/slice | solution.py:291
  98.1 17.3 %collective-permute-start.16 = (bf16[256,1280]{1,0:T(8,128)(2,1)S(1)}, bf16[256,1280]{1,0:T(8,128)(2,1)S(1)}, u32[]{:S(2)}, u32[]{:S(2)}) collective-permute-start(bf16[256,1280]{1,0:T(8,128)(2,1)S(1)} %broadcast_select_fusion.refs_1_), channel_id=1, source_target_pairs={{0,1},{1,0},{2,3},{3,2},{4,5},{5,4},{6,7},{7,6},{8,9},{9,8},{10,11... | collective-permute-start | bytes 1966088 | tf_op jit(solution)/shard_map/piece_1/ppermute | solution.py:213
  112.3 17.1 %collective-permute-start.14 = (bf16[256,1280]{1,0:T(8,128)(2,1)S(1)}, bf16[256,1280]{1,0:T(8,128)(2,1)S(1)}, u32[]{:S(2)}, u32[]{:S(2)}) collective-permute-start(bf16[256,1280]{1,0:T(8,128)(2,1)S(1)} %add_convert_fusion.1), channel_id=1, source_target_pairs={{4,8},{8,4},{5,9},{9,5},{6,10},{10,6},{7,11},{11,7},{20,24},{24,20... | collective-permute-start | bytes 1966088 | tf_op jit(solution)/shard_map/mid_3/ppermute | solution.py:271
  114.9 2.2 %collective-permute-start.15 = (bf16[256,1280]{1,0:T(8,128)(2,1)S(1)}, bf16[256,1280]{1,0:T(8,128)(2,1)S(1)}, u32[]{:S(2)}, u32[]{:S(2)}) collective-permute-start(bf16[256,1280]{1,0:T(8,128)(2,1)S(1)} %broadcast_select_fusion.1.refs_0_), channel_id=1, source_target_pairs={{0,1},{1,0},{2,3},{3,2},{4,5},{5,4},{6,7},{7,6},{8,9},{9,8},{10,11... | collective-permute-start | bytes 1966088 | tf_op jit(solution)/shard_map/piece_0/ppermute | solution.py:213
  115.2 17.2 %collective-permute-start.13 = (bf16[256,1280]{1,0:T(8,128)(2,1)S(1)}, bf16[256,1280]{1,0:T(8,128)(2,1)S(1)}, u32[]{:S(2)}, u32[]{:S(2)}) collective-permute-start(bf16[256,1280]{1,0:T(8,128)(2,1)S(1)} %add_convert_fusion.2), channel_id=1, source_target_pairs={{0,4},{4,0},{8,12},{12,8},{1,5},{5,1},{9,13},{13,9},{2,6},{6,2},{1... | collective-permute-start | bytes 1966088 | tf_op jit(solution)/shard_map/swap_3/ppermute | solution.py:271
  115.3 17.0 %copy-start.2 = (bf16[512,1280]{1,0:T(8,128)(2,1)S(1)}, bf16[512,1280]{1,0:T(8,128)(2,1)}, u32[]{:S(2)}) copy-start(bf16[512,1280]{1,0:T(8,128)(2,1)} %copy-done.1) | copy-start | bytes 3932164

commit v3 on v2

--- a/solution.py
+++ b/solution.py
@@ -161,6 +161,32 @@
     )(assign, row_at, place_of, segs, recv)
 
 
+def project_kernel(*refs):
+    parts, weights, outs = refs[:-3], refs[-3], refs[-2:]
+    rows = jnp.concatenate([x[...] for x in parts], 1)
+    total = jnp.dot(rows, weights[...], preferred_element_type=jnp.float32).astype(jnp.bfloat16)
+    for i, out in enumerate(outs):
+        out[...] = total[i * out.shape[0] : (i + 1) * out.shape[0]]
+
+
+def project(parts, weights):
+    tokens, width = parts[0].shape
+    depth, half = weights.shape
+    tile = math.gcd(half, 256)
+    whole = pl.BlockSpec((tokens, width), lambda t: (0, 0))
+    out = pl.BlockSpec((tokens // 2, tile), lambda t: (0, t))
+    return pl.pallas_call(
+        project_kernel,
+        out_shape=[jax.ShapeDtypeStruct((tokens // 2, half), jnp.bfloat16)] * 2,
+        grid=(half // tile,),
+        in_specs=[whole] * len(parts) + [pl.BlockSpec((depth, tile), lambda t: (0, t))],
+        out_specs=[out] * 2,
+        compiler_params=pltpu.CompilerParams(vmem_limit_bytes=32 << 20),
+        cost_estimate=SHORT,
+        name="project",
+    )(*parts, weights)
+
+
 def gradient_kernel(place, far, near, far_seq, near_seq, *refs):
     own, other, out, turned = refs[:4], refs[4:8], refs[8], refs[9]
     width = far.shape[1]
@@ -213,10 +239,6 @@
         return lax.ppermute(x, axis, [(0, 1), (1, 0)])
 
 
-def after(x, *first):
-    return lax.optimization_barrier((x, *first))[0]
-
-
 def add(x, y):
     return (x.astype(jnp.float32) + y.astype(jnp.float32)).astype(jnp.bfloat16)
 
@@ -270,33 +292,29 @@
         with jax.named_scope(name):
             return lax.ppermute(x, "dp", perm)
 
-    def project(att, att_head, att_seq, att_diag):
-        rows = jnp.concatenate([att, att_head, att_seq, att_diag], 1)
-        return jnp.dot(rows, weights, preferred_element_type=jnp.float32).astype(jnp.bfloat16)
-
     inner = (me == 1) | (me == 2)
 
     from_2, mid_1 = send(scaled, across, "swap_0"), send(scaled, middle, "mid_0")
 
     far = attend((0, 1), recv)
     far_seq, far_head = swap(far, "seq", "far_seq"), swap(far, "head", "far_head")
-    near = after(attend((2, 3), recv), far_seq)
-    far_seq, from_2, mid_1 = lax.optimization_barrier((far_seq, from_2, mid_1))
+    near = attend((2, 3), recv)
+    far_seq, near = lax.optimization_barrier((far_seq, near))
     far_diag = swap(far_seq, "head", "far_diag")
     near_seq, near_head = swap(near, "seq", "near_seq"), swap(near, "head", "near_head")
-    far_terms = project(far, far_head, far_seq, far_diag)
-    first, second = far_terms[:row_len], far_terms[row_len:]
+    first, second = project((far, far_head, far_seq, far_diag), weights)
     near_diag = swap(near_seq, "head", "near_diag")
-    near_terms = project(near, near_head, near_seq, near_diag)
-    third, own = near_terms[:row_len], near_terms[row_len:]
-
+    third, own = project((near, near_head, near_seq, near_diag), weights)
+
+    first, from_2 = lax.optimization_barrier((first, from_2))
     swapped_1 = send(jnp.where(inner, mid_1, first), across, "swap_1")
-    mid_0 = send(after(from_2, first), middle, "mid_1")
+    mid_0 = send(from_2, middle, "mid_1")
     swapped_1, mid_0, second, third = lax.optimization_barrier((swapped_1, mid_0, second, third))
     swapped_2 = send(jnp.where(inner, mid_0, second), across, "swap_2")
     crossed_2 = send(add(first, swapped_1), middle, "mid_2")
     swapped_2, crossed_2 = lax.optimization_barrier((swapped_2, crossed_2))
-    swapped_3 = send(add(third, crossed_2), across, "swap_3")
+    to_swap, second = lax.optimization_barrier((add(third, crossed_2), second))
+    swapped_3 = send(to_swap, across, "swap_3")
     crossed_3 = send(add(second, swapped_2), middle, "mid_3")
 
     pieces = [jnp.where(inner, mid_0, swapped_2), jnp.where(inner, mid_1, swapped_1), from_2, scaled]

time: 135 us -> 132 us (0.978)
  Pallas kernels: 11.7 us -> 19.4 us
  matrix products: 4.89 us -> 0 us
  starting transfers between devices: 25.3 us -> 22 us
  local copies, waits for them, and re-layouts: 9.03 us -> 7.02 us
  other arithmetic: 10.1 us -> 8.2 us
    ppermute x8, waiting for transfers between devices: 39.6 us -> 25.8 us  [send(): return lax.ppermute(x, 'dp', perm)]
    ppermute x11, waiting for transfers between devices: 6.05 us -> 17.5 us  [swap(): return lax.ppermute(x, axis, [(0, 1), (1, 0)])]
    pallas_call x0 -> x2, Pallas kernels: none -> 6.11 us  [project(): pl.pallas_call(project_kernel, out_shape=[jax.ShapeDtypeStruct((tokens //...]
    dot_general x2 -> x0, matrix products: 4.89 us -> none  [project(): jnp.dot(rows, weights, preferred_element_type=jnp.float32)]
    all_to_all x1, waiting for transfers between devices: 26 us -> 28.8 us  [body_heads(): lax.all_to_all(sent, ('dp', 'seq'), split_axis=0, concat_axis=0, tiled=True)]
    ppermute x8, starting transfers between devices: 14.5 us -> 12.7 us  [send(): return lax.ppermute(x, 'dp', perm)]
    ppermute x11, starting transfers between devices: 4.52 us -> 2.79 us  [swap(): return lax.ppermute(x, axis, [(0, 1), (1, 0)])]
    pallas_call x2, Pallas kernels: 4.18 us -> 5.83 us  [attend_rows(): pl.pallas_call(functools.partial(attention_kernel, places, labels, nblk,...]
  transfers between devices with their start and end apart: 20 -> 20, of which waited for: 11 -> 13; matrix products, arithmetic and copies ran while one was open for 13% -> 5% of each run, Pallas kernels for 9% -> 15%
where the time goes in v3:
time: 132 us; the launch traced here: 130 us
  waiting for transfers between devices  72.1 us (55%)
  starting transfers between devices  22 us (17%)
  Pallas kernels  19.4 us (15%)
  other arithmetic  8.2 us (6%)
  local copies, waits for them, and re-layouts  7.02 us (5%)
    all_to_all x1, waiting for transfers between devices, body_heads(): lax.all_to_all(sent, ('dp', 'seq'), split_axis=0, concat_axis=0, tiled=True)  28.8 us
    ppermute x8, waiting for transfers between devices, send(): return lax.ppermute(x, 'dp', perm)  25.8 us
    ppermute x11, waiting for transfers between devices, swap(): return lax.ppermute(x, axis, [(0, 1), (1, 0)])  17.5 us
    ppermute x8, starting transfers between devices, send(): return lax.ppermute(x, 'dp', perm)  12.7 us
    pallas_call x1, Pallas kernels, weight_gradient(): pl.pallas_call(gradient_kernel, out_shape=jax.ShapeDtypeStruct((2 * width...  7.51 us
    all_to_all x1, starting transfers between devices, body_heads(): lax.all_to_all(sent, ('dp', 'seq'), split_axis=0, concat_axis=0, tiled=True)  6.51 us
    pallas_call x2, Pallas kernels, project(): pl.pallas_call(project_kernel, out_shape=[jax.ShapeDtypeStruct((tokens //...  6.11 us
    pallas_call x2, Pallas kernels, attend_rows(): pl.pallas_call(functools.partial(attention_kernel, places, labels, nblk,...  5.83 us
  transfers between devices with their start and end apart: 20, of which 13 were waited for; matrix products, arithmetic and copies ran while one was open for 5% of the time, Pallas kernels for 15%

profile of v3, /device:TPU:8, one launch (start us, length us, event | category | flops | bytes accessed | tf_op | source)
XLA Modules:
  0.0 129.7 jit_solution(11166176604357960703)
XLA Ops:
  2.0 1.8 %copy.12 = bf16[3,128,8,2,128]{4,1,3,0,2:T(8,128)(2,1)S(1)} copy(bf16[3,128,8,2,128]{4,3,2,1,0:T(2,128)(2,1)} %bitcast.28) | data formatting | bytes 3145728 | tf_op jit(solution)/shard_map/reshape | solution.py:258
  3.9 1.3 pad_maximum_fusion.1
  5.2 6.5 %all-to-all-start = ((bf16[8,784,128]{2,1,0:T(8,128)(2,1)}), bf16[8,784,128]{2,1,0:T(8,128)(2,1)}, u32[]{:S(2)}, u32[]{:S(2)}) async-start(bf16[8,784,128]{2,1,0:T(8,128)(2,1)} %pad_maximum_fusion.1), calls=%async_computation | async-start | bytes 3211264 | tf_op jit(solution)/shard_map/all_to_all | solution.py:263
  11.7 1.2 constant_dynamic-slice_fusion.4
  14.4 1.9 %collective-permute-done = bf16[512,1280]{1,0:T(8,128)(2,1)} collective-permute-done((bf16[512,1280]{1,0:T(8,128)(2,1)}, bf16[512,1280]{1,0:T(8,128)(2,1)}, u32[]{:S(2)}, u32[]{:S(2)}) %collective-permute-start) | collective-permute-done | bytes 1310752 | tf_op jit(solution)/shard_map/swap/ppermute | solution.py:239
  16.2 1.4 %constant_dynamic-slice_fusion.3 = (bf16[256,1280]{1,0:T(8,128)(2,1)S(1)}, bf16[256,1280]{1,0:T(8,128)(2,1)S(1)}) fusion(bf16[512,1280]{1,0:T(8,128)(2,1)} %collective-permute-done, s32[]{:T(128)S(6)} %select_n.46, s32[]{:T(128)S(6)} %select_n.50), kind=kLoop, calls=%fused_computation.20 | loop fusion | bytes 2621448 | tf_op jit(solution)/shard_map/dynamic_slice | solution.py:276
  17.9 28.8 %all-to-all-done.recv = bf16[8,784,128]{2,1,0:T(8,128)(2,1)} async-done(((bf16[8,784,128]{2,1,0:T(8,128)(2,1)}), bf16[8,784,128]{2,1,0:T(8,128)(2,1)}, u32[]{:S(2)}, u32[]{:S(2)}) %all-to-all-start) | async-done | bytes 1605664 | tf_op jit(solution)/shard_map/all_to_all | solution.py:263
  47.5 2.8 %collective-permute-start.8 = (bf16[256,1280]{1,0:T(8,128)(2,1)S(1)}, bf16[256,1280]{1,0:T(8,128)(2,1)}, u32[]{:S(2)}, u32[]{:S(2)}) collective-permute-start(bf16[256,1280]{1,0:T(8,128)(2,1)S(1)} %multiply_convert_fusion.refs_3_), channel_id=1, source_target_pairs={{0,4},{4,0},{8,12},{12,8},{1,5},{5,1},{9,13},{13,9},{2,6},{6,2},{1... | collective-permute-start | bytes 1966088 | tf_op jit(solution)/shard_map/swap_0/ppermute | solution.py:293
  50.4 3.1 %collective-permute-start.5 = (bf16[256,1280]{1,0:T(8,128)(2,1)S(1)}, bf16[256,1280]{1,0:T(8,128)(2,1)}, u32[]{:S(2)}, u32[]{:S(2)}) collective-permute-start(bf16[256,1280]{1,0:T(8,128)(2,1)S(1)} %multiply_convert_fusion.refs_3_), channel_id=1, source_target_pairs={{4,8},{8,4},{5,9},{9,5},{6,10},{10,6},{7,11},{11,7},{20,24},{24,20... | collective-permute-start | bytes 1966088 | tf_op jit(solution)/shard_map/mid_0/ppermute | solution.py:293
  54.2 2.9 %attend_rows.2.refs_0_.far = bf16[512,256]{1,0:T(8,128)(2,1)S(1)} custom-call(s32[8,4]{1,0:T(8,128)S(1)} %slice.13.assign, s32[4]{0:T(128)S(1)} %get-tuple-element.60.row_at, s32[4]{0:T(128)S(1)} %get-tuple-element.61.place_of, s32[4,256]{1,0:T(4,128)S(1)} %slice.11.segs, bf16[8,784,128]{2,1,0:T(8,128)(2,1)} %all-to-all-done.recv), custom_call_target="tpu_custom_call" | custom-call | flops 1000 | bytes 1000 | tf_op jit(solution)/shard_map/attend_rows/pallas_call | solution.py:149
  58.0 2.9 %attend_rows.3.refs_0_.near = bf16[512,256]{1,0:T(8,128)(2,1)S(1)} custom-call(s32[8,4]{1,0:T(8,128)S(1)} %slice.13.assign, s32[4]{0:T(128)S(1)} %get-tuple-element.60.row_at, s32[4]{0:T(128)S(1)} %get-tuple-element.61.place_of, s32[4,256]{1,0:T(4,128)S(1)} %slice.11.segs, bf16[8,784,128]{2,1,0:T(8,128)(2,1)} %all-to-all-done.recv), custom_call_target="tpu_custom_call" | custom-call | flops 1000 | bytes 1000 | tf_op jit(solution)/shard_map/attend_rows/pallas_call | solution.py:149
  61.6 3.3 %collective-permute-done.1.refs_2_.far_seq = bf16[512,256]{1,0:T(8,128)(2,1)} collective-permute-done((bf16[512,256]{1,0:T(8,128)(2,1)S(1)}, bf16[512,256]{1,0:T(8,128)(2,1)}, u32[]{:S(2)}, u32[]{:S(2)}) %collective-permute-start.1) | collective-permute-done | bytes 262176 | tf_op jit(solution)/shard_map/far_seq/ppermute | solution.py:239
  64.9 1.9 %collective-permute-done.7.refs_3_ = bf16[512,256]{1,0:T(8,128)(2,1)} collective-permute-done((bf16[512,256]{1,0:T(8,128)(2,1)}, bf16[512,256]{1,0:T(8,128)(2,1)}, u32[]{:S(2)}, u32[]{:S(2)}) %collective-permute-start.7) | collective-permute-done | bytes 262176 | tf_op jit(solution)/shard_map/far_diag/ppermute | solution.py:239
  66.8 3.6 %project.3 = (bf16[256,1280]{1,0:T(8,128)(2,1)S(1)}, bf16[256,1280]{1,0:T(8,128)(2,1)S(1)}) custom-call(bf16[512,256]{1,0:T(8,128)(2,1)S(1)} %attend_rows.2.refs_0_.far, bf16[512,256]{1,0:T(8,128)(2,1)} %collective-permute-done.6.refs_1_, bf16[512,256]{1,0:T(8,128)(2,1)} %collective-permute-done.1.refs_2_.far_seq, ...), custom_call_target="tpu_custom_call" | custom-call | flops 1000 | bytes 1000 | tf_op jit(solution)/shard_map/project/pallas_call | solution.py:178
  70.5 1.2 broadcast_select_fusion.3
  71.7 2.2 %collective-permute-start.10 = (bf16[256,1280]{1,0:T(8,128)(2,1)}, bf16[256,1280]{1,0:T(8,128)(2,1)S(1)}, u32[]{:S(2)}, u32[]{:S(2)}) collective-permute-start(bf16[256,1280]{1,0:T(8,128)(2,1)} %collective-permute-done.8.refs_2_), channel_id=1, source_target_pairs={{4,8},{8,4},{5,9},{9,5},{6,10},{10,6},{7,11},{11,7},{20,24},{24,20... | collective-permute-start | bytes 1966088 | tf_op jit(solution)/shard_map/mid_1/ppermute | solution.py:293
  74.0 1.1 collective-permute-start.3
  75.0 7.0 %collective-permute-done.3.refs_2_.near_seq = bf16[512,256]{1,0:T(8,128)(2,1)S(1)} collective-permute-done((bf16[512,256]{1,0:T(8,128)(2,1)S(1)}, bf16[512,256]{1,0:T(8,128)(2,1)S(1)}, u32[]{:S(2)}, u32[]{:S(2)}) %collective-permute-start.3) | collective-permute-done | bytes 262176 | tf_op jit(solution)/shard_map/near_seq/ppermute | solution.py:239
  82.1 1.5 %collective-permute-done.4.refs_3_ = bf16[512,256]{1,0:T(8,128)(2,1)S(1)} collective-permute-done((bf16[512,256]{1,0:T(8,128)(2,1)S(1)}, bf16[512,256]{1,0:T(8,128)(2,1)S(1)}, u32[]{:S(2)}, u32[]{:S(2)}) %collective-permute-start.4) | collective-permute-done | bytes 262176 | tf_op jit(solution)/shard_map/near_diag/ppermute | solution.py:239
  83.6 2.5 %project.2 = (bf16[256,1280]{1,0:T(8,128)(2,1)S(1)}, bf16[256,1280]{1,0:T(8,128)(2,1)S(1)}) custom-call(bf16[512,256]{1,0:T(8,128)(2,1)S(1)} %copy-done.1, bf16[512,256]{1,0:T(8,128)(2,1)S(1)} %collective-permute-done.2.refs_1_, bf16[512,256]{1,0:T(8,128)(2,1)S(1)} %collective-permute-done.3.refs_2_.near_seq, ...), custom_call_target="tpu_custom_call" | custom-call | flops 1000 | bytes 1000 | tf_op jit(solution)/shard_map/project/pallas_call | solution.py:178
  86.1 2.4 %collective-permute-done.9 = bf16[256,1280]{1,0:T(8,128)(2,1)S(1)} collective-permute-done((bf16[256,1280]{1,0:T(8,128)(2,1)S(1)}, bf16[256,1280]{1,0:T(8,128)(2,1)S(1)}, u32[]{:S(2)}, u32[]{:S(2)}) %collective-permute-start.9) | collective-permute-done | bytes 655392 | tf_op jit(solution)/shard_map/swap_1/ppermute | solution.py:293
  88.5 2.1 %collective-permute-done.10 = bf16[256,1280]{1,0:T(8,128)(2,1)S(1)} collective-permute-done((bf16[256,1280]{1,0:T(8,128)(2,1)}, bf16[256,1280]{1,0:T(8,128)(2,1)S(1)}, u32[]{:S(2)}, u32[]{:S(2)}) %collective-permute-start.10) | collective-permute-done | bytes 655392 | tf_op jit(solution)/shard_map/mid_1/ppermute | solution.py:293
  91.0 2.2 %collective-permute-start.12 = (bf16[256,1280]{1,0:T(8,128)(2,1)S(1)}, bf16[256,1280]{1,0:T(8,128)(2,1)S(1)}, u32[]{:S(2)}, u32[]{:S(2)}) collective-permute-start(bf16[256,1280]{1,0:T(8,128)(2,1)S(1)} %add_convert_fusion.3), channel_id=1, source_target_pairs={{4,8},{8,4},{5,9},{9,5},{6,10},{10,6},{7,11},{11,7},{20,24},{24,20... | collective-permute-start | bytes 1966088 | tf_op jit(solution)/shard_map/mid_2/ppermute | solution.py:293
  93.7 1.2 broadcast_select_fusion.refs_1_
  95.1 11.8 %collective-permute-done.11 = bf16[256,1280]{1,0:T(8,128)(2,1)S(1)} collective-permute-done((bf16[256,1280]{1,0:T(8,128)(2,1)S(1)}, bf16[256,1280]{1,0:T(8,128)(2,1)S(1)}, u32[]{:S(2)}, u32[]{:S(2)}) %collective-permute-start.11) | collective-permute-done | bytes 655392 | tf_op jit(solution)/shard_map/swap_2/ppermute | solution.py:293
  106.9 1.9 %collective-permute-done.12 = bf16[256,1280]{1,0:T(8,128)(2,1)S(1)} collective-permute-done((bf16[256,1280]{1,0:T(8,128)(2,1)S(1)}, bf16[256,1280]{1,0:T(8,128)(2,1)S(1)}, u32[]{:S(2)}, u32[]{:S(2)}) %collective-permute-start.12) | collective-permute-done | bytes 655392 | tf_op jit(solution)/shard_map/mid_2/ppermute | solution.py:293
  109.2 2.2 %collective-permute-start.14 = (bf16[256,1280]{1,0:T(8,128)(2,1)S(1)}, bf16[256,1280]{1,0:T(8,128)(2,1)S(1)}, u32[]{:S(2)}, u32[]{:S(2)}) collective-permute-start(bf16[256,1280]{1,0:T(8,128)(2,1)S(1)} %add_convert_fusion.1), channel_id=1, source_target_pairs={{4,8},{8,4},{5,9},{9,5},{6,10},{10,6},{7,11},{11,7},{20,24},{24,20... | collective-permute-start | bytes 1966088 | tf_op jit(solution)/shard_map/mid_3/ppermute | solution.py:293
  111.7 1.9 %collective-permute-done.15.refs_4_ = bf16[256,1280]{1,0:T(8,128)(2,1)S(1)} collective-permute-done((bf16[256,1280]{1,0:T(8,128)(2,1)S(1)}, bf16[256,1280]{1,0:T(8,128)(2,1)S(1)}, u32[]{:S(2)}, u32[]{:S(2)}) %collective-permute-start.15) | collective-permute-done | bytes 655392 | tf_op jit(solution)/shard_map/piece_0/ppermute | solution.py:239
  113.6 7.5 %weight_gradient.1 = f32[512,2560]{1,0:T(8,128)} custom-call(s32[2]{0:T(128)S(1)} %pad_add_fusion.place, bf16[512,256]{1,0:T(8,128)(2,1)S(1)} %attend_rows.2.refs_0_.far, bf16[512,256]{1,0:T(8,128)(2,1)S(1)} %copy-done.1, bf16[512,256]{1,0:T(8,128)(2,1)} %collective-permute-done.1.refs_2_.far_seq, ...), custom_call_target="tpu_custom_call" | custom-call | flops 1000 | bytes 1000 | tf_op jit(solution)/shard_map/weight_gradient/pallas_call | solution.py:221
  121.1 5.0 %collective-permute-done.14 = bf16[256,1280]{1,0:T(8,128)(2,1)S(1)} collective-permute-done((bf16[256,1280]{1,0:T(8,128)(2,1)S(1)}, bf16[256,1280]{1,0:T(8,128)(2,1)S(1)}, u32[]{:S(2)}, u32[]{:S(2)}) %collective-permute-start.14) | collective-permute-done | bytes 655392 | tf_op jit(solution)/shard_map/mid_3/ppermute | solution.py:293
  126.1 2.5 %collective-permute-done.13 = bf16[256,1280]{1,0:T(8,128)(2,1)S(1)} collective-permute-done((bf16[256,1280]{1,0:T(8,128)(2,1)S(1)}, bf16[256,1280]{1,0:T(8,128)(2,1)S(1)}, u32[]{:S(2)}, u32[]{:S(2)}) %collective-permute-start.13) | collective-permute-done | bytes 655392 | tf_op jit(solution)/shard_map/swap_3/ppermute | solution.py:293
  128.6 1.1 add_convert_fusion
  (54 shorter events, 8.1 us)
Async XLA Ops:
  5.2 6.5 %copy-start.2 = (bf16[4,1,128,2560]{3,2,1,0:T(8,128)(2,1)S(1)}, bf16[4,1,128,2560]{3,2,1,0:T(8,128)(2,1)}, u32[]{:S(2)}) copy-start(bf16[4,1,128,2560]{3,2,1,0:T(8,128)(2,1)} %param.12) | copy-start | bytes 7864324
  5.2 41.6 %all-to-all-start = ((bf16[8,784,128]{2,1,0:T(8,128)(2,1)}), bf16[8,784,128]{2,1,0:T(8,128)(2,1)}, u32[]{:S(2)}, u32[]{:S(2)}) async-start(bf16[8,784,128]{2,1,0:T(8,128)(2,1)} %pad_maximum_fusion.1), calls=%async_computation | async-start | bytes 3211264 | tf_op jit(solution)/shard_map/all_to_all | solution.py:263
  11.7 1.2 copy-start.4
  11.7 1.3 %copy-start.5 = (f32[1,4]{1,0:T(1,128)S(1)}, f32[1,4]{1,0:T(1,128)}, u32[]{:S(2)}) copy-start(f32[1,4]{1,0:T(1,128)} %param.11) | copy-start | bytes 52
  12.8 3.4 %collective-permute-start = (bf16[512,1280]{1,0:T(8,128)(2,1)}, bf16[512,1280]{1,0:T(8,128)(2,1)}, u32[]{:S(2)}, u32[]{:S(2)}) collective-permute-start(bf16[512,1280]{1,0:T(8,128)(2,1)} %constant_dynamic-slice_fusion.4), channel_id=1, source_target_pairs={{0,1},{1,0},{2,3},{3,2},{4,5},{5,4},{6,7},{7,6},{8,9},{9,8},{10,11... | collective-permute-start | bytes 3932168 | tf_op jit(solution)/shard_map/swap/ppermute | solution.py:239
  12.9 1.3 %copy-start.3 = (bf16[256,2560]{1,0:T(8,128)(2,1)S(1)}, bf16[256,2560]{1,0:T(8,128)(2,1)}, u32[]{:S(2)}) copy-start(bf16[256,2560]{1,0:T(8,128)(2,1)} %param.13) | copy-start | bytes 3932164
  47.5 22.9 %collective-permute-start.8 = (bf16[256,1280]{1,0:T(8,128)(2,1)S(1)}, bf16[256,1280]{1,0:T(8,128)(2,1)}, u32[]{:S(2)}, u32[]{:S(2)}) collective-permute-start(bf16[256,1280]{1,0:T(8,128)(2,1)S(1)} %multiply_convert_fusion.refs_3_), channel_id=1, source_target_pairs={{0,4},{4,0},{8,12},{12,8},{1,5},{5,1},{9,13},{13,9},{2,6},{6,2},{1... | collective-permute-start | bytes 1966088 | tf_op jit(solution)/shard_map/swap_0/ppermute | solution.py:293
  50.4 20.1 %collective-permute-start.5 = (bf16[256,1280]{1,0:T(8,128)(2,1)S(1)}, bf16[256,1280]{1,0:T(8,128)(2,1)}, u32[]{:S(2)}, u32[]{:S(2)}) collective-permute-start(bf16[256,1280]{1,0:T(8,128)(2,1)S(1)} %multiply_convert_fusion.refs_3_), channel_id=1, source_target_pairs={{4,8},{8,4},{5,9},{9,5},{6,10},{10,6},{7,11},{11,7},{20,24},{24,20... | collective-permute-start | bytes 1966088 | tf_op jit(solution)/shard_map/mid_0/ppermute | solution.py:293
  57.1 7.8 %collective-permute-start.1 = (bf16[512,256]{1,0:T(8,128)(2,1)S(1)}, bf16[512,256]{1,0:T(8,128)(2,1)}, u32[]{:S(2)}, u32[]{:S(2)}) collective-permute-start(bf16[512,256]{1,0:T(8,128)(2,1)S(1)} %attend_rows.2.refs_0_.far), channel_id=1, source_target_pairs={{0,2},{2,0},{1,3},{3,1},{4,6},{6,4},{5,7},{7,5},{8,10},{10,8},{9,1... | collective-permute-start | bytes 786440 | tf_op jit(solution)/shard_map/far_seq/ppermute | solution.py:239
  60.9 0.7 copy-start
  61.6 3.3 %collective-permute-start.6 = (bf16[512,256]{1,0:T(8,128)(2,1)S(1)}, bf16[512,256]{1,0:T(8,128)(2,1)}, u32[]{:S(2)}, u32[]{:S(2)}) collective-permute-start(bf16[512,256]{1,0:T(8,128)(2,1)S(1)} %attend_rows.2.refs_0_.far), channel_id=1, source_target_pairs={{0,1},{1,0},{2,3},{3,2},{4,5},{5,4},{6,7},{7,6},{8,9},{9,8},{10,11... | collective-permute-start | bytes 786440 | tf_op jit(solution)/shard_map/far_head/ppermute | solution.py:239
  64.9 1.9 %collective-permute-start.7 = (bf16[512,256]{1,0:T(8,128)(2,1)}, bf16[512,256]{1,0:T(8,128)(2,1)}, u32[]{:S(2)}, u32[]{:S(2)}) collective-permute-start(bf16[512,256]{1,0:T(8,128)(2,1)} %collective-permute-done.1.refs_2_.far_seq), channel_id=1, source_target_pairs={{0,1},{1,0},{2,3},{3,2},{4,5},{5,4},{6,7},{7,6},{8,9},{9,8},{10,11... | collective-permute-start | bytes 786440 | tf_op jit(solution)/shard_map/far_diag/ppermute | solution.py:239
  70.4 3.5 %copy-start.1 = (bf16[512,256]{1,0:T(8,128)(2,1)S(1)}, bf16[512,256]{1,0:T(8,128)(2,1)}, u32[]{:S(2)}) copy-start(bf16[512,256]{1,0:T(8,128)(2,1)} %copy-done) | copy-start | bytes 786436
  71.7 16.8 %collective-permute-start.9 = (bf16[256,1280]{1,0:T(8,128)(2,1)S(1)}, bf16[256,1280]{1,0:T(8,128)(2,1)S(1)}, u32[]{:S(2)}, u32[]{:S(2)}) collective-permute-start(bf16[256,1280]{1,0:T(8,128)(2,1)S(1)} %broadcast_select_fusion.3), channel_id=1, source_target_pairs={{0,4},{4,0},{8,12},{12,8},{1,5},{5,1},{9,13},{13,9},{2,6},{6,2},{1... | collective-permute-start | bytes 1966088 | tf_op jit(solution)/shard_map/swap_1/ppermute | solution.py:293
  71.7 18.9 %collective-permute-start.10 = (bf16[256,1280]{1,0:T(8,128)(2,1)}, bf16[256,1280]{1,0:T(8,128)(2,1)S(1)}, u32[]{:S(2)}, u32[]{:S(2)}) collective-permute-start(bf16[256,1280]{1,0:T(8,128)(2,1)} %collective-permute-done.8.refs_2_), channel_id=1, source_target_pairs={{4,8},{8,4},{5,9},{9,5},{6,10},{10,6},{7,11},{11,7},{20,24},{24,20... | collective-permute-start | bytes 1966088 | tf_op jit(solution)/shard_map/mid_1/ppermute | solution.py:293
  74.0 8.1 %collective-permute-start.3 = (bf16[512,256]{1,0:T(8,128)(2,1)S(1)}, bf16[512,256]{1,0:T(8,128)(2,1)S(1)}, u32[]{:S(2)}, u32[]{:S(2)}) collective-permute-start(bf16[512,256]{1,0:T(8,128)(2,1)S(1)} %copy-done.1), channel_id=1, source_target_pairs={{0,2},{2,0},{1,3},{3,1},{4,6},{6,4},{5,7},{7,5},{8,10},{10,8},{9,1... | collective-permute-start | bytes 786440 | tf_op jit(solution)/shard_map/near_seq/ppermute | solution.py:239
  75.0 7.1 %collective-permute-start.2 = (bf16[512,256]{1,0:T(8,128)(2,1)S(1)}, bf16[512,256]{1,0:T(8,128)(2,1)S(1)}, u32[]{:S(2)}, u32[]{:S(2)}) collective-permute-start(bf16[512,256]{1,0:T(8,128)(2,1)S(1)} %copy-done.1), channel_id=1, source_target_pairs={{0,1},{1,0},{2,3},{3,2},{4,5},{5,4},{6,7},{7,6},{8,9},{9,8},{10,11... | collective-permute-start | bytes 786440 | tf_op jit(solution)/shard_map/near_head/ppermute | solution.py:239
  82.1 1.5 %collective-permute-start.4 = (bf16[512,256]{1,0:T(8,128)(2,1)S(1)}, bf16[512,256]{1,0:T(8,128)(2,1)S(1)}, u32[]{:S(2)}, u32[]{:S(2)}) collective-permute-start(bf16[512,256]{1,0:T(8,128)(2,1)S(1)} %collective-permute-done.3.refs_2_.near_seq), channel_id=1, source_target_pairs={{0,1},{1,0},{2,3},{3,2},{4,5},{5,4},{6,7},{7,6},{8,9},{9,8},{10,11... | collective-permute-start | bytes 786440 | tf_op jit(solution)/shard_map/near_diag/ppermute | solution.py:239
  90.9 16.0 %collective-permute-start.11 = (bf16[256,1280]{1,0:T(8,128)(2,1)S(1)}, bf16[256,1280]{1,0:T(8,128)(2,1)S(1)}, u32[]{:S(2)}, u32[]{:S(2)}) collective-permute-start(bf16[256,1280]{1,0:T(8,128)(2,1)S(1)} %broadcast_select_fusion.2), channel_id=1, source_target_pairs={{0,4},{4,0},{8,12},{12,8},{1,5},{5,1},{9,13},{13,9},{2,6},{6,2},{1... | collective-permute-start | bytes 1966088 | tf_op jit(solution)/shard_map/swap_2/ppermute | solution.py:293
  91.0 17.8 %collective-permute-start.12 = (bf16[256,1280]{1,0:T(8,128)(2,1)S(1)}, bf16[256,1280]{1,0:T(8,128)(2,1)S(1)}, u32[]{:S(2)}, u32[]{:S(2)}) collective-permute-start(bf16[256,1280]{1,0:T(8,128)(2,1)S(1)} %add_convert_fusion.3), channel_id=1, source_target_pairs={{4,8},{8,4},{5,9},{9,5},{6,10},{10,6},{7,11},{11,7},{20,24},{24,20... | collective-permute-start | bytes 1966088 | tf_op jit(solution)/shard_map/mid_2/ppermute | solution.py:293
  93.2 18.3 %collective-permute-start.18 = (bf16[256,1280]{1,0:T(8,128)(2,1)S(1)}, bf16[256,1280]{1,0:T(8,128)(2,1)S(1)}, u32[]{:S(2)}, u32[]{:S(2)}) collective-permute-start(bf16[256,1280]{1,0:T(8,128)(2,1)S(1)} %multiply_convert_fusion.refs_3_), channel_id=1, source_target_pairs={{0,1},{1,0},{2,3},{3,2},{4,5},{5,4},{6,7},{7,6},{8,9},{9,8},{10,11... | collective-permute-start | bytes 1966088 | tf_op jit(solution)/shard_map/piece_3/ppermute | solution.py:239
  93.2 18.4 %collective-permute-start.17 = (bf16[256,1280]{1,0:T(8,128)(2,1)}, bf16[256,1280]{1,0:T(8,128)(2,1)S(1)}, u32[]{:S(2)}, u32[]{:S(2)}) collective-permute-start(bf16[256,1280]{1,0:T(8,128)(2,1)} %collective-permute-done.8.refs_2_), channel_id=1, source_target_pairs={{0,1},{1,0},{2,3},{3,2},{4,5},{5,4},{6,7},{7,6},{8,9},{9,8},{10,11... | collective-permute-start | bytes 1966088 | tf_op jit(solution)/shard_map/piece_2/ppermute | solution.py:239
  94.9 16.7 %collective-permute-start.16 = (bf16[256,1280]{1,0:T(8,128)(2,1)S(1)}, bf16[256,1280]{1,0:T(8,128)(2,1)S(1)}, u32[]{:S(2)}, u32[]{:S(2)}) collective-permute-start(bf16[256,1280]{1,0:T(8,128)(2,1)S(1)} %broadcast_select_fusion.refs_1_), channel_id=1, source_target_pairs={{0,1},{1,0},{2,3},{3,2},{4,5},{5,4},{6,7},{7,6},{8,9},{9,8},{10,11... | collective-permute-start | bytes 1966088 | tf_op jit(solution)/shard_map/piece_1/ppermute | solution.py:239
  109.2 16.9 %collective-permute-start.14 = (bf16[256,1280]{1,0:T(8,128)(2,1)S(1)}, bf16[256,1280]{1,0:T(8,128)(2,1)S(1)}, u32[]{:S(2)}, u32[]{:S(2)}) collective-permute-start(bf16[256,1280]{1,0:T(8,128)(2,1)S(1)} %add_convert_fusion.1), channel_id=1, source_target_pairs={{4,8},{8,4},{5,9},{9,5},{6,10},{10,6},{7,11},{11,7},{20,24},{24,20... | collective-permute-start | bytes 1966088 | tf_op jit(solution)/shard_map/mid_3/ppermute | solution.py:293
  111.4 2.2 %collective-permute-start.15 = (bf16[256,1280]{1,0:T(8,128)(2,1)S(1)}, bf16[256,1280]{1,0:T(8,128)(2,1)S(1)}, u32[]{:S(2)}, u32[]{:S(2)}) collective-permute-start(bf16[256,1280]{1,0:T(8,128)(2,1)S(1)} %broadcast_select_fusion.1.refs_0_), channel_id=1, source_target_pairs={{0,1},{1,0},{2,3},{3,2},{4,5},{5,4},{6,7},{7,6},{8,9},{9,8},{10,11... | collective-permute-start | bytes 1966088 | tf_op jit(solution)/shard_map/piece_0/ppermute | solution.py:239
  111.5 17.1 %collective-permute-start.13 = (bf16[256,1280]{1,0:T(8,128)(2,1)S(1)}, bf16[256,1280]{1,0:T(8,128)(2,1)S(1)}, u32[]{:S(2)}, u32[]{:S(2)}) collective-permute-start(bf16[256,1280]{1,0:T(8,128)(2,1)S(1)} %add_convert_fusion.2), channel_id=1, source_target_pairs={{0,4},{4,0},{8,12},{12,8},{1,5},{5,1},{9,13},{13,9},{2,6},{6,2},{1... | collective-permute-start | bytes 1966088 | tf_op jit(solution)/shard_map/swap_3/ppermute | solution.py:293

commit v4 on v3

--- a/solution.py
+++ b/solution.py
@@ -85,6 +85,43 @@
         tiled=True,
     ).astype(jnp.float32)
     return (mixed, weight_grad)
+
+
+def pack_kernel(assign, segs, x, out):
+    peers, rows, head_size = out.shape
+    _, tokens, pairs, _ = x.shape
+    mine = pairs // peers
+    row_len = segs.shape[1]
+    line = lax.broadcasted_iota(jnp.int32, (16, head_size), 0)
+    lane = lax.broadcasted_iota(jnp.int32, (16, head_size), 1)
+    small = jnp.zeros((16, head_size), jnp.int32)
+    for i in range(row_len // head_size):
+        small = jnp.where(line == i, segs[:, i * head_size : (i + 1) * head_size], small)
+    for i in range(assign.shape[1]):
+        small = jnp.where((line == row_len // head_size) & (lane == i), assign[:, i : i + 1], small)
+    small = small.astype(jnp.float32).astype(jnp.bfloat16)
+    for p in range(peers):
+        out[p, rows - 16 :, :] = small
+    for c in range(3):
+        turned = jnp.swapaxes(x[c], 0, 1)
+        for p in range(peers):
+            for i in range(mine):
+                first = (c * mine + i) * tokens
+                out[p, first : first + tokens, :] = turned[p * mine + i]
+
+
+def pack(x, segs, assign, peers):
+    _, tokens, pairs, head_size = x.shape
+    vmem = pl.BlockSpec(memory_space=pltpu.VMEM)
+    return pl.pallas_call(
+        pack_kernel,
+        out_shape=jax.ShapeDtypeStruct((peers, 3 * tokens * pairs // peers + 16, head_size), x.dtype),
+        in_specs=[vmem, vmem, vmem],
+        out_specs=vmem,
+        compiler_params=pltpu.CompilerParams(vmem_limit_bytes=60 << 20),
+        cost_estimate=SHORT,
+        name="pack",
+    )(assign, segs, x)
 
 
 def attention_kernel(places, labels, nblk, blk, assign, row_at, place_of, segs, recv, out, packed, order):
@@ -155,33 +192,34 @@
             pltpu.VMEM((3, heads, row_len, head_size), jnp.bfloat16),
             pltpu.SMEM((recv.shape[0] * nblk,), jnp.int32),
         ],
-        compiler_params=pltpu.CompilerParams(vmem_limit_bytes=32 << 20),
+        compiler_params=pltpu.CompilerParams(vmem_limit_bytes=10 << 20),
         cost_estimate=SHORT,
         name="attend_rows",
     )(assign, row_at, place_of, segs, recv)
 
 
-def project_kernel(*refs):
+def project_kernel(tile, *refs):
     parts, weights, outs = refs[:-3], refs[-3], refs[-2:]
     rows = jnp.concatenate([x[...] for x in parts], 1)
-    total = jnp.dot(rows, weights[...], preferred_element_type=jnp.float32).astype(jnp.bfloat16)
-    for i, out in enumerate(outs):
-        out[...] = total[i * out.shape[0] : (i + 1) * out.shape[0]]
+
+    @pl.loop(0, weights.shape[1] // tile)
+    def _(t):
+        columns = pl.ds(pl.multiple_of(t * tile, tile), tile)
+        total = jnp.dot(rows, weights[:, columns], preferred_element_type=jnp.float32).astype(jnp.bfloat16)
+        for i, out in enumerate(outs):
+            out[:, columns] = total[i * out.shape[0] : (i + 1) * out.shape[0]]
 
 
 def project(parts, weights):
-    tokens, width = parts[0].shape
-    depth, half = weights.shape
-    tile = math.gcd(half, 256)
-    whole = pl.BlockSpec((tokens, width), lambda t: (0, 0))
-    out = pl.BlockSpec((tokens // 2, tile), lambda t: (0, t))
+    tokens = parts[0].shape[0]
+    half = weights.shape[1]
+    vmem = pl.BlockSpec(memory_space=pltpu.VMEM)
     return pl.pallas_call(
-        project_kernel,
+        functools.partial(project_kernel, math.gcd(half, 256)),
         out_shape=[jax.ShapeDtypeStruct((tokens // 2, half), jnp.bfloat16)] * 2,
-        grid=(half // tile,),
-        in_specs=[whole] * len(parts) + [pl.BlockSpec((depth, tile), lambda t: (0, t))],
-        out_specs=[out] * 2,
-        compiler_params=pltpu.CompilerParams(vmem_limit_bytes=32 << 20),
+        in_specs=[vmem] * (len(parts) + 1),
+        out_specs=[vmem] * 2,
+        compiler_params=pltpu.CompilerParams(vmem_limit_bytes=14 << 20),
         cost_estimate=SHORT,
         name="project",
     )(*parts, weights)
@@ -228,7 +266,7 @@
             out_specs=out,
             scratch_shapes=[pltpu.VMEM((2 * width, 4 * row_len), jnp.bfloat16)],
         ),
-        compiler_params=pltpu.CompilerParams(vmem_limit_bytes=40 << 20),
+        compiler_params=pltpu.CompilerParams(vmem_limit_bytes=20 << 20),
         cost_estimate=SHORT,
         name="weight_gradient",
     )(jnp.stack([my_seq, my_head]).astype(jnp.int32), *att, *att_seq, *pieces, *others)
@@ -255,11 +293,7 @@
     half = cols // 2
     width = mine * head_size
 
-    sent = projected.reshape(3, tokens, peers, mine, head_size).transpose(2, 0, 3, 1, 4)
-    sent = sent.reshape(peers, 3 * mine * tokens, head_size)
-    small = [segments[0], assignment.reshape(nblk), jnp.zeros((16 * head_size - row_len - nblk,), jnp.int32)]
-    small = jnp.concatenate(small).astype(jnp.bfloat16).reshape(1, 16, head_size)
-    sent = jnp.concatenate([sent, jnp.broadcast_to(small, (peers, 16, head_size))], 1)
+    sent = pack(projected.reshape(3, tokens, pairs, head_size), segments, assignment.reshape(1, nblk), peers)
     recv = lax.all_to_all(sent, ("dp", "seq"), split_axis=0, concat_axis=0, tiled=True)
     small = recv[:, 3 * mine * tokens :].astype(jnp.int32).reshape(peers, 16 * head_size)
     assign, segs = small[:, row_len : row_len + nblk], small[::nseq, :row_len]
@@ -279,10 +313,13 @@
         [slab(keep_w, my_seq), slab(other_w, my_seq), slab(keep_w, 1 - my_seq), slab(other_w, 1 - my_seq)], 0
     )
 
-    recv, assign, segs, scaled, weights = lax.optimization_barrier((recv, assign, segs, scaled, weights))
-
     row_at = jnp.asarray(ROW_AT, jnp.int32)[me]
     place_of = jnp.asarray(PLACE_OF, jnp.int32)[me]
+    early = scaled
+    recv, assign, segs, scaled, weights, row_at, place_of = lax.optimization_barrier(
+        (recv, assign, segs, scaled, weights, row_at, place_of)
+    )
+
     attend = functools.partial(
         attend_rows, assign=assign, row_at=row_at, place_of=place_of, segs=segs, labels=advantage.shape[1], heads=mine
     )
@@ -294,9 +331,10 @@
 
     inner = (me == 1) | (me == 2)
 
-    from_2, mid_1 = send(scaled, across, "swap_0"), send(scaled, middle, "mid_0")
+    from_2, mid_1 = send(early, across, "swap_0"), send(scaled, middle, "mid_0")
 
     far = attend((0, 1), recv)
+    far, from_2 = lax.optimization_barrier((far, from_2))
     far_seq, far_head = swap(far, "seq", "far_seq"), swap(far, "head", "far_head")
     near = attend((2, 3), recv)
     far_seq, near = lax.optimization_barrier((far_seq, near))
@@ -306,8 +344,8 @@
     near_diag = swap(near_seq, "head", "near_diag")
     third, own = project((near, near_head, near_seq, near_diag), weights)
 
-    first, from_2 = lax.optimization_barrier((first, from_2))
-    swapped_1 = send(jnp.where(inner, mid_1, first), across, "swap_1")
+    to_swap, from_2 = lax.optimization_barrier((jnp.where(inner, mid_1, first), from_2))
+    swapped_1 = send(to_swap, across, "swap_1")
     mid_0 = send(from_2, middle, "mid_1")
     swapped_1, mid_0, second, third = lax.optimization_barrier((swapped_1, mid_0, second, third))
     swapped_2 = send(jnp.where(inner, mid_0, second), across, "swap_2")
@@ -320,7 +358,7 @@
     pieces = [jnp.where(inner, mid_0, swapped_2), jnp.where(inner, mid_1, swapped_1), from_2, scaled]
     others = [swap(x, "head", f"piece_{i}") for i, x in enumerate(pieces)]
     grad = weight_gradient((far, near), (far_seq, near_seq), pieces, others, my_seq, my_head)
-    swapped_3, crossed_3, grad = lax.optimization_barrier((swapped_3, crossed_3, grad))
+    swapped_3, grad = lax.optimization_barrier((swapped_3, grad))
     mixed = own.astype(jnp.float32) + swapped_3.astype(jnp.float32) + crossed_3.astype(jnp.float32)
     return mixed.astype(jnp.bfloat16), grad.reshape(nseq * mine, 1, head_size, cols)
 

time: 132 us -> 125 us (0.947); the launches traced: 130 us -> 124 us
  waiting for transfers between devices: 72.1 us -> 65.8 us
  Pallas kernels: 19.4 us -> 22.2 us
  local copies, waits for them, and re-layouts: 7.02 us -> 4.7 us
  starting transfers between devices: 22 us -> 24 us
  other arithmetic: 8.2 us -> 6.59 us
    ppermute x11, waiting for transfers between devices: 17.5 us -> 13.2 us  [swap(): return lax.ppermute(x, axis, [(0, 1), (1, 0)])]
    pallas_call x2 -> x3, Pallas kernels: 6.11 us -> 8.85 us  [the longest x2 5.67 us: project(): pl.pallas_call(functools.partial(project_kernel, math.gcd(half, 256)), ou...]
    ppermute x8, waiting for transfers between devices: 25.8 us -> 23.8 us  [send(): return lax.ppermute(x, 'dp', perm)]
    reshape x1 -> x0, local copies, waits for them, and re-layouts: 1.81 us -> none  [body_heads(): projected.reshape(3, tokens, peers, mine, head_size)]
    ppermute x8, starting transfers between devices: 12.7 us -> 14.2 us  [send(): return lax.ppermute(x, 'dp', perm)]
  transfers between devices with their start and end apart: 20 -> 20, of which waited for: 13 -> 13; matrix products, arithmetic and copies ran while one was open for 5% -> 7% of each run, Pallas kernels for 15% -> 15%
where the time goes in v4:
time: 125 us; the launch traced here: 124 us
  waiting for transfers between devices  65.8 us (53%)
  starting transfers between devices  24 us (19%)
  Pallas kernels  22.2 us (18%)
  other arithmetic  6.59 us (5%)
  local copies, waits for them, and re-layouts  4.7 us (4%)
    all_to_all x1, waiting for transfers between devices, body_heads(): lax.all_to_all(sent, ('dp', 'seq'), split_axis=0, concat_axis=0, tiled=True)  28.9 us
    ppermute x8, waiting for transfers between devices, send(): return lax.ppermute(x, 'dp', perm)  23.8 us
    ppermute x8, starting transfers between devices, send(): return lax.ppermute(x, 'dp', perm)  14.2 us
    ppermute x11, waiting for transfers between devices, swap(): return lax.ppermute(x, axis, [(0, 1), (1, 0)])  13.2 us
    pallas_call x1, Pallas kernels, weight_gradient(): pl.pallas_call(gradient_kernel, out_shape=jax.ShapeDtypeStruct((2 * width...  7.52 us
    all_to_all x1, starting transfers between devices, body_heads(): lax.all_to_all(sent, ('dp', 'seq'), split_axis=0, concat_axis=0, tiled=True)  6.51 us
    pallas_call x2, Pallas kernels, attend_rows(): pl.pallas_call(functools.partial(attention_kernel, places, labels, nblk,...  5.83 us
    pallas_call x2, Pallas kernels, project(): pl.pallas_call(functools.partial(project_kernel, math.gcd(half, 256)), ou...  5.67 us
  transfers between devices with their start and end apart: 20, of which 13 were waited for; matrix products, arithmetic and copies ran while one was open for 7% of the time, Pallas kernels for 15%

profile of v4, /device:TPU:8, one launch (start us, length us, event | category | flops | bytes accessed | tf_op | source)
XLA Modules:
  0.0 124.1 jit_solution(16760191047024853685)
XLA Ops:
  0.6 3.2 %pack.1 = bf16[8,784,128]{2,1,0:T(8,128)(2,1)} custom-call(s32[1,4]{1,0:T(1,128)} %bitcast.27, s32[1,256]{1,0:T(1,128)} %segs.1, bf16[3,128,16,128]{3,2,1,0:T(8,128)(2,1)} %bitcast.22), custom_call_target="tpu_custom_call" | custom-call | flops 1000 | bytes 1000 | tf_op jit(solution)/shard_map/pack/pallas_call | solution.py:116
  3.8 6.5 %all-to-all-start = ((bf16[8,784,128]{2,1,0:T(8,128)(2,1)}), bf16[8,784,128]{2,1,0:T(8,128)(2,1)}, u32[]{:S(2)}, u32[]{:S(2)}) async-start(bf16[8,784,128]{2,1,0:T(8,128)(2,1)} %pack.1), calls=%async_computation | async-start | bytes 3211264 | tf_op jit(solution)/shard_map/all_to_all | solution.py:297
  10.3 1.2 constant_dynamic-slice_fusion.4
  11.7 1.3 %multiply_convert_fusion.refs_3_ = bf16[256,1280]{1,0:T(8,128)(2,1)S(1)} fusion(f32[256]{0:T(256)S(1)} %div.7, bf16[256,2560]{1,0:T(8,128)(2,1)} %param.13, s32[]{:T(128)S(6)} %select_n.45), kind=kLoop, calls=%fused_computation.5 | loop fusion | flops 983040 | bytes 1311748 | tf_op jit(solution)/shard_map/convert_element_type | solution.py:303
  13.1 0.7 fusion
  14.9 1.4 %constant_dynamic-slice_fusion.3 = (bf16[256,1280]{1,0:T(8,128)(2,1)S(1)}, bf16[256,1280]{1,0:T(8,128)(2,1)S(1)}) fusion(bf16[512,1280]{1,0:T(8,128)(2,1)} %collective-permute-done, s32[]{:T(128)S(6)} %select_n.46, s32[]{:T(128)S(6)} %select_n.50), kind=kLoop, calls=%fused_computation.19 | loop fusion | bytes 2621448 | tf_op jit(solution)/shard_map/dynamic_slice | solution.py:310
  16.5 28.9 %all-to-all-done.recv = bf16[8,784,128]{2,1,0:T(8,128)(2,1)} async-done(((bf16[8,784,128]{2,1,0:T(8,128)(2,1)}), bf16[8,784,128]{2,1,0:T(8,128)(2,1)}, u32[]{:S(2)}, u32[]{:S(2)}) %all-to-all-start) | async-done | bytes 1605664 | tf_op jit(solution)/shard_map/all_to_all | solution.py:297
  45.4 0.8 convert_bitcast_fusion
  46.2 2.8 %collective-permute-start.6 = (bf16[256,1280]{1,0:T(8,128)(2,1)S(1)}, bf16[256,1280]{1,0:T(8,128)(2,1)}, u32[]{:S(2)}, u32[]{:S(2)}) collective-permute-start(bf16[256,1280]{1,0:T(8,128)(2,1)S(1)} %multiply_convert_fusion.refs_3_), channel_id=1, source_target_pairs={{4,8},{8,4},{5,9},{9,5},{6,10},{10,6},{7,11},{11,7},{20,24},{24,20... | collective-permute-start | bytes 1966088 | tf_op jit(solution)/shard_map/mid_0/ppermute | solution.py:330
  49.0 2.9 %attend_rows.2.refs_0_.far = bf16[512,256]{1,0:T(8,128)(2,1)S(1)} custom-call(s32[8,4]{1,0:T(8,128)S(1)} %slice.13.assign, s32[4]{0:T(128)S(1)} %get-tuple-element.30.row_at, s32[4]{0:T(128)S(1)} %get-tuple-element.31.place_of, s32[4,256]{1,0:T(4,128)S(1)} %slice.11.segs, bf16[8,784,128]{2,1,0:T(8,128)(2,1)} %all-to-all-done.recv), custom_call_target="tpu_custom_call" | custom-call | flops 1000 | bytes 1000 | tf_op jit(solution)/shard_map/attend_rows/pallas_call | solution.py:186
  51.9 1.5 %collective-permute-start.2 = (bf16[512,256]{1,0:T(8,128)(2,1)S(1)}, bf16[512,256]{1,0:T(8,128)(2,1)}, u32[]{:S(2)}, u32[]{:S(2)}) collective-permute-start(bf16[512,256]{1,0:T(8,128)(2,1)S(1)} %attend_rows.2.refs_0_.far), channel_id=1, source_target_pairs={{0,2},{2,0},{1,3},{3,1},{4,6},{6,4},{5,7},{7,5},{8,10},{10,8},{9,1... | collective-permute-start | bytes 786440 | tf_op jit(solution)/shard_map/far_seq/ppermute | solution.py:277
  53.4 2.9 %attend_rows.3.refs_0_.near = bf16[512,256]{1,0:T(8,128)(2,1)S(1)} custom-call(s32[8,4]{1,0:T(8,128)S(1)} %slice.13.assign, s32[4]{0:T(128)S(1)} %get-tuple-element.30.row_at, s32[4]{0:T(128)S(1)} %get-tuple-element.31.place_of, s32[4,256]{1,0:T(4,128)S(1)} %slice.11.segs, bf16[8,784,128]{2,1,0:T(8,128)(2,1)} %all-to-all-done.recv), custom_call_target="tpu_custom_call" | custom-call | flops 1000 | bytes 1000 | tf_op jit(solution)/shard_map/attend_rows/pallas_call | solution.py:186
  57.1 2.4 %collective-permute-done.2.refs_2_.far_seq = bf16[512,256]{1,0:T(8,128)(2,1)} collective-permute-done((bf16[512,256]{1,0:T(8,128)(2,1)S(1)}, bf16[512,256]{1,0:T(8,128)(2,1)}, u32[]{:S(2)}, u32[]{:S(2)}) %collective-permute-start.2) | collective-permute-done | bytes 262176 | tf_op jit(solution)/shard_map/far_seq/ppermute | solution.py:277
  59.5 1.9 %collective-permute-done.8.refs_3_ = bf16[512,256]{1,0:T(8,128)(2,1)} collective-permute-done((bf16[512,256]{1,0:T(8,128)(2,1)}, bf16[512,256]{1,0:T(8,128)(2,1)}, u32[]{:S(2)}, u32[]{:S(2)}) %collective-permute-start.8) | collective-permute-done | bytes 262176 | tf_op jit(solution)/shard_map/far_diag/ppermute | solution.py:277
  61.4 3.4 %project.3 = (bf16[256,1280]{1,0:T(8,128)(2,1)S(1)}, bf16[256,1280]{1,0:T(8,128)(2,1)S(1)}) custom-call(bf16[512,256]{1,0:T(8,128)(2,1)S(1)} %attend_rows.2.refs_0_.far, bf16[512,256]{1,0:T(8,128)(2,1)} %collective-permute-done.7.refs_1_, bf16[512,256]{1,0:T(8,128)(2,1)} %collective-permute-done.2.refs_2_.far_seq, ...), custom_call_target="tpu_custom_call" | custom-call | flops 1000 | bytes 1000 | tf_op jit(solution)/shard_map/project/pallas_call | solution.py:217
  64.9 1.2 broadcast_select_fusion.3
  66.1 4.2 %collective-permute-start.10 = (bf16[256,1280]{1,0:T(8,128)(2,1)}, bf16[256,1280]{1,0:T(8,128)(2,1)S(1)}, u32[]{:S(2)}, u32[]{:S(2)}) collective-permute-start(bf16[256,1280]{1,0:T(8,128)(2,1)} %collective-permute-done.1.refs_2_), channel_id=1, source_target_pairs={{4,8},{8,4},{5,9},{9,5},{6,10},{10,6},{7,11},{11,7},{20,24},{24,20... | collective-permute-start | bytes 1966088 | tf_op jit(solution)/shard_map/mid_1/ppermute | solution.py:330
  70.4 0.9 collective-permute-start.4
  71.3 6.9 %collective-permute-done.4.refs_2_.near_seq = bf16[512,256]{1,0:T(8,128)(2,1)S(1)} collective-permute-done((bf16[512,256]{1,0:T(8,128)(2,1)S(1)}, bf16[512,256]{1,0:T(8,128)(2,1)S(1)}, u32[]{:S(2)}, u32[]{:S(2)}) %collective-permute-start.4) | collective-permute-done | bytes 262176 | tf_op jit(solution)/shard_map/near_seq/ppermute | solution.py:277
  78.2 1.5 %collective-permute-done.5.refs_3_ = bf16[512,256]{1,0:T(8,128)(2,1)S(1)} collective-permute-done((bf16[512,256]{1,0:T(8,128)(2,1)S(1)}, bf16[512,256]{1,0:T(8,128)(2,1)S(1)}, u32[]{:S(2)}, u32[]{:S(2)}) %collective-permute-start.5) | collective-permute-done | bytes 262176 | tf_op jit(solution)/shard_map/near_diag/ppermute | solution.py:277
  79.8 2.3 %project.2 = (bf16[256,1280]{1,0:T(8,128)(2,1)S(1)}, bf16[256,1280]{1,0:T(8,128)(2,1)S(1)}) custom-call(bf16[512,256]{1,0:T(8,128)(2,1)S(1)} %copy-done.1, bf16[512,256]{1,0:T(8,128)(2,1)S(1)} %collective-permute-done.3.refs_1_, bf16[512,256]{1,0:T(8,128)(2,1)S(1)} %collective-permute-done.4.refs_2_.near_seq, ...), custom_call_target="tpu_custom_call" | custom-call | flops 1000 | bytes 1000 | tf_op jit(solution)/shard_map/project/pallas_call | solution.py:217
  82.1 0.8 collective-permute-done.9
  82.8 2.5 %collective-permute-done.10 = bf16[256,1280]{1,0:T(8,128)(2,1)S(1)} collective-permute-done((bf16[256,1280]{1,0:T(8,128)(2,1)}, bf16[256,1280]{1,0:T(8,128)(2,1)S(1)}, u32[]{:S(2)}, u32[]{:S(2)}) %collective-permute-start.10) | collective-permute-done | bytes 655392 | tf_op jit(solution)/shard_map/mid_1/ppermute | solution.py:330
  85.6 3.6 %collective-permute-start.12 = (bf16[256,1280]{1,0:T(8,128)(2,1)S(1)}, bf16[256,1280]{1,0:T(8,128)(2,1)S(1)}, u32[]{:S(2)}, u32[]{:S(2)}) collective-permute-start(bf16[256,1280]{1,0:T(8,128)(2,1)S(1)} %add_convert_fusion.3), channel_id=1, source_target_pairs={{4,8},{8,4},{5,9},{9,5},{6,10},{10,6},{7,11},{11,7},{20,24},{24,20... | collective-permute-start | bytes 1966088 | tf_op jit(solution)/shard_map/mid_2/ppermute | solution.py:330
  89.9 1.2 broadcast_select_fusion.refs_1_
  91.2 10.4 %collective-permute-done.11 = bf16[256,1280]{1,0:T(8,128)(2,1)S(1)} collective-permute-done((bf16[256,1280]{1,0:T(8,128)(2,1)S(1)}, bf16[256,1280]{1,0:T(8,128)(2,1)S(1)}, u32[]{:S(2)}, u32[]{:S(2)}) %collective-permute-start.11) | collective-permute-done | bytes 655392 | tf_op jit(solution)/shard_map/swap_2/ppermute | solution.py:330
  101.6 1.9 %collective-permute-done.12 = bf16[256,1280]{1,0:T(8,128)(2,1)S(1)} collective-permute-done((bf16[256,1280]{1,0:T(8,128)(2,1)S(1)}, bf16[256,1280]{1,0:T(8,128)(2,1)S(1)}, u32[]{:S(2)}, u32[]{:S(2)}) %collective-permute-start.12) | collective-permute-done | bytes 655392 | tf_op jit(solution)/shard_map/mid_2/ppermute | solution.py:330
  104.0 3.3 %collective-permute-start.18 = (bf16[256,1280]{1,0:T(8,128)(2,1)S(1)}, bf16[256,1280]{1,0:T(8,128)(2,1)S(1)}, u32[]{:S(2)}, u32[]{:S(2)}) collective-permute-start(bf16[256,1280]{1,0:T(8,128)(2,1)S(1)} %add_convert_fusion.1), channel_id=1, source_target_pairs={{4,8},{8,4},{5,9},{9,5},{6,10},{10,6},{7,11},{11,7},{20,24},{24,20... | collective-permute-start | bytes 1966088 | tf_op jit(solution)/shard_map/mid_3/ppermute | solution.py:330
  107.5 7.5 %weight_gradient.1 = f32[512,2560]{1,0:T(8,128)} custom-call(s32[2]{0:T(128)S(1)} %pad_add_fusion.place, bf16[512,256]{1,0:T(8,128)(2,1)S(1)} %attend_rows.2.refs_0_.far, bf16[512,256]{1,0:T(8,128)(2,1)S(1)} %copy-done.1, bf16[512,256]{1,0:T(8,128)(2,1)} %collective-permute-done.2.refs_2_.far_seq, ...), custom_call_target="tpu_custom_call" | custom-call | flops 1000 | bytes 1000 | tf_op jit(solution)/shard_map/weight_gradient/pallas_call | solution.py:259
  115.0 3.8 %collective-permute-done.13 = bf16[256,1280]{1,0:T(8,128)(2,1)S(1)} collective-permute-done((bf16[256,1280]{1,0:T(8,128)(2,1)S(1)}, bf16[256,1280]{1,0:T(8,128)(2,1)S(1)}, u32[]{:S(2)}, u32[]{:S(2)}) %collective-permute-start.13) | collective-permute-done | bytes 655392 | tf_op jit(solution)/shard_map/swap_3/ppermute | solution.py:330
  118.8 4.3 %collective-permute-done.18 = bf16[256,1280]{1,0:T(8,128)(2,1)S(1)} collective-permute-done((bf16[256,1280]{1,0:T(8,128)(2,1)S(1)}, bf16[256,1280]{1,0:T(8,128)(2,1)S(1)}, u32[]{:S(2)}, u32[]{:S(2)}) %collective-permute-start.18) | collective-permute-done | bytes 655392 | tf_op jit(solution)/shard_map/mid_3/ppermute | solution.py:330
  123.1 1.1 add_convert_fusion
  (46 shorter events, 4.2 us)
Async XLA Ops:
  3.8 6.5 %copy-start.2 = (bf16[4,1,128,2560]{3,2,1,0:T(8,128)(2,1)S(1)}, bf16[4,1,128,2560]{3,2,1,0:T(8,128)(2,1)}, u32[]{:S(2)}) copy-start(bf16[4,1,128,2560]{3,2,1,0:T(8,128)(2,1)} %param.12) | copy-start | bytes 7864324
  3.8 41.6 %all-to-all-start = ((bf16[8,784,128]{2,1,0:T(8,128)(2,1)}), bf16[8,784,128]{2,1,0:T(8,128)(2,1)}, u32[]{:S(2)}, u32[]{:S(2)}) async-start(bf16[8,784,128]{2,1,0:T(8,128)(2,1)} %pack.1), calls=%async_computation | async-start | bytes 3211264 | tf_op jit(solution)/shard_map/all_to_all | solution.py:297
  10.3 1.2 copy-start.3
  10.3 1.3 %copy-start.4 = (f32[1,4]{1,0:T(1,128)S(1)}, f32[1,4]{1,0:T(1,128)}, u32[]{:S(2)}) copy-start(f32[1,4]{1,0:T(1,128)} %param.11) | copy-start | bytes 52
  11.5 3.4 %collective-permute-start = (bf16[512,1280]{1,0:T(8,128)(2,1)}, bf16[512,1280]{1,0:T(8,128)(2,1)}, u32[]{:S(2)}, u32[]{:S(2)}) collective-permute-start(bf16[512,1280]{1,0:T(8,128)(2,1)} %constant_dynamic-slice_fusion.4), channel_id=1, source_target_pairs={{0,1},{1,0},{2,3},{3,2},{4,5},{5,4},{6,7},{7,6},{8,9},{9,8},{10,11... | collective-permute-start | bytes 3932168 | tf_op jit(solution)/shard_map/swap/ppermute | solution.py:277
  13.0 38.9 %collective-permute-start.1 = (bf16[256,1280]{1,0:T(8,128)(2,1)S(1)}, bf16[256,1280]{1,0:T(8,128)(2,1)}, u32[]{:S(2)}, u32[]{:S(2)}) collective-permute-start(bf16[256,1280]{1,0:T(8,128)(2,1)S(1)} %multiply_convert_fusion.refs_3_), channel_id=1, source_target_pairs={{0,4},{4,0},{8,12},{12,8},{1,5},{5,1},{9,13},{13,9},{2,6},{6,2},{1... | collective-permute-start | bytes 1966088 | tf_op jit(solution)/shard_map/swap_0/ppermute | solution.py:330
  46.2 18.7 %collective-permute-start.6 = (bf16[256,1280]{1,0:T(8,128)(2,1)S(1)}, bf16[256,1280]{1,0:T(8,128)(2,1)}, u32[]{:S(2)}, u32[]{:S(2)}) collective-permute-start(bf16[256,1280]{1,0:T(8,128)(2,1)S(1)} %multiply_convert_fusion.refs_3_), channel_id=1, source_target_pairs={{4,8},{8,4},{5,9},{9,5},{6,10},{10,6},{7,11},{11,7},{20,24},{24,20... | collective-permute-start | bytes 1966088 | tf_op jit(solution)/shard_map/mid_0/ppermute | solution.py:330
  51.9 7.6 %collective-permute-start.2 = (bf16[512,256]{1,0:T(8,128)(2,1)S(1)}, bf16[512,256]{1,0:T(8,128)(2,1)}, u32[]{:S(2)}, u32[]{:S(2)}) collective-permute-start(bf16[512,256]{1,0:T(8,128)(2,1)S(1)} %attend_rows.2.refs_0_.far), channel_id=1, source_target_pairs={{0,2},{2,0},{1,3},{3,1},{4,6},{6,4},{5,7},{7,5},{8,10},{10,8},{9,1... | collective-permute-start | bytes 786440 | tf_op jit(solution)/shard_map/far_seq/ppermute | solution.py:277
  56.3 0.7 copy-start
  57.1 2.5 %collective-permute-start.7 = (bf16[512,256]{1,0:T(8,128)(2,1)S(1)}, bf16[512,256]{1,0:T(8,128)(2,1)}, u32[]{:S(2)}, u32[]{:S(2)}) collective-permute-start(bf16[512,256]{1,0:T(8,128)(2,1)S(1)} %attend_rows.2.refs_0_.far), channel_id=1, source_target_pairs={{0,1},{1,0},{2,3},{3,2},{4,5},{5,4},{6,7},{7,6},{8,9},{9,8},{10,11... | collective-permute-start | bytes 786440 | tf_op jit(solution)/shard_map/far_head/ppermute | solution.py:277
  59.5 1.9 %collective-permute-start.8 = (bf16[512,256]{1,0:T(8,128)(2,1)}, bf16[512,256]{1,0:T(8,128)(2,1)}, u32[]{:S(2)}, u32[]{:S(2)}) collective-permute-start(bf16[512,256]{1,0:T(8,128)(2,1)} %collective-permute-done.2.refs_2_.far_seq), channel_id=1, source_target_pairs={{0,1},{1,0},{2,3},{3,2},{4,5},{5,4},{6,7},{7,6},{8,9},{9,8},{10,11... | collective-permute-start | bytes 786440 | tf_op jit(solution)/shard_map/far_diag/ppermute | solution.py:277
  64.8 5.6 %copy-start.1 = (bf16[512,256]{1,0:T(8,128)(2,1)S(1)}, bf16[512,256]{1,0:T(8,128)(2,1)}, u32[]{:S(2)}) copy-start(bf16[512,256]{1,0:T(8,128)(2,1)} %copy-done) | copy-start | bytes 786436
  66.1 16.8 %collective-permute-start.9 = (bf16[256,1280]{1,0:T(8,128)(2,1)S(1)}, bf16[256,1280]{1,0:T(8,128)(2,1)S(1)}, u32[]{:S(2)}, u32[]{:S(2)}) collective-permute-start(bf16[256,1280]{1,0:T(8,128)(2,1)S(1)} %broadcast_select_fusion.3), channel_id=1, source_target_pairs={{0,4},{4,0},{8,12},{12,8},{1,5},{5,1},{9,13},{13,9},{2,6},{6,2},{1... | collective-permute-start | bytes 1966088 | tf_op jit(solution)/shard_map/swap_1/ppermute | solution.py:330
  66.1 19.2 %collective-permute-start.10 = (bf16[256,1280]{1,0:T(8,128)(2,1)}, bf16[256,1280]{1,0:T(8,128)(2,1)S(1)}, u32[]{:S(2)}, u32[]{:S(2)}) collective-permute-start(bf16[256,1280]{1,0:T(8,128)(2,1)} %collective-permute-done.1.refs_2_), channel_id=1, source_target_pairs={{4,8},{8,4},{5,9},{9,5},{6,10},{10,6},{7,11},{11,7},{20,24},{24,20... | collective-permute-start | bytes 1966088 | tf_op jit(solution)/shard_map/mid_1/ppermute | solution.py:330
  70.4 7.9 %collective-permute-start.4 = (bf16[512,256]{1,0:T(8,128)(2,1)S(1)}, bf16[512,256]{1,0:T(8,128)(2,1)S(1)}, u32[]{:S(2)}, u32[]{:S(2)}) collective-permute-start(bf16[512,256]{1,0:T(8,128)(2,1)S(1)} %copy-done.1), channel_id=1, source_target_pairs={{0,2},{2,0},{1,3},{3,1},{4,6},{6,4},{5,7},{7,5},{8,10},{10,8},{9,1... | collective-permute-start | bytes 786440 | tf_op jit(solution)/shard_map/near_seq/ppermute | solution.py:277
  71.3 6.9 %collective-permute-start.3 = (bf16[512,256]{1,0:T(8,128)(2,1)S(1)}, bf16[512,256]{1,0:T(8,128)(2,1)S(1)}, u32[]{:S(2)}, u32[]{:S(2)}) collective-permute-start(bf16[512,256]{1,0:T(8,128)(2,1)S(1)} %copy-done.1), channel_id=1, source_target_pairs={{0,1},{1,0},{2,3},{3,2},{4,5},{5,4},{6,7},{7,6},{8,9},{9,8},{10,11... | collective-permute-start | bytes 786440 | tf_op jit(solution)/shard_map/near_head/ppermute | solution.py:277
  78.2 1.5 %collective-permute-start.5 = (bf16[512,256]{1,0:T(8,128)(2,1)S(1)}, bf16[512,256]{1,0:T(8,128)(2,1)S(1)}, u32[]{:S(2)}, u32[]{:S(2)}) collective-permute-start(bf16[512,256]{1,0:T(8,128)(2,1)S(1)} %collective-permute-done.4.refs_2_.near_seq), channel_id=1, source_target_pairs={{0,1},{1,0},{2,3},{3,2},{4,5},{5,4},{6,7},{7,6},{8,9},{9,8},{10,11... | collective-permute-start | bytes 786440 | tf_op jit(solution)/shard_map/near_diag/ppermute | solution.py:277
  85.6 16.0 %collective-permute-start.11 = (bf16[256,1280]{1,0:T(8,128)(2,1)S(1)}, bf16[256,1280]{1,0:T(8,128)(2,1)S(1)}, u32[]{:S(2)}, u32[]{:S(2)}) collective-permute-start(bf16[256,1280]{1,0:T(8,128)(2,1)S(1)} %broadcast_select_fusion.2), channel_id=1, source_target_pairs={{0,4},{4,0},{8,12},{12,8},{1,5},{5,1},{9,13},{13,9},{2,6},{6,2},{1... | collective-permute-start | bytes 1966088 | tf_op jit(solution)/shard_map/swap_2/ppermute | solution.py:330
  85.6 17.8 %collective-permute-start.12 = (bf16[256,1280]{1,0:T(8,128)(2,1)S(1)}, bf16[256,1280]{1,0:T(8,128)(2,1)S(1)}, u32[]{:S(2)}, u32[]{:S(2)}) collective-permute-start(bf16[256,1280]{1,0:T(8,128)(2,1)S(1)} %add_convert_fusion.3), channel_id=1, source_target_pairs={{4,8},{8,4},{5,9},{9,5},{6,10},{10,6},{7,11},{11,7},{20,24},{24,20... | collective-permute-start | bytes 1966088 | tf_op jit(solution)/shard_map/mid_2/ppermute | solution.py:330
  89.3 14.8 %collective-permute-start.17 = (bf16[256,1280]{1,0:T(8,128)(2,1)S(1)}, bf16[256,1280]{1,0:T(8,128)(2,1)S(1)}, u32[]{:S(2)}, u32[]{:S(2)}) collective-permute-start(bf16[256,1280]{1,0:T(8,128)(2,1)S(1)} %multiply_convert_fusion.refs_3_), channel_id=1, source_target_pairs={{0,1},{1,0},{2,3},{3,2},{4,5},{5,4},{6,7},{7,6},{8,9},{9,8},{10,11... | collective-permute-start | bytes 1966088 | tf_op jit(solution)/shard_map/piece_3/ppermute | solution.py:277
  89.4 18.1 %collective-permute-start.16 = (bf16[256,1280]{1,0:T(8,128)(2,1)}, bf16[256,1280]{1,0:T(8,128)(2,1)S(1)}, u32[]{:S(2)}, u32[]{:S(2)}) collective-permute-start(bf16[256,1280]{1,0:T(8,128)(2,1)} %collective-permute-done.1.refs_2_), channel_id=1, source_target_pairs={{0,1},{1,0},{2,3},{3,2},{4,5},{5,4},{6,7},{7,6},{8,9},{9,8},{10,11... | collective-permute-start | bytes 1966088 | tf_op jit(solution)/shard_map/piece_2/ppermute | solution.py:277
  91.0 16.4 %collective-permute-start.15 = (bf16[256,1280]{1,0:T(8,128)(2,1)S(1)}, bf16[256,1280]{1,0:T(8,128)(2,1)S(1)}, u32[]{:S(2)}, u32[]{:S(2)}) collective-permute-start(bf16[256,1280]{1,0:T(8,128)(2,1)S(1)} %broadcast_select_fusion.refs_1_), channel_id=1, source_target_pairs={{0,1},{1,0},{2,3},{3,2},{4,5},{5,4},{6,7},{7,6},{8,9},{9,8},{10,11... | collective-permute-start | bytes 1966088 | tf_op jit(solution)/shard_map/piece_1/ppermute | solution.py:277
  103.7 15.1 %collective-permute-start.13 = (bf16[256,1280]{1,0:T(8,128)(2,1)S(1)}, bf16[256,1280]{1,0:T(8,128)(2,1)S(1)}, u32[]{:S(2)}, u32[]{:S(2)}) collective-permute-start(bf16[256,1280]{1,0:T(8,128)(2,1)S(1)} %add_convert_fusion.2), channel_id=1, source_target_pairs={{0,4},{4,0},{8,12},{12,8},{1,5},{5,1},{9,13},{13,9},{2,6},{6,2},{1... | collective-permute-start | bytes 1966088 | tf_op jit(solution)/shard_map/swap_3/ppermute | solution.py:330
  103.8 3.7 %collective-permute-start.14 = (bf16[256,1280]{1,0:T(8,128)(2,1)S(1)}, bf16[256,1280]{1,0:T(8,128)(2,1)S(1)}, u32[]{:S(2)}, u32[]{:S(2)}) collective-permute-start(bf16[256,1280]{1,0:T(8,128)(2,1)S(1)} %broadcast_select_fusion.1.refs_0_), channel_id=1, source_target_pairs={{0,1},{1,0},{2,3},{3,2},{4,5},{5,4},{6,7},{7,6},{8,9},{9,8},{10,11... | collective-permute-start | bytes 1966088 | tf_op jit(solution)/shard_map/piece_0/ppermute | solution.py:277
  104.0 19.0 %collective-permute-start.18 = (bf16[256,1280]{1,0:T(8,128)(2,1)S(1)}, bf16[256,1280]{1,0:T(8,128)(2,1)S(1)}, u32[]{:S(2)}, u32[]{:S(2)}) collective-permute-start(bf16[256,1280]{1,0:T(8,128)(2,1)S(1)} %add_convert_fusion.1), channel_id=1, source_target_pairs={{4,8},{8,4},{5,9},{9,5},{6,10},{10,6},{7,11},{11,7},{20,24},{24,20... | collective-permute-start | bytes 1966088 | tf_op jit(solution)/shard_map/mid_3/ppermute | solution.py:330

commit v5 on v4

--- a/solution.py
+++ b/solution.py
@@ -199,7 +199,7 @@
 
 
 def project_kernel(tile, *refs):
-    parts, weights, outs = refs[:-3], refs[-3], refs[-2:]
+    parts, weights, outs = refs[:4], refs[4], refs[5:]
     rows = jnp.concatenate([x[...] for x in parts], 1)
 
     @pl.loop(0, weights.shape[1] // tile)
@@ -210,15 +210,15 @@
             out[:, columns] = total[i * out.shape[0] : (i + 1) * out.shape[0]]
 
 
-def project(parts, weights):
-    tokens = parts[0].shape[0]
+def project(parts, weights, row_len):
+    count = parts[0].shape[0] // row_len
     half = weights.shape[1]
     vmem = pl.BlockSpec(memory_space=pltpu.VMEM)
     return pl.pallas_call(
         functools.partial(project_kernel, math.gcd(half, 256)),
-        out_shape=[jax.ShapeDtypeStruct((tokens // 2, half), jnp.bfloat16)] * 2,
+        out_shape=[jax.ShapeDtypeStruct((row_len, half), jnp.bfloat16)] * count,
         in_specs=[vmem] * (len(parts) + 1),
-        out_specs=[vmem] * 2,
+        out_specs=[vmem] * count,
         compiler_params=pltpu.CompilerParams(vmem_limit_bytes=14 << 20),
         cost_estimate=SHORT,
         name="project",
@@ -234,8 +234,10 @@
     def _():
         for s, parts in enumerate(((far, near), (far_seq, near_seq))):
             first = pl.multiple_of(width * (place[0] if s == 0 else 1 - place[0]), width)
-            for i, part in enumerate(parts):
-                turned[pl.ds(first, width), 2 * i * row_len : 2 * (i + 1) * row_len] = part[...].T
+            done = 0
+            for part in parts:
+                turned[pl.ds(first, width), done : done + part.shape[0]] = part[...].T
+                done += part.shape[0]
 
     for side, group in enumerate((own, other)):
 
@@ -250,7 +252,7 @@
     row_len, half = pieces[0].shape
     tile = math.gcd(half, 640)
     tiles = half // tile
-    whole = pl.BlockSpec(att[0].shape, lambda side, t, place: (0, 0))
+    whole = [pl.BlockSpec(x.shape, lambda side, t, place: (0, 0)) for x in (*att, *att_seq)]
     own = pl.BlockSpec((row_len, tile), lambda side, t, place: (0, jnp.where(side == 0, t, tiles - 1)))
     other = pl.BlockSpec((row_len, tile), lambda side, t, place: (0, jnp.where(side == 0, 0, t)))
     out = pl.BlockSpec(
@@ -262,7 +264,7 @@
         grid_spec=pltpu.PrefetchScalarGridSpec(
             num_scalar_prefetch=1,
             grid=(2, tiles),
-            in_specs=[whole] * 4 + [own] * 4 + [other] * 4,
+            in_specs=whole + [own] * 4 + [other] * 4,
             out_specs=out,
             scratch_shapes=[pltpu.VMEM((2 * width, 4 * row_len), jnp.bfloat16)],
         ),
@@ -331,18 +333,18 @@
 
     inner = (me == 1) | (me == 2)
 
-    from_2, mid_1 = send(early, across, "swap_0"), send(scaled, middle, "mid_0")
-
-    far = attend((0, 1), recv)
-    far, from_2 = lax.optimization_barrier((far, from_2))
+    from_2, mid_1 = send(early, across, "swap_0"), send(early, middle, "mid_0")
+
+    far = attend((0,), recv)
     far_seq, far_head = swap(far, "seq", "far_seq"), swap(far, "head", "far_head")
-    near = attend((2, 3), recv)
+    near = attend((1, 2, 3), recv)
+    near, from_2 = lax.optimization_barrier((near, from_2))
     far_seq, near = lax.optimization_barrier((far_seq, near))
     far_diag = swap(far_seq, "head", "far_diag")
     near_seq, near_head = swap(near, "seq", "near_seq"), swap(near, "head", "near_head")
-    first, second = project((far, far_head, far_seq, far_diag), weights)
+    (first,) = project((far, far_head, far_seq, far_diag), weights, row_len)
     near_diag = swap(near_seq, "head", "near_diag")
-    third, own = project((near, near_head, near_seq, near_diag), weights)
+    second, third, own = project((near, near_head, near_seq, near_diag), weights, row_len)
 
     to_swap, from_2 = lax.optimization_barrier((jnp.where(inner, mid_1, first), from_2))
     swapped_1 = send(to_swap, across, "swap_1")

time: 125 us -> 120 us (0.960)
  waiting for transfers between devices: 65.8 us -> 62.4 us
  Pallas kernels: 22.2 us -> 20.9 us
    ppermute x8, waiting for transfers between devices: 23.8 us -> 33.2 us  [send(): return lax.ppermute(x, 'dp', perm)]
    ppermute x11, waiting for transfers between devices: 13.2 us -> 4.12 us  [swap(): return lax.ppermute(x, axis, [(0, 1), (1, 0)])]
    all_to_all x1, waiting for transfers between devices: 28.9 us -> 25.1 us  [body_heads(): lax.all_to_all(sent, ('dp', 'seq'), split_axis=0, concat_axis=0, tiled=True)]
  transfers between devices with their start and end apart: 20 -> 20, of which waited for: 13 -> 13; matrix products, arithmetic and copies ran while one was open for 7% -> 9% of each run, Pallas kernels for 15% -> 15%
where the time goes in v5:
time: 120 us; the launch traced here: 119 us
  waiting for transfers between devices  62.4 us (52%)
  starting transfers between devices  23.2 us (19%)
  Pallas kernels  20.9 us (17%)
  other arithmetic  7.42 us (6%)
  local copies, waits for them, and re-layouts  4.02 us (3%)
    ppermute x8, waiting for transfers between devices, send(): return lax.ppermute(x, 'dp', perm)  33.2 us
    all_to_all x1, waiting for transfers between devices, body_heads(): lax.all_to_all(sent, ('dp', 'seq'), split_axis=0, concat_axis=0, tiled=True)  25.1 us
    ppermute x8, starting transfers between devices, send(): return lax.ppermute(x, 'dp', perm)  14 us
    pallas_call x1, Pallas kernels, weight_gradient(): pl.pallas_call(gradient_kernel, out_shape=jax.ShapeDtypeStruct((2 * width...  7.39 us
    all_to_all x1, starting transfers between devices, body_heads(): lax.all_to_all(sent, ('dp', 'seq'), split_axis=0, concat_axis=0, tiled=True)  6.51 us
    pallas_call x2, Pallas kernels, attend_rows(): pl.pallas_call(functools.partial(attention_kernel, places, labels, nblk,...  5.8 us
    pallas_call x2, Pallas kernels, project(): pl.pallas_call(functools.partial(project_kernel, math.gcd(half, 256)), ou...  4.53 us
    ppermute x11, waiting for transfers between devices, swap(): return lax.ppermute(x, axis, [(0, 1), (1, 0)])  4.12 us
  transfers between devices with their start and end apart: 20, of which 13 were waited for; matrix products, arithmetic and copies ran while one was open for 9% of the time, Pallas kernels for 15%

profile of v5, /device:TPU:8, one launch (start us, length us, event | category | flops | bytes accessed | tf_op | source)
XLA Modules:
  0.0 118.9 jit_solution(12456446216290872958)
XLA Ops:
  0.6 3.2 %pack.1 = bf16[8,784,128]{2,1,0:T(8,128)(2,1)} custom-call(s32[1,4]{1,0:T(1,128)} %bitcast.27, s32[1,256]{1,0:T(1,128)} %segs.1, bf16[3,128,16,128]{3,2,1,0:T(8,128)(2,1)} %bitcast.22), custom_call_target="tpu_custom_call" | custom-call | flops 1000 | bytes 1000 | tf_op jit(solution)/shard_map/pack/pallas_call | solution.py:116
  3.8 6.5 %all-to-all-start = ((bf16[8,784,128]{2,1,0:T(8,128)(2,1)}), bf16[8,784,128]{2,1,0:T(8,128)(2,1)}, u32[]{:S(2)}, u32[]{:S(2)}) async-start(bf16[8,784,128]{2,1,0:T(8,128)(2,1)} %pack.1), calls=%async_computation | async-start | bytes 3211264 | tf_op jit(solution)/shard_map/all_to_all | solution.py:299
  10.3 1.2 constant_dynamic-slice_fusion.4
  11.7 2.1 %multiply_convert_fusion.refs_3_ = bf16[256,1280]{1,0:T(8,128)(2,1)} fusion(f32[256]{0:T(256)S(1)} %div.7, bf16[256,2560]{1,0:T(8,128)(2,1)} %param.13, s32[]{:T(128)S(6)} %select_n.45), kind=kLoop, calls=%fused_computation.5 | loop fusion | flops 983040 | bytes 1311748 | tf_op jit(solution)/shard_map/convert_element_type | solution.py:305
  13.8 3.4 %collective-permute-start.6 = (bf16[256,1280]{1,0:T(8,128)(2,1)}, bf16[256,1280]{1,0:T(8,128)(2,1)}, u32[]{:S(2)}, u32[]{:S(2)}) collective-permute-start(bf16[256,1280]{1,0:T(8,128)(2,1)} %multiply_convert_fusion.refs_3_), channel_id=1, source_target_pairs={{4,8},{8,4},{5,9},{9,5},{6,10},{10,6},{7,11},{11,7},{20,24},{24,20... | collective-permute-start | bytes 1966088 | tf_op jit(solution)/shard_map/mid_0/ppermute | solution.py:332
  17.3 0.7 fusion
  18.0 0.7 fusion.2
  18.7 1.4 %constant_dynamic-slice_fusion.3 = (bf16[256,1280]{1,0:T(8,128)(2,1)S(1)}, bf16[256,1280]{1,0:T(8,128)(2,1)S(1)}) fusion(bf16[512,1280]{1,0:T(8,128)(2,1)} %collective-permute-done, s32[]{:T(128)S(6)} %select_n.46, s32[]{:T(128)S(6)} %select_n.50), kind=kLoop, calls=%fused_computation.19 | loop fusion | bytes 2621448 | tf_op jit(solution)/shard_map/dynamic_slice | solution.py:312
  20.4 25.1 %all-to-all-done.recv = bf16[8,784,128]{2,1,0:T(8,128)(2,1)} async-done(((bf16[8,784,128]{2,1,0:T(8,128)(2,1)}), bf16[8,784,128]{2,1,0:T(8,128)(2,1)}, u32[]{:S(2)}, u32[]{:S(2)}) %all-to-all-start) | async-done | bytes 1605664 | tf_op jit(solution)/shard_map/all_to_all | solution.py:299
  45.5 0.8 convert_bitcast_fusion
  46.3 2.6 %attend_rows.2.refs_0_.far = bf16[256,256]{1,0:T(8,128)(2,1)S(1)} custom-call(s32[8,4]{1,0:T(8,128)S(1)} %slice.13.assign, s32[4]{0:T(128)S(1)} %get-tuple-element.29.row_at, s32[4]{0:T(128)S(1)} %get-tuple-element.30.place_of, s32[4,256]{1,0:T(4,128)S(1)} %slice.11.segs, bf16[8,784,128]{2,1,0:T(8,128)(2,1)} %all-to-all-done.recv), custom_call_target="tpu_custom_call" | custom-call | flops 1000 | bytes 1000 | tf_op jit(solution)/shard_map/attend_rows/pallas_call | solution.py:186
  49.0 0.9 collective-permute-start.1
  49.9 3.2 %attend_rows.3.refs_0_.near = bf16[768,256]{1,0:T(8,128)(2,1)S(1)} custom-call(s32[8,4]{1,0:T(8,128)S(1)} %slice.13.assign, s32[4]{0:T(128)S(1)} %get-tuple-element.29.row_at, s32[4]{0:T(128)S(1)} %get-tuple-element.30.place_of, s32[4,256]{1,0:T(4,128)S(1)} %slice.11.segs, bf16[8,784,128]{2,1,0:T(8,128)(2,1)} %all-to-all-done.recv), custom_call_target="tpu_custom_call" | custom-call | flops 1000 | bytes 1000 | tf_op jit(solution)/shard_map/attend_rows/pallas_call | solution.py:186
  53.1 1.2 %collective-permute-done.1.refs_2_.far_seq = bf16[256,256]{1,0:T(8,128)(2,1)S(1)} collective-permute-done((bf16[256,256]{1,0:T(8,128)(2,1)S(1)}, bf16[256,256]{1,0:T(8,128)(2,1)S(1)}, u32[]{:S(2)}, u32[]{:S(2)}) %collective-permute-start.1) | collective-permute-done | bytes 131104 | tf_op jit(solution)/shard_map/far_seq/ppermute | solution.py:279
  54.3 0.8 collective-permute-start.4
  55.7 1.6 %project.3 = bf16[256,1280]{1,0:T(8,128)(2,1)S(1)} custom-call(bf16[256,256]{1,0:T(8,128)(2,1)S(1)} %attend_rows.2.refs_0_.far, bf16[256,256]{1,0:T(8,128)(2,1)S(1)} %collective-permute-done.7.refs_1_, bf16[256,256]{1,0:T(8,128)(2,1)S(1)} %collective-permute-done.1.refs_2_.far_seq, bf16[256,256]{1,0:T(8,128)(2,1)S(1)} %collective-permute-done.8.refs_3_, ...), custom_call_target="tpu_custom_call" | custom-call | flops 1000 | bytes 1000 | tf_op jit(solution)/shard_map/project/pallas_call | solution.py:217
  57.3 3.5 %collective-permute-done.6 = bf16[256,1280]{1,0:T(8,128)(2,1)} collective-permute-done((bf16[256,1280]{1,0:T(8,128)(2,1)}, bf16[256,1280]{1,0:T(8,128)(2,1)}, u32[]{:S(2)}, u32[]{:S(2)}) %collective-permute-start.6) | collective-permute-done | bytes 655392 | tf_op jit(solution)/shard_map/mid_0/ppermute | solution.py:332
  60.8 1.2 broadcast_select_fusion.3
  62.0 3.1 %collective-permute-start.10 = (bf16[256,1280]{1,0:T(8,128)(2,1)}, bf16[256,1280]{1,0:T(8,128)(2,1)S(1)}, u32[]{:S(2)}, u32[]{:S(2)}) collective-permute-start(bf16[256,1280]{1,0:T(8,128)(2,1)} %collective-permute-done.2.refs_2_), channel_id=1, source_target_pairs={{4,8},{8,4},{5,9},{9,5},{6,10},{10,6},{7,11},{11,7},{20,24},{24,20... | collective-permute-start | bytes 1966088 | tf_op jit(solution)/shard_map/mid_1/ppermute | solution.py:332
  65.9 1.0 collective-permute-done.3.refs_1_
  67.6 3.0 %project.2 = (bf16[256,1280]{1,0:T(8,128)(2,1)S(1)}, bf16[256,1280]{1,0:T(8,128)(2,1)S(1)}, bf16[256,1280]{1,0:T(8,128)(2,1)S(1)}) custom-call(bf16[768,256]{1,0:T(8,128)(2,1)S(1)} %attend_rows.3.refs_0_.near, bf16[768,256]{1,0:T(8,128)(2,1)S(1)} %collective-permute-done.3.refs_1_, bf16[768,256]{1,0:T(8,128)(2,1)S(1)} %collective-permute-done.4.refs_2_.near_seq, ...), custom_call_target="tpu_custom_call" | custom-call | flops 1000 | bytes 1000 | tf_op jit(solution)/shard_map/project/pallas_call | solution.py:217
  70.6 6.8 %collective-permute-done.9 = bf16[256,1280]{1,0:T(8,128)(2,1)S(1)} collective-permute-done((bf16[256,1280]{1,0:T(8,128)(2,1)S(1)}, bf16[256,1280]{1,0:T(8,128)(2,1)S(1)}, u32[]{:S(2)}, u32[]{:S(2)}) %collective-permute-start.9) | collective-permute-done | bytes 655392 | tf_op jit(solution)/shard_map/swap_1/ppermute | solution.py:332
  77.3 2.9 %collective-permute-done.10 = bf16[256,1280]{1,0:T(8,128)(2,1)S(1)} collective-permute-done((bf16[256,1280]{1,0:T(8,128)(2,1)}, bf16[256,1280]{1,0:T(8,128)(2,1)S(1)}, u32[]{:S(2)}, u32[]{:S(2)}) %collective-permute-start.10) | collective-permute-done | bytes 655392 | tf_op jit(solution)/shard_map/mid_1/ppermute | solution.py:332
  80.5 3.6 %collective-permute-start.12 = (bf16[256,1280]{1,0:T(8,128)(2,1)S(1)}, bf16[256,1280]{1,0:T(8,128)(2,1)S(1)}, u32[]{:S(2)}, u32[]{:S(2)}) collective-permute-start(bf16[256,1280]{1,0:T(8,128)(2,1)S(1)} %add_convert_fusion.3), channel_id=1, source_target_pairs={{4,8},{8,4},{5,9},{9,5},{6,10},{10,6},{7,11},{11,7},{20,24},{24,20... | collective-permute-start | bytes 1966088 | tf_op jit(solution)/shard_map/mid_2/ppermute | solution.py:332
  84.8 1.2 broadcast_select_fusion.refs_1_
  86.1 9.6 %collective-permute-done.11 = bf16[256,1280]{1,0:T(8,128)(2,1)S(1)} collective-permute-done((bf16[256,1280]{1,0:T(8,128)(2,1)S(1)}, bf16[256,1280]{1,0:T(8,128)(2,1)S(1)}, u32[]{:S(2)}, u32[]{:S(2)}) %collective-permute-start.11) | collective-permute-done | bytes 655392 | tf_op jit(solution)/shard_map/swap_2/ppermute | solution.py:332
  95.7 2.5 %collective-permute-done.12 = bf16[256,1280]{1,0:T(8,128)(2,1)S(1)} collective-permute-done((bf16[256,1280]{1,0:T(8,128)(2,1)S(1)}, bf16[256,1280]{1,0:T(8,128)(2,1)S(1)}, u32[]{:S(2)}, u32[]{:S(2)}) %collective-permute-start.12) | collective-permute-done | bytes 655392 | tf_op jit(solution)/shard_map/mid_2/ppermute | solution.py:332
  98.8 3.6 %collective-permute-start.18 = (bf16[256,1280]{1,0:T(8,128)(2,1)S(1)}, bf16[256,1280]{1,0:T(8,128)(2,1)S(1)}, u32[]{:S(2)}, u32[]{:S(2)}) collective-permute-start(bf16[256,1280]{1,0:T(8,128)(2,1)S(1)} %add_convert_fusion.1), channel_id=1, source_target_pairs={{4,8},{8,4},{5,9},{9,5},{6,10},{10,6},{7,11},{11,7},{20,24},{24,20... | collective-permute-start | bytes 1966088 | tf_op jit(solution)/shard_map/mid_3/ppermute | solution.py:332
  102.5 7.4 %weight_gradient.1 = f32[512,2560]{1,0:T(8,128)} custom-call(s32[2]{0:T(128)S(1)} %pad_add_fusion.place, bf16[256,256]{1,0:T(8,128)(2,1)S(1)} %attend_rows.2.refs_0_.far, bf16[768,256]{1,0:T(8,128)(2,1)S(1)} %attend_rows.3.refs_0_.near, bf16[256,256]{1,0:T(8,128)(2,1)S(1)} %collective-permute-done.1.refs_2_.far_seq, ...), custom_call_target="tpu_custom_call" | custom-call | flops 1000 | bytes 1000 | tf_op jit(solution)/shard_map/weight_gradient/pallas_call | solution.py:261
  109.9 3.5 %collective-permute-done.13 = bf16[256,1280]{1,0:T(8,128)(2,1)S(1)} collective-permute-done((bf16[256,1280]{1,0:T(8,128)(2,1)S(1)}, bf16[256,1280]{1,0:T(8,128)(2,1)S(1)}, u32[]{:S(2)}, u32[]{:S(2)}) %collective-permute-start.13) | collective-permute-done | bytes 655392 | tf_op jit(solution)/shard_map/swap_3/ppermute | solution.py:332
  113.4 4.4 %collective-permute-done.18 = bf16[256,1280]{1,0:T(8,128)(2,1)S(1)} collective-permute-done((bf16[256,1280]{1,0:T(8,128)(2,1)S(1)}, bf16[256,1280]{1,0:T(8,128)(2,1)S(1)}, u32[]{:S(2)}, u32[]{:S(2)}) %collective-permute-start.18) | collective-permute-done | bytes 655392 | tf_op jit(solution)/shard_map/mid_3/ppermute | solution.py:332
  117.8 1.1 add_convert_fusion
  (42 shorter events, 4.3 us)
Async XLA Ops:
  3.8 6.5 %copy-start = (bf16[4,1,128,2560]{3,2,1,0:T(8,128)(2,1)S(1)}, bf16[4,1,128,2560]{3,2,1,0:T(8,128)(2,1)}, u32[]{:S(2)}) copy-start(bf16[4,1,128,2560]{3,2,1,0:T(8,128)(2,1)} %param.12) | copy-start | bytes 7864324
  3.8 41.7 %all-to-all-start = ((bf16[8,784,128]{2,1,0:T(8,128)(2,1)}), bf16[8,784,128]{2,1,0:T(8,128)(2,1)}, u32[]{:S(2)}, u32[]{:S(2)}) async-start(bf16[8,784,128]{2,1,0:T(8,128)(2,1)} %pack.1), calls=%async_computation | async-start | bytes 3211264 | tf_op jit(solution)/shard_map/all_to_all | solution.py:299
  10.3 1.2 copy-start.1
  10.3 1.3 %copy-start.2 = (f32[1,4]{1,0:T(1,128)S(1)}, f32[1,4]{1,0:T(1,128)}, u32[]{:S(2)}) copy-start(f32[1,4]{1,0:T(1,128)} %param.11) | copy-start | bytes 52
  11.5 7.2 %collective-permute-start = (bf16[512,1280]{1,0:T(8,128)(2,1)}, bf16[512,1280]{1,0:T(8,128)(2,1)}, u32[]{:S(2)}, u32[]{:S(2)}) collective-permute-start(bf16[512,1280]{1,0:T(8,128)(2,1)} %constant_dynamic-slice_fusion.4), channel_id=1, source_target_pairs={{0,1},{1,0},{2,3},{3,2},{4,5},{5,4},{6,7},{7,6},{8,9},{9,8},{10,11... | collective-permute-start | bytes 3932168 | tf_op jit(solution)/shard_map/swap/ppermute | solution.py:279
  13.8 46.9 %collective-permute-start.6 = (bf16[256,1280]{1,0:T(8,128)(2,1)}, bf16[256,1280]{1,0:T(8,128)(2,1)}, u32[]{:S(2)}, u32[]{:S(2)}) collective-permute-start(bf16[256,1280]{1,0:T(8,128)(2,1)} %multiply_convert_fusion.refs_3_), channel_id=1, source_target_pairs={{4,8},{8,4},{5,9},{9,5},{6,10},{10,6},{7,11},{11,7},{20,24},{24,20... | collective-permute-start | bytes 1966088 | tf_op jit(solution)/shard_map/mid_0/ppermute | solution.py:332
  17.2 35.9 %collective-permute-start.2 = (bf16[256,1280]{1,0:T(8,128)(2,1)}, bf16[256,1280]{1,0:T(8,128)(2,1)}, u32[]{:S(2)}, u32[]{:S(2)}) collective-permute-start(bf16[256,1280]{1,0:T(8,128)(2,1)} %multiply_convert_fusion.refs_3_), channel_id=1, source_target_pairs={{0,4},{4,0},{8,12},{12,8},{1,5},{5,1},{9,13},{13,9},{2,6},{6,2},{1... | collective-permute-start | bytes 1966088 | tf_op jit(solution)/shard_map/swap_0/ppermute | solution.py:332
  49.0 5.4 %collective-permute-start.1 = (bf16[256,256]{1,0:T(8,128)(2,1)S(1)}, bf16[256,256]{1,0:T(8,128)(2,1)S(1)}, u32[]{:S(2)}, u32[]{:S(2)}) collective-permute-start(bf16[256,256]{1,0:T(8,128)(2,1)S(1)} %attend_rows.2.refs_0_.far), channel_id=1, source_target_pairs={{0,2},{2,0},{1,3},{3,1},{4,6},{6,4},{5,7},{7,5},{8,10},{10,8},{9,1... | collective-permute-start | bytes 393224 | tf_op jit(solution)/shard_map/far_seq/ppermute | solution.py:279
  53.1 2.1 %collective-permute-start.7 = (bf16[256,256]{1,0:T(8,128)(2,1)S(1)}, bf16[256,256]{1,0:T(8,128)(2,1)S(1)}, u32[]{:S(2)}, u32[]{:S(2)}) collective-permute-start(bf16[256,256]{1,0:T(8,128)(2,1)S(1)} %attend_rows.2.refs_0_.far), channel_id=1, source_target_pairs={{0,1},{1,0},{2,3},{3,2},{4,5},{5,4},{6,7},{7,6},{8,9},{9,8},{10,11... | collective-permute-start | bytes 393224 | tf_op jit(solution)/shard_map/far_head/ppermute | solution.py:279
  54.3 1.3 %collective-permute-start.8 = (bf16[256,256]{1,0:T(8,128)(2,1)S(1)}, bf16[256,256]{1,0:T(8,128)(2,1)S(1)}, u32[]{:S(2)}, u32[]{:S(2)}) collective-permute-start(bf16[256,256]{1,0:T(8,128)(2,1)S(1)} %collective-permute-done.1.refs_2_.far_seq), channel_id=1, source_target_pairs={{0,1},{1,0},{2,3},{3,2},{4,5},{5,4},{6,7},{7,6},{8,9},{9,8},{10,11... | collective-permute-start | bytes 393224 | tf_op jit(solution)/shard_map/far_diag/ppermute | solution.py:279
  54.3 11.5 %collective-permute-start.4 = (bf16[768,256]{1,0:T(8,128)(2,1)S(1)}, bf16[768,256]{1,0:T(8,128)(2,1)S(1)}, u32[]{:S(2)}, u32[]{:S(2)}) collective-permute-start(bf16[768,256]{1,0:T(8,128)(2,1)S(1)} %attend_rows.3.refs_0_.near), channel_id=1, source_target_pairs={{0,2},{2,0},{1,3},{3,1},{4,6},{6,4},{5,7},{7,5},{8,10},{10,8},{9,1... | collective-permute-start | bytes 1179656 | tf_op jit(solution)/shard_map/near_seq/ppermute | solution.py:279
  61.9 15.4 %collective-permute-start.9 = (bf16[256,1280]{1,0:T(8,128)(2,1)S(1)}, bf16[256,1280]{1,0:T(8,128)(2,1)S(1)}, u32[]{:S(2)}, u32[]{:S(2)}) collective-permute-start(bf16[256,1280]{1,0:T(8,128)(2,1)S(1)} %broadcast_select_fusion.3), channel_id=1, source_target_pairs={{0,4},{4,0},{8,12},{12,8},{1,5},{5,1},{9,13},{13,9},{2,6},{6,2},{1... | collective-permute-start | bytes 1966088 | tf_op jit(solution)/shard_map/swap_1/ppermute | solution.py:332
  62.0 18.2 %collective-permute-start.10 = (bf16[256,1280]{1,0:T(8,128)(2,1)}, bf16[256,1280]{1,0:T(8,128)(2,1)S(1)}, u32[]{:S(2)}, u32[]{:S(2)}) collective-permute-start(bf16[256,1280]{1,0:T(8,128)(2,1)} %collective-permute-done.2.refs_2_), channel_id=1, source_target_pairs={{4,8},{8,4},{5,9},{9,5},{6,10},{10,6},{7,11},{11,7},{20,24},{24,20... | collective-permute-start | bytes 1966088 | tf_op jit(solution)/shard_map/mid_1/ppermute | solution.py:332
  65.1 1.8 %collective-permute-start.3 = (bf16[768,256]{1,0:T(8,128)(2,1)S(1)}, bf16[768,256]{1,0:T(8,128)(2,1)S(1)}, u32[]{:S(2)}, u32[]{:S(2)}) collective-permute-start(bf16[768,256]{1,0:T(8,128)(2,1)S(1)} %attend_rows.3.refs_0_.near), channel_id=1, source_target_pairs={{0,1},{1,0},{2,3},{3,2},{4,5},{5,4},{6,7},{7,6},{8,9},{9,8},{10,11... | collective-permute-start | bytes 1179656 | tf_op jit(solution)/shard_map/near_head/ppermute | solution.py:279
  65.9 1.7 %collective-permute-start.5 = (bf16[768,256]{1,0:T(8,128)(2,1)S(1)}, bf16[768,256]{1,0:T(8,128)(2,1)S(1)}, u32[]{:S(2)}, u32[]{:S(2)}) collective-permute-start(bf16[768,256]{1,0:T(8,128)(2,1)S(1)} %collective-permute-done.4.refs_2_.near_seq), channel_id=1, source_target_pairs={{0,1},{1,0},{2,3},{3,2},{4,5},{5,4},{6,7},{7,6},{8,9},{9,8},{10,11... | collective-permute-start | bytes 1179656 | tf_op jit(solution)/shard_map/near_diag/ppermute | solution.py:279
  80.4 15.2 %collective-permute-start.11 = (bf16[256,1280]{1,0:T(8,128)(2,1)S(1)}, bf16[256,1280]{1,0:T(8,128)(2,1)S(1)}, u32[]{:S(2)}, u32[]{:S(2)}) collective-permute-start(bf16[256,1280]{1,0:T(8,128)(2,1)S(1)} %broadcast_select_fusion.2), channel_id=1, source_target_pairs={{0,4},{4,0},{8,12},{12,8},{1,5},{5,1},{9,13},{13,9},{2,6},{6,2},{1... | collective-permute-start | bytes 1966088 | tf_op jit(solution)/shard_map/swap_2/ppermute | solution.py:332
  80.5 17.7 %collective-permute-start.12 = (bf16[256,1280]{1,0:T(8,128)(2,1)S(1)}, bf16[256,1280]{1,0:T(8,128)(2,1)S(1)}, u32[]{:S(2)}, u32[]{:S(2)}) collective-permute-start(bf16[256,1280]{1,0:T(8,128)(2,1)S(1)} %add_convert_fusion.3), channel_id=1, source_target_pairs={{4,8},{8,4},{5,9},{9,5},{6,10},{10,6},{7,11},{11,7},{20,24},{24,20... | collective-permute-start | bytes 1966088 | tf_op jit(solution)/shard_map/mid_2/ppermute | solution.py:332
  84.2 14.6 %collective-permute-start.17 = (bf16[256,1280]{1,0:T(8,128)(2,1)}, bf16[256,1280]{1,0:T(8,128)(2,1)S(1)}, u32[]{:S(2)}, u32[]{:S(2)}) collective-permute-start(bf16[256,1280]{1,0:T(8,128)(2,1)} %multiply_convert_fusion.refs_3_), channel_id=1, source_target_pairs={{0,1},{1,0},{2,3},{3,2},{4,5},{5,4},{6,7},{7,6},{8,9},{9,8},{10,11... | collective-permute-start | bytes 1966088 | tf_op jit(solution)/shard_map/piece_3/ppermute | solution.py:279
  84.3 18.3 %collective-permute-start.16 = (bf16[256,1280]{1,0:T(8,128)(2,1)}, bf16[256,1280]{1,0:T(8,128)(2,1)S(1)}, u32[]{:S(2)}, u32[]{:S(2)}) collective-permute-start(bf16[256,1280]{1,0:T(8,128)(2,1)} %collective-permute-done.2.refs_2_), channel_id=1, source_target_pairs={{0,1},{1,0},{2,3},{3,2},{4,5},{5,4},{6,7},{7,6},{8,9},{9,8},{10,11... | collective-permute-start | bytes 1966088 | tf_op jit(solution)/shard_map/piece_2/ppermute | solution.py:279
  85.9 16.6 %collective-permute-start.15 = (bf16[256,1280]{1,0:T(8,128)(2,1)S(1)}, bf16[256,1280]{1,0:T(8,128)(2,1)S(1)}, u32[]{:S(2)}, u32[]{:S(2)}) collective-permute-start(bf16[256,1280]{1,0:T(8,128)(2,1)S(1)} %broadcast_select_fusion.refs_1_), channel_id=1, source_target_pairs={{0,1},{1,0},{2,3},{3,2},{4,5},{5,4},{6,7},{7,6},{8,9},{9,8},{10,11... | collective-permute-start | bytes 1966088 | tf_op jit(solution)/shard_map/piece_1/ppermute | solution.py:279
  98.5 15.0 %collective-permute-start.13 = (bf16[256,1280]{1,0:T(8,128)(2,1)S(1)}, bf16[256,1280]{1,0:T(8,128)(2,1)S(1)}, u32[]{:S(2)}, u32[]{:S(2)}) collective-permute-start(bf16[256,1280]{1,0:T(8,128)(2,1)S(1)} %add_convert_fusion.2), channel_id=1, source_target_pairs={{0,4},{4,0},{8,12},{12,8},{1,5},{5,1},{9,13},{13,9},{2,6},{6,2},{1... | collective-permute-start | bytes 1966088 | tf_op jit(solution)/shard_map/swap_3/ppermute | solution.py:332
  98.5 4.0 %collective-permute-start.14 = (bf16[256,1280]{1,0:T(8,128)(2,1)S(1)}, bf16[256,1280]{1,0:T(8,128)(2,1)S(1)}, u32[]{:S(2)}, u32[]{:S(2)}) collective-permute-start(bf16[256,1280]{1,0:T(8,128)(2,1)S(1)} %broadcast_select_fusion.1.refs_0_), channel_id=1, source_target_pairs={{0,1},{1,0},{2,3},{3,2},{4,5},{5,4},{6,7},{7,6},{8,9},{9,8},{10,11... | collective-permute-start | bytes 1966088 | tf_op jit(solution)/shard_map/piece_0/ppermute | solution.py:279
  98.8 19.0 %collective-permute-start.18 = (bf16[256,1280]{1,0:T(8,128)(2,1)S(1)}, bf16[256,1280]{1,0:T(8,128)(2,1)S(1)}, u32[]{:S(2)}, u32[]{:S(2)}) collective-permute-start(bf16[256,1280]{1,0:T(8,128)(2,1)S(1)} %add_convert_fusion.1), channel_id=1, source_target_pairs={{4,8},{8,4},{5,9},{9,5},{6,10},{10,6},{7,11},{11,7},{20,24},{24,20... | collective-permute-start | bytes 1966088 | tf_op jit(solution)/shard_map/mid_3/ppermute | solution.py:332
